TPU v7x, 512 devices: a whole 4x4x16 slice. The times are simulated.
512 devices in a mesh: section: 32 (over z, core), tensor: 2 (over y_lo), dp: 8 (over x, y_hi).
Axes of the slice: x: 4, y: 4 (y_hi: 2, y_lo: 2; y = y_hi * 2 + y_lo), z: 16, core: 2. Of those that a mesh axis runs over, the one named last changes fastest.
Arguments:
- residual: bfloat16 [256, 2304], P(('tensor', 'dp')), may hold values from -6 to 6
- final_gain: float32 [2304], replicated, may hold values from 0.5 to 1.5
- table: bfloat16 [256000, 2304], P(('section', 'tensor', 'dp')), may hold values from -1.1953125 to 1.1953125
- targets: int32 [256], replicated, may hold values from 0 to 255999
- input_ids: int32 [256], replicated, may hold values from 0 to 255999
- loss_mask: int32 [256], replicated, may hold values 0 or 1
- embed_cotangent: bfloat16 [256, 2304], P(('tensor', 'dp')), may hold values from -0.119628906 to 0.119628906
Outputs:
- grad_residual: bfloat16 [256, 2304], P(('tensor', 'dp'))
- grad_gain: float32 [2304], replicated
- grad_table: bfloat16 [256000, 2304], P(('section', 'tensor', 'dp'))
All inputs are finite; a program needn't handle non-finite values.
Results may differ from a plain program's by a relative error of at most 0.0044.
Values may be sent and summed in bfloat16 or wider, within the bound.
No kernel may reach another device: no remote copies, remote signals or barrier semaphores. Data moves between devices by JAX's collectives and lax.ppermute only.
A program may use at most 64 MiB of HBM per device.

v0:
```python
import math

import jax
import jax.numpy as jnp
from jax import lax
from jax.sharding import PartitionSpec as P


def on_device(residual, final_gain, table, targets, input_ids, loss_mask, embed_cotangent):
    stream = residual.astype(jnp.float32)
    root_mean = jnp.sqrt(jnp.mean(stream * stream, axis=-1, keepdims=True) + 1e-06)
    normed = stream / root_mean
    hidden = (normed * final_gain).astype(jnp.bfloat16)
    all_hidden, all_cotangent = (
        lax.all_gather(hidden, ("tensor", "dp"), axis=0, tiled=True),
        lax.all_gather(embed_cotangent, ("tensor", "dp"), axis=0, tiled=True),
    )
    vocab_rows = table.shape[0]
    offset = lax.axis_index(("section", "tensor", "dp")) * vocab_rows
    contract = (((1,), (1,)), ((), ()))
    first_dims = (((0,), (0,)), ((), ()))
    scores = lax.dot_general(all_hidden, table, contract, preferred_element_type=jnp.float32)
    capped = 30.0 * jnp.tanh(scores / 30.0)
    expterm = jnp.exp(capped)
    totals = lax.psum(jnp.sum(expterm, axis=1), ("section", "tensor", "dp"))
    columns = offset + jnp.arange(vocab_rows, dtype=jnp.int32)
    target_hit = (targets[:, None] == columns[None, :]).astype(jnp.float32)
    weight = loss_mask.astype(jnp.float32)[:, None]
    dlogits = (
        weight * (expterm / totals[:, None] - target_hit) * (1.0 - (capped / 30.0) ** 2)
    ).astype(jnp.bfloat16)
    onehot_in = (input_ids[:, None] == columns[None, :]).astype(jnp.bfloat16)
    head_part = lax.dot_general(dlogits, all_hidden, first_dims, preferred_element_type=jnp.float32)
    input_part = lax.dot_general(
        onehot_in, all_cotangent, first_dims, preferred_element_type=jnp.float32
    )
    grad_table = (head_part + math.sqrt(table.shape[1]) * input_part).astype(jnp.bfloat16)
    summed = lax.psum(jnp.dot(dlogits, table, preferred_element_type=jnp.float32), "section")
    grad_hidden = lax.psum_scatter(summed, ("tensor", "dp"), scatter_dimension=0, tiled=True)
    scaled = grad_hidden * final_gain
    grad_residual = (
        (scaled - normed * jnp.mean(scaled * normed, axis=-1, keepdims=True)) / root_mean
    ).astype(jnp.bfloat16)
    grad_gain = lax.psum(jnp.sum(grad_hidden * normed, axis=0), ("tensor", "dp"))
    return (grad_residual, grad_gain, grad_table)


def solution(mesh):
    placed = (
        P(("tensor", "dp"), None),
        P(),
        P(("section", "tensor", "dp"), None),
        P(),
        P(),
        P(),
        P(("tensor", "dp"), None),
    )
    return jax.shard_map(
        on_device,
        mesh=mesh,
        in_specs=placed,
        out_specs=(P(("tensor", "dp"), None), P(), P(("section", "tensor", "dp"), None)),
        check_vma=False,
    )
```

profile of v0, /device:TPU:2, one launch (start us, length us, event | category | flops | bytes accessed | tf_op | source)
XLA Modules:
  0.0 657.9 jit_solution(11011076207691511992)
XLA Ops:
  7.2 0.0 copy-start
  7.2 0.0 all-gather.3.cloned.1.call-start
  7.2 1.2 fusion.7
  8.4 1.6 multiply_convert_fusion.1
  10.0 0.0 all-gather.3.cloned.1.call-update
  10.1 0.0 reduce-scatter.2.cloned.1.call-start
  10.1 0.7 convert_element_type.22
  10.8 87.4 %all-gather.3.cloned.1.call-done = bf16[256,2304]{1,0:T(8,128)(2,1)} async-done(((bf16[16,2304]{1,0:T(8,128)(2,1)}), bf16[256,2304]{1,0:T(8,128)(2,1)}) %all-gather.3.cloned.1.call-update) | async-done | bytes 1179664 | tf_op jit(solution)/shard_map/all_gather | solution.py:15
  98.2 2.1 fusion.3
  100.3 102.8 %psum.21 = f32[256]{0:T(256)S(1)} all-reduce(f32[256]{0:T(256)S(1)} %get-tuple-element.5), channel_id=1, replica_groups=mesh['section'=32,'tensor'=2,'dp'=8] {'section','tensor','dp'}, use_global_device_ids=true, to_apply=%region_2.0 | all-reduce | flops 256 | bytes 2048 | tf_op jit(solution)/shard_map/psum | solution.py:25
  203.2 2.4 fusion.9
  205.6 0.0 reduce-scatter.2.cloned.1.call-update
  205.6 0.0 all-gather.5.cloned.1.call-start
  205.6 0.7 all-gather.5.cloned.1.call-update
  206.3 0.0 all-reduce.2.cloned.1.call-start
  206.4 4.3 fusion.8
  210.6 80.4 %reduce-scatter.2.cloned.1.call-done = f32[16,2304]{1,0:T(8,128)} async-done(((f32[256,2304]{1,0:T(8,128)}), f32[16,2304]{1,0:T(8,128)}) %reduce-scatter.2.cloned.1.call-update) | async-done | bytes 147472 | tf_op jit(solution)/shard_map/reduce_scatter | solution.py:39
  291.0 0.0 all-reduce.2.cloned.1.call-update
  291.1 84.4 %all-gather.5.cloned.1.call-done = bf16[256,2304]{1,0:T(8,128)(2,1)} async-done(((bf16[16,2304]{1,0:T(8,128)(2,1)}), bf16[256,2304]{1,0:T(8,128)(2,1)}) %all-gather.5.cloned.1.call-update) | async-done | bytes 1179664 | tf_op jit(solution)/shard_map/all_gather | solution.py:16
  375.5 4.9 fusion.1
  380.4 195.7 %all-reduce.2.cloned.1.call-done = f32[16,2304]{1,0:T(8,128)} async-done(((f32[16,2304]{1,0:T(8,128)}), f32[16,2304]{1,0:T(8,128)}) %all-reduce.2.cloned.1.call-update) | async-done | bytes 147472 | tf_op jit(solution)/shard_map/psum | solution.py:38
  576.1 1.1 multiply_reduce_fusion
  577.2 72.5 %psum.23 = f32[2304]{0:T(1024)} all-reduce(f32[2304]{0:T(1024)S(1)} %get-tuple-element.3), channel_id=1, replica_groups=mesh['section'=32,'tensor'=2,'dp'=8] {'tensor','dp'}, use_global_device_ids=true, to_apply=%region_7.0 | all-reduce | flops 2304 | bytes 18432 | tf_op jit(solution)/shard_map/psum | solution.py:44
  649.7 1.6 divide_convert_fusion
  (12 shorter events, 0.0 us)
Async XLA Ops:
  7.2 91.0 %copy-start = (bf16[500,2304]{1,0:T(8,128)(2,1)S(1)}, bf16[500,2304]{1,0:T(8,128)(2,1)}, u32[]{:S(2)}) copy-start(bf16[500,2304]{1,0:T(8,128)(2,1)} %param.9) | copy-start | bytes 6912004
  7.2 91.0 %all-gather.3.cloned.1.call-start = ((), (), s32[]{:S(2)}) async-start(), calls=%async_computation.1 | async-start | bytes 1253376 | tf_op jit(solution)/shard_map/all_gather | solution.py:15
  10.1 281.0 %reduce-scatter.2.cloned.1.call-start = ((), (), s32[]{:S(2)}) async-start(), calls=%async_computation.3 | async-start | bytes 2506752 | tf_op jit(solution)/shard_map/reduce_scatter | solution.py:39
  10.8 192.4 %copy-start.3 = (s32[256]{0:T(256)S(1)}, s32[256]{0:T(256)}, u32[]{:S(2)}) copy-start(s32[256]{0:T(256)} %param.10) | copy-start | bytes 3076
  205.6 169.9 %all-gather.5.cloned.1.call-start = ((), (), s32[]{:S(2)}) async-start(), calls=%async_computation.2 | async-start | bytes 1253376 | tf_op jit(solution)/shard_map/all_gather | solution.py:16
  206.3 169.2 %copy-start.4 = (s32[256]{0:T(256)S(1)}, s32[256]{0:T(256)}, u32[]{:S(2)}) copy-start(s32[256]{0:T(256)} %param.11) | copy-start | bytes 3076
  206.3 369.8 %all-reduce.2.cloned.1.call-start = ((), (), s32[]{:S(2)}) async-start(), calls=%async_computation.4 | async-start | bytes 294912 | tf_op jit(solution)/shard_map/psum | solution.py:38
  291.1 285.0 %copy-start.1 = (bf16[16,2304]{1,0:T(8,128)(2,1)S(1)}, bf16[16,2304]{1,0:T(8,128)(2,1)}, u32[]{:S(2)}) copy-start(bf16[16,2304]{1,0:T(8,128)(2,1)} %param.7) | copy-start | bytes 221188
  291.1 285.0 %copy-start.2 = (f32[2304]{0:T(1024)S(1)}, f32[2304]{0:T(1024)}, u32[]{:S(2)}) copy-start(f32[2304]{0:T(1024)} %param.8) | copy-start | bytes 27652
Sparse Core Ops, SparseCore 0:
  10.7 87.4 all-gather.2
  205.7 85.2 reduce-scatter.1
  293.1 82.3 all-gather.4
  377.7 198.3 all-reduce.1
where the time goes:
time: 658 us
  waiting for transfers between devices  449 us (68%)
  blocking collectives  175 us (27%)
  between operations  13.8 us (2%)
  matrix products  13.7 us (2%)
    psum x1, waiting for transfers between devices, on_device(): lax.psum(jnp.dot(dlogits, table, preferred_element_type=jnp.float32), 'se...  196 us
    psum x1, blocking collectives, on_device(): totals = lax.psum(jnp.sum(expterm, axis=1), ('section', 'tensor', 'dp'))  103 us
    all_gather x1, waiting for transfers between devices, on_device(): lax.all_gather(hidden, ('tensor', 'dp'), axis=0, tiled=True)  87.4 us
    all_gather x1, waiting for transfers between devices, on_device(): lax.all_gather(embed_cotangent, ('tensor', 'dp'), axis=0, tiled=True)  84.4 us
    reduce_scatter x1, waiting for transfers between devices, on_device(): lax.psum_scatter(summed, ('tensor', 'dp'), scatter_dimension=0, tiled=True)  80.4 us
    psum x1, blocking collectives, on_device(): lax.psum(jnp.sum(grad_hidden * normed, axis=0), ('tensor', 'dp'))  72.5 us
  transfers between devices with their start and end apart: 4, of which 4 were waited for; matrix products, arithmetic and copies ran while one was open for 1% of the time, Pallas kernels for 0%

commit v1 on v0

v1 whole, which is shorter than its diff:
```python
import math

import jax
import jax.numpy as jnp
from jax import lax
from jax.sharding import PartitionSpec as P

PLANE = ("tensor", "dp")
EVERY = ("section", "tensor", "dp")


def exchange(pieces, axes):
    return lax.all_to_all(pieces, axes, 0, 0, tiled=True)


def to_all(x, axes):
    return exchange(jnp.broadcast_to(x[None], (lax.axis_size(axes),) + x.shape), axes)


def on_device(residual, final_gain, table, targets, input_ids, loss_mask, embed_cotangent):
    own, width = residual.shape
    vocab_rows = table.shape[0]
    n_plane, n_section = lax.axis_size(PLANE), lax.axis_size("section")
    tokens = own * n_plane
    all_cotangent = lax.all_gather(embed_cotangent, PLANE, axis=0, tiled=True)

    stream = to_all(residual, PLANE).reshape(tokens, width).astype(jnp.float32)
    root_mean = jnp.sqrt(jnp.mean(stream * stream, axis=-1, keepdims=True) + 1e-06)
    normed = stream / root_mean
    hidden = (normed * final_gain).astype(jnp.bfloat16)

    contract = (((1,), (1,)), ((), ()))
    first_dims = (((0,), (0,)), ((), ()))
    scores = lax.dot_general(hidden, table, contract, preferred_element_type=jnp.float32)
    capped = 30.0 * jnp.tanh(scores / 30.0)
    expterm = jnp.exp(capped)
    sums = jnp.sum(expterm, axis=1)
    sums = jnp.sum(to_all(sums, "section"), axis=0)
    totals = jnp.sum(to_all(sums, PLANE), axis=0)

    columns = lax.axis_index(EVERY) * vocab_rows + jnp.arange(vocab_rows, dtype=jnp.int32)
    target_hit = (targets[:, None] == columns[None, :]).astype(jnp.float32)
    weight = loss_mask.astype(jnp.float32)[:, None]
    dlogits = (
        weight * (expterm / totals[:, None] - target_hit) * (1.0 - (capped / 30.0) ** 2)
    ).astype(jnp.bfloat16)

    partial = jnp.dot(dlogits, table, preferred_element_type=jnp.float32)
    gain_part = jnp.sum(partial * normed, axis=0)
    high = gain_part.astype(jnp.bfloat16)
    low = (gain_part - high.astype(jnp.float32)).astype(jnp.bfloat16)
    rider = jnp.concatenate([high, low]).reshape(own, -1)
    rider_width = rider.shape[1]
    lanes = -(width + rider_width) % 128
    packed = jnp.concatenate(
        [
            partial.astype(jnp.bfloat16).reshape(n_plane, own, width),
            jnp.broadcast_to(rider[None], (n_plane, own, rider_width)),
            jnp.zeros((n_plane, own, lanes), jnp.bfloat16),
        ],
        axis=2,
    )
    arrived = jnp.sum(exchange(packed, PLANE).astype(jnp.float32), axis=0)
    grad_own = arrived[:, :width]
    gain_plane = arrived[:, width : width + rider_width].reshape(2, width).sum(axis=0)

    split = jnp.concatenate(
        [grad_own.reshape(n_section, -1), gain_plane.reshape(n_section, -1)], axis=1
    )
    summed = to_all(jnp.sum(exchange(split, "section"), axis=0), "section")
    cut = own * width // n_section
    grad_hidden = summed[:, :cut].reshape(own, width)
    grad_gain = summed[:, cut:].reshape(width)

    onehot_in = (input_ids[:, None] == columns[None, :]).astype(jnp.bfloat16)
    head_part = lax.dot_general(dlogits, hidden, first_dims, preferred_element_type=jnp.float32)
    input_part = lax.dot_general(
        onehot_in, all_cotangent, first_dims, preferred_element_type=jnp.float32
    )
    grad_table = (head_part + math.sqrt(width) * input_part).astype(jnp.bfloat16)

    stream = residual.astype(jnp.float32)
    root_mean = jnp.sqrt(jnp.mean(stream * stream, axis=-1, keepdims=True) + 1e-06)
    normed = stream / root_mean
    scaled = grad_hidden * final_gain
    grad_residual = (
        (scaled - normed * jnp.mean(scaled * normed, axis=-1, keepdims=True)) / root_mean
    ).astype(jnp.bfloat16)
    return (grad_residual, grad_gain, grad_table)


def solution(mesh):
    placed = (
        P(PLANE, None),
        P(),
        P(EVERY, None),
        P(),
        P(),
        P(),
        P(PLANE, None),
    )
    return jax.shard_map(
        on_device,
        mesh=mesh,
        in_specs=placed,
        out_specs=(P(PLANE, None), P(), P(EVERY, None)),
        check_vma=False,
    )
```

time: 658 us -> 186 us (0.28)
  waiting for transfers between devices: 449 us -> 75.6 us
  blocking collectives: 175 us -> 24.6 us
  starting transfers between devices: 0.16 us -> 35 us
  local copies, waits for them, and re-layouts: 0.03 us -> 13.7 us
    psum x1 -> x0, waiting for transfers between devices: 196 us -> none  [on_device(): lax.psum(jnp.dot(dlogits, table, preferred_element_type=jnp.float32), 'se...]
    psum x2 -> x0, blocking collectives: 175 us -> none  [the longest x1 103 us: on_device(): totals = lax.psum(jnp.sum(expterm, axis=1), ('section', 'tensor', 'dp'))]
    all_gather x2 -> x1, waiting for transfers between devices: 172 us -> 17.8 us  [on_device(): all_cotangent = lax.all_gather(embed_cotangent, PLANE, axis=0, tiled=True)]
    reduce_scatter x1 -> x0, waiting for transfers between devices: 80.4 us -> none  [on_device(): lax.psum_scatter(summed, ('tensor', 'dp'), scatter_dimension=0, tiled=True)]
    all_to_all x0 -> x5, waiting for transfers between devices: none -> 57.1 us  [exchange(): return lax.all_to_all(pieces, axes, 0, 0, tiled=True)]
    all_to_all x0 -> x5, starting transfers between devices: none -> 34.9 us  [exchange(): return lax.all_to_all(pieces, axes, 0, 0, tiled=True)]
    all_to_all x0 -> x1, blocking collectives: none -> 24.6 us  [exchange(): return lax.all_to_all(pieces, axes, 0, 0, tiled=True)]
  transfers between devices with their start and end apart: 4 -> 6, of which waited for: 4 -> 5; matrix products, arithmetic and copies ran while one was open for 1% -> 11% of each run, Pallas kernels for 0% -> 0%
where the time goes in v1:
time: 186 us; the launch traced here: 185 us
  waiting for transfers between devices  75.6 us (41%)
  starting transfers between devices  35 us (19%)
  blocking collectives  24.6 us (13%)
  between operations  14.2 us (8%)
  local copies, waits for them, and re-layouts  13.7 us (7%)
  matrix products  13.6 us (7%)
  other arithmetic  8.3 us (4%)
    all_to_all x5, waiting for transfers between devices, exchange(): return lax.all_to_all(pieces, axes, 0, 0, tiled=True)  57.1 us
    all_to_all x5, starting transfers between devices, exchange(): return lax.all_to_all(pieces, axes, 0, 0, tiled=True)  34.9 us
    all_to_all x1, blocking collectives, exchange(): return lax.all_to_all(pieces, axes, 0, 0, tiled=True)  24.6 us
    all_gather x1, waiting for transfers between devices, on_device(): all_cotangent = lax.all_gather(embed_cotangent, PLANE, axis=0, tiled=True)  17.8 us
    dot_general x1, matrix products, on_device(): lax.dot_general(onehot_in, all_cotangent, first_dims, preferred_element_t...  4.89 us
    dot_general x1, matrix products, on_device(): lax.dot_general(dlogits, hidden, first_dims, preferred_element_type=jnp.f...  4.04 us
  transfers between devices with their start and end apart: 6, of which 5 were waited for; matrix products, arithmetic and copies ran while one was open for 11% of the time, Pallas kernels for 0%

profile of v1, /device:TPU:2, one launch (start us, length us, event | category | flops | bytes accessed | tf_op | source)
XLA Modules:
  0.0 185.0 jit_solution(5724524031096795981)
XLA Ops:
  7.2 1.1 broadcast_in_dim.12
  8.3 24.6 %all_to_all.40 = bf16[16,16,2304]{2,1,0:T(8,128)(2,1)S(1)} all-to-all(bf16[16,16,2304]{2,1,0:T(8,128)(2,1)S(1)} %broadcast_in_dim.12), channel_id=1, replica_groups=mesh['section'=32,'tensor'=2,'dp'=8] {'tensor','dp'}, dimensions={0} | all-to-all | bytes 2359296 | tf_op jit(solution)/shard_map/all_to_all | solution.py:13
  33.7 1.0 copy-done.1
  34.8 1.6 fusion.3
  37.0 15.5 %all-to-all-start.1 = ((f32[32,1,256]{2,1,0:T(1,128)}), f32[32,1,256]{2,1,0:T(1,128)S(1)}, u32[]{:S(2)}, u32[]{:S(2)}) async-start(f32[32,1,256]{2,1,0:T(1,128)} %broadcast_in_dim.13), calls=%async_computation.1 | async-start | bytes 65536 | tf_op jit(solution)/shard_map/all_to_all | solution.py:13
  52.5 13.0 %all-to-all-done.1 = f32[32,1,256]{2,1,0:T(1,128)S(1)} async-done(((f32[32,1,256]{2,1,0:T(1,128)}), f32[32,1,256]{2,1,0:T(1,128)S(1)}, u32[]{:S(2)}, u32[]{:S(2)}) %all-to-all-start.1) | async-done | bytes 32800 | tf_op jit(solution)/shard_map/all_to_all | solution.py:13
  66.2 4.7 %all-to-all-start.2 = ((f32[16,1,256]{2,1,0:T(1,128)}), f32[16,1,256]{2,1,0:T(1,128)S(1)}, u32[]{:S(2)}, u32[]{:S(2)}) async-start(f32[16,1,256]{2,1,0:T(1,128)} %broadcast_in_dim.14), calls=%async_computation.2 | async-start | bytes 32768 | tf_op jit(solution)/shard_map/all_to_all | solution.py:13
  71.6 5.6 %all-to-all-done.2 = f32[16,1,256]{2,1,0:T(1,128)S(1)} async-done(((f32[16,1,256]{2,1,0:T(1,128)}), f32[16,1,256]{2,1,0:T(1,128)S(1)}, u32[]{:S(2)}, u32[]{:S(2)}) %all-to-all-start.2) | async-done | bytes 16416 | tf_op jit(solution)/shard_map/all_to_all | solution.py:13
  77.3 3.1 %multiply_reduce_fusion = (f32[2304]{0:T(1024)S(1)}, bf16[256,2304]{1,0:T(8,128)(2,1)}) fusion(f32[256]{0:T(256)S(1)} %sqrt.20, bf16[16,16,2304]{2,1,0:T(8,128)(2,1)S(1)} %all_to_all.40, bf16[500,2304]{1,0:T(8,128)(2,1)S(1)} %copy-done, f32[256,500]{0,1:T(8,128)} %get-tuple-element.8, s32[256]{0:T(256)} %param.10, f32[256]{0:T(256)S(1)} %reduce_sum.95, ...), kind=kOutput, calls=%fused_computation.5 | convolution fusion | flops 594050816 | bytes 5190608 | tf_op jit(solution)/shard_map/dot_general | solution.py:48
  80.5 3.1 %concatenate.11 = bf16[16,16,2688]{2,1,0:T(8,128)(2,1)} concatenate(bf16[16,16,2304]{2,1,0:T(8,128)(2,1)} %bitcast.15, bf16[16,16,288]{2,1,0:T(8,128)(2,1)S(1)} %broadcast_in_dim.15, bf16[16,16,96]{2,1,0:T(8,128)(2,1)S(1)} %broadcast_in_dim.16), dimensions={2} | concatenate | bytes 2752512 | tf_op jit(solution)/shard_map/concatenate | solution.py:55
  83.6 5.6 %all-to-all-start.3 = ((bf16[16,16,2688]{2,1,0:T(8,128)(2,1)}), bf16[16,16,2688]{2,1,0:T(8,128)(2,1)}, u32[]{:S(2)}, u32[]{:S(2)}) async-start(bf16[16,16,2688]{2,1,0:T(8,128)(2,1)} %concatenate.11), calls=%async_computation.3 | async-start | bytes 2752512 | tf_op jit(solution)/shard_map/all_to_all | solution.py:13
  89.9 20.9 %all-to-all-done.3 = bf16[16,16,2688]{2,1,0:T(8,128)(2,1)} async-done(((bf16[16,16,2688]{2,1,0:T(8,128)(2,1)}), bf16[16,16,2688]{2,1,0:T(8,128)(2,1)}, u32[]{:S(2)}, u32[]{:S(2)}) %all-to-all-start.3) | async-done | bytes 1376288 | tf_op jit(solution)/shard_map/all_to_all | solution.py:13
  110.9 1.5 convert_reduce_fusion
  113.8 1.3 reduce_sum.99
  115.1 1.6 reshape.92
  119.2 4.6 %all-to-all-start.4 = ((f32[32,1,1224]{2,1,0:T(1,128)}), f32[32,1,1224]{2,1,0:T(1,128)}, u32[]{:S(2)}, u32[]{:S(2)}) async-start(f32[32,1,1224]{2,1,0:T(1,128)} %all_to_all.30), calls=%async_computation.4 | async-start | bytes 327680 | tf_op jit(solution)/shard_map/all_to_all | solution.py:13
  123.8 1.0 fusion.7
  124.8 17.5 %all-to-all-done.4 = f32[32,1,1224]{2,1,0:T(1,128)} async-done(((f32[32,1,1224]{2,1,0:T(1,128)}), f32[32,1,1224]{2,1,0:T(1,128)}, u32[]{:S(2)}, u32[]{:S(2)}) %all-to-all-start.4) | async-done | bytes 156704 | tf_op jit(solution)/shard_map/all_to_all | solution.py:13
  142.4 1.0 reduce_sum.100
  144.2 4.6 %all-to-all-start.5 = ((f32[32,1,1224]{2,1,0:T(1,128)}), f32[32,1,1224]{2,1,0:T(1,128)}, u32[]{:S(2)}, u32[]{:S(2)}) async-start(f32[32,1,1224]{2,1,0:T(1,128)} %broadcast_in_dim.17), calls=%async_computation.5 | async-start | bytes 327680 | tf_op jit(solution)/shard_map/all_to_all | solution.py:13
  148.8 4.0 %fusion.8 = f32[500,2304]{1,0:T(8,128)} fusion(bf16[256,2304]{1,0:T(8,128)(2,1)S(1)} %copy-done.2, f32[256,500]{0,1:T(8,128)} %get-tuple-element.8, s32[256]{0:T(256)S(1)} %copy-done.5, f32[256]{0:T(256)S(1)} %reduce_sum.95, f32[256]{0:T(256)S(1)} %convert_element_type.50, s32[500]{0:T(512)S(1)} %iota_add_fusion), kind=kOutput, calls=%fused_computation.29 | convolution fusion | flops 591104000 | bytes 6304720 | tf_op jit(solution)/shard_map/dot_general | solution.py:76
  152.8 17.8 %all-gather.2.cloned.1.call-done = bf16[256,2304]{1,0:T(8,128)(2,1)} async-done(((bf16[16,2304]{1,0:T(8,128)(2,1)}), bf16[256,2304]{1,0:T(8,128)(2,1)}) %all-gather.2.cloned.1.call-update) | async-done | bytes 1179664 | tf_op jit(solution)/shard_map/all_gather | solution.py:25
  170.6 4.9 %fusion.1 = bf16[500,2304]{1,0:T(8,128)(2,1)} fusion(f32[500,2304]{1,0:T(8,128)} %fusion.8, bf16[256,2304]{1,0:T(8,128)(2,1)} %all-gather.2.cloned.1.call-done, s32[256]{0:T(256)S(1)} %copy-done.6, s32[500]{0:T(512)S(1)} %iota_add_fusion), kind=kOutput, calls=%fused_computation.2 | convolution fusion | flops 593408000 | bytes 8094672 | tf_op jit(solution)/shard_map/dot_general | solution.py:77
  175.5 0.9 copy.16
  (46 shorter events, 10.0 us)
Async XLA Ops:
  7.2 27.6 %copy-start = (bf16[500,2304]{1,0:T(8,128)(2,1)S(1)}, bf16[500,2304]{1,0:T(8,128)(2,1)}, u32[]{:S(2)}) copy-start(bf16[500,2304]{1,0:T(8,128)(2,1)} %param.9) | copy-start | bytes 6912004
  7.2 26.2 %copy-start.4 = (f32[2304]{0:T(1024)S(1)}, f32[2304]{0:T(1024)}, u32[]{:S(2)}) copy-start(f32[2304]{0:T(1024)} %param.8) | copy-start | bytes 27652
  33.7 1.0 copy-start.1
  37.0 28.5 %all-to-all-start.1 = ((f32[32,1,256]{2,1,0:T(1,128)}), f32[32,1,256]{2,1,0:T(1,128)S(1)}, u32[]{:S(2)}, u32[]{:S(2)}) async-start(f32[32,1,256]{2,1,0:T(1,128)} %broadcast_in_dim.13), calls=%async_computation.1 | async-start | bytes 65536 | tf_op jit(solution)/shard_map/all_to_all | solution.py:13
  66.2 11.1 %all-to-all-start.2 = ((f32[16,1,256]{2,1,0:T(1,128)}), f32[16,1,256]{2,1,0:T(1,128)S(1)}, u32[]{:S(2)}, u32[]{:S(2)}) async-start(f32[16,1,256]{2,1,0:T(1,128)} %broadcast_in_dim.14), calls=%async_computation.2 | async-start | bytes 32768 | tf_op jit(solution)/shard_map/all_to_all | solution.py:13
  83.6 27.3 %all-to-all-start.3 = ((bf16[16,16,2688]{2,1,0:T(8,128)(2,1)}), bf16[16,16,2688]{2,1,0:T(8,128)(2,1)}, u32[]{:S(2)}, u32[]{:S(2)}) async-start(bf16[16,16,2688]{2,1,0:T(8,128)(2,1)} %concatenate.11), calls=%async_computation.3 | async-start | bytes 2752512 | tf_op jit(solution)/shard_map/all_to_all | solution.py:13
  89.2 59.5 %copy-start.2 = (bf16[256,2304]{1,0:T(8,128)(2,1)S(1)}, bf16[256,2304]{1,0:T(8,128)(2,1)}, u32[]{:S(2)}) copy-start(bf16[256,2304]{1,0:T(8,128)(2,1)} %copy-done.1) | copy-start | bytes 3538948
  89.2 59.5 %copy-start.5 = (s32[256]{0:T(256)S(1)}, s32[256]{0:T(256)}, u32[]{:S(2)}) copy-start(s32[256]{0:T(256)} %param.10) | copy-start | bytes 3076
  89.2 81.4 %all-gather.2.cloned.1.call-start = ((), (), s32[]{:S(2)}) async-start(), calls=%async_computation.6 | async-start | bytes 1253376 | tf_op jit(solution)/shard_map/all_gather | solution.py:25
  119.2 23.2 %all-to-all-start.4 = ((f32[32,1,1224]{2,1,0:T(1,128)}), f32[32,1,1224]{2,1,0:T(1,128)}, u32[]{:S(2)}, u32[]{:S(2)}) async-start(f32[32,1,1224]{2,1,0:T(1,128)} %all_to_all.30), calls=%async_computation.4 | async-start | bytes 327680 | tf_op jit(solution)/shard_map/all_to_all | solution.py:13
  144.2 31.3 %all-to-all-start.5 = ((f32[32,1,1224]{2,1,0:T(1,128)}), f32[32,1,1224]{2,1,0:T(1,128)}, u32[]{:S(2)}, u32[]{:S(2)}) async-start(f32[32,1,1224]{2,1,0:T(1,128)} %broadcast_in_dim.17), calls=%async_computation.5 | async-start | bytes 327680 | tf_op jit(solution)/shard_map/all_to_all | solution.py:13
  148.8 21.9 %copy-start.6 = (s32[256]{0:T(256)S(1)}, s32[256]{0:T(256)}, u32[]{:S(2)}) copy-start(s32[256]{0:T(256)} %param.11) | copy-start | bytes 3076
  152.8 24.4 %copy-start.3 = (bf16[16,2304]{1,0:T(8,128)(2,1)S(1)}, bf16[16,2304]{1,0:T(8,128)(2,1)}, u32[]{:S(2)}) copy-start(bf16[16,2304]{1,0:T(8,128)(2,1)} %param.7) | copy-start | bytes 221188
Sparse Core Ops, SparseCore 0:
  92.1 78.4 all-gather.1

commit v2 on v0

v2 whole, which is shorter than its diff:
```python
import math

import jax
import jax.numpy as jnp
from jax import lax
from jax.experimental import pallas as pl
from jax.experimental.pallas import tpu as pltpu
from jax.sharding import PartitionSpec as P

PLANE = ("tensor", "dp")
EVERY = ("section", "tensor", "dp")
LANES = 128
VMEM_LIMIT = 24 * 1024 * 1024
F32 = jnp.float32
BF16 = jnp.bfloat16
VMEM = pl.BlockSpec(memory_space=pltpu.VMEM)
SMEM = pl.BlockSpec(memory_space=pltpu.SMEM)


def exchange(pieces, axes):
    return lax.all_to_all(pieces, axes, 0, 0, tiled=True)


def call(body, outs, flops, moved, *operands, in_specs=None, out_specs=None, scratch=()):
    several = isinstance(outs, tuple)
    return pl.pallas_call(
        body,
        out_shape=outs,
        in_specs=in_specs or [VMEM] * len(operands),
        out_specs=out_specs or ((VMEM,) * len(outs) if several else VMEM),
        scratch_shapes=list(scratch),
        compiler_params=pltpu.CompilerParams(vmem_limit_bytes=VMEM_LIMIT),
        cost_estimate=pl.CostEstimate(flops=flops, bytes_accessed=moved, transcendentals=0),
    )(*operands)


def capped_scores(res_ref, gain_ref, table_ref, hidden_ref, inverse_ref):
    tokens = res_ref.shape[0]
    step = 16

    def norm(i, carry):
        rows = pl.ds(pl.multiple_of(i * step, step), step)
        x = res_ref[rows, :].astype(F32)
        inverse = 1.0 / jnp.sqrt(jnp.mean(x * x, axis=1, keepdims=True) + 1e-06)
        inverse_ref[rows, :] = jnp.broadcast_to(inverse, (step, LANES))
        hidden_ref[rows, :] = (x * inverse * gain_ref[...]).astype(BF16)
        return carry

    lax.fori_loop(0, tokens // step, norm, 0, unroll=4)
    scores = lax.dot_general(
        table_ref[...], hidden_ref[...], (((1,), (1,)), ((), ())), preferred_element_type=F32
    )
    return 30.0 * jnp.tanh(scores * (1.0 / 30.0))


def logit_grads(capped, first_ref, arrived_ref, targets_ref, mask_ref):
    totals = arrived_ref[0]
    for i in range(1, arrived_ref.shape[0]):
        totals = totals + arrived_ref[i]
    rows = lax.broadcasted_iota(jnp.int32, capped.shape, 0)
    hit = (targets_ref[...] - first_ref[0] == rows).astype(F32)
    share = jnp.exp(capped) * (1.0 / totals)
    bend = capped * (1.0 / 30.0)
    return (mask_ref[...].astype(F32) * (share - hit) * (1.0 - bend * bend)).astype(BF16)


def sums_body(res_ref, gain_ref, table_ref, sums_ref, hidden_ref, inverse_ref):
    capped = capped_scores(res_ref, gain_ref, table_ref, hidden_ref, inverse_ref)
    sums = jnp.sum(jnp.exp(capped), axis=0, keepdims=True)
    for i in range(sums_ref.shape[0]):
        sums_ref[i] = sums


def spread_body(in_ref, out_ref):
    total = in_ref[0]
    for i in range(1, in_ref.shape[0]):
        total = total + in_ref[i]
    for i in range(out_ref.shape[0]):
        out_ref[i] = total


def partial_body(
    first_ref, arrived_ref, targets_ref, mask_ref, res_ref, gain_ref, table_ref,
    packed_ref, hidden_ref, inverse_ref, rider_ref,
):
    n_plane, own, packed_width = packed_ref.shape
    width = res_ref.shape[1]
    capped = capped_scores(res_ref, gain_ref, table_ref, hidden_ref, inverse_ref)
    dlogits = logit_grads(capped, first_ref, arrived_ref, targets_ref, mask_ref)
    rider_ref[...] = jnp.zeros_like(rider_ref)
    tile = 2 * LANES
    n_lanes = width // LANES
    inverse = jnp.concatenate([inverse_ref[...]] * 2, axis=1)
    for n in range(width // tile):
        columns = slice(n * tile, (n + 1) * tile)
        part = lax.dot_general(
            dlogits, table_ref[:, columns], (((0,), (0,)), ((), ())), preferred_element_type=F32
        )
        packed_ref[:, :, columns] = part.astype(BF16).reshape(n_plane, own, tile)
        normed = res_ref[:, columns].astype(F32) * inverse
        gain = jnp.sum(part * normed, axis=0, keepdims=True)
        high = gain.astype(BF16).astype(F32)
        low = gain - high
        for k in range(2):
            piece = slice(k * LANES, (k + 1) * LANES)
            rider_ref[2 * n + k : 2 * n + k + 1, :] = high[:, piece]
            rider_ref[n_lanes + 2 * n + k : n_lanes + 2 * n + k + 1, :] = low[:, piece]
    for j in range(rider_ref.shape[0] // own):
        block = rider_ref[j * own : (j + 1) * own, :].astype(BF16)
        for i in range(n_plane):
            packed_ref[i, :, width + j * LANES : width + (j + 1) * LANES] = block


def split_body(in_ref, out_ref, gain_ref):
    n_plane, own, packed_width = in_ref.shape
    n_section = out_ref.shape[0]
    cut = out_ref.shape[2] - LANES
    halves = n_section // own
    width = halves * cut
    n_lanes = width // LANES
    total = in_ref[0].astype(F32)
    for i in range(1, n_plane):
        total = total + in_ref[i].astype(F32)
    for h in range(halves):
        out_ref[h * own : (h + 1) * own, 0, :cut] = total[:, h * cut : (h + 1) * cut]
    for j in range((packed_width - width) // LANES):
        gain_ref[j * own : (j + 1) * own, :] = total[:, width + j * LANES : width + (j + 1) * LANES]
    rows = gain_ref[:n_lanes, :] + gain_ref[n_lanes : 2 * n_lanes, :]
    out_ref[:n_lanes, 0, cut:] = rows
    out_ref[n_lanes:, 0, cut:] = jnp.zeros((n_section - n_lanes, LANES), F32)


def finish_body(in_ref, res_ref, gain_ref, grad_ref, grad_gain_ref):
    n_section = in_ref.shape[0]
    own, width = res_ref.shape
    cut = in_ref.shape[2] - LANES
    halves = n_section // own
    x = res_ref[...].astype(F32)
    inverse = 1.0 / jnp.sqrt(jnp.mean(x * x, axis=1, keepdims=True) + 1e-06)
    normed = x * inverse
    grad_hidden = jnp.concatenate(
        [in_ref[h * own : (h + 1) * own, 0, :cut] for h in range(halves)], axis=1
    )
    scaled = grad_hidden * gain_ref[...]
    along = jnp.mean(scaled * normed, axis=1, keepdims=True)
    grad_ref[...] = ((scaled - normed * along) * inverse).astype(BF16)
    grad_gain_ref[...] = in_ref[: width // LANES, 0, cut:]


def table_body(
    first_ref, arrived_ref, targets_ref, mask_ref, res_ref, gain_ref, table_ref, ids_ref,
    cotangent_ref, out_ref, hidden_ref, inverse_ref,
):
    vocab_rows, width = out_ref.shape
    capped = capped_scores(res_ref, gain_ref, table_ref, hidden_ref, inverse_ref)
    dlogits = logit_grads(capped, first_ref, arrived_ref, targets_ref, mask_ref)
    rows = lax.broadcasted_iota(jnp.int32, capped.shape, 0)
    onehot = (ids_ref[...] - first_ref[0] == rows).astype(F32).astype(BF16)
    scale = math.sqrt(width)
    tile = 2 * LANES
    for n in range(width // tile):
        columns = slice(n * tile, (n + 1) * tile)
        head = jnp.dot(dlogits, hidden_ref[:, columns], preferred_element_type=F32)
        inputs = jnp.dot(onehot, cotangent_ref[:, columns], preferred_element_type=F32)
        out_ref[:, columns] = (head + scale * inputs).astype(BF16)


def on_device(residual, final_gain, table, targets, input_ids, loss_mask, embed_cotangent):
    own, width = residual.shape
    vocab_rows = table.shape[0]
    n_plane, n_section = lax.axis_size(PLANE), lax.axis_size("section")
    tokens = own * n_plane
    cut = own * width // n_section
    n_lanes = width // LANES
    rider = -(-2 * n_lanes // own) * own
    product = 2 * tokens * vocab_rows * width
    shape = jax.ShapeDtypeStruct
    first = (lax.axis_index(EVERY) * vocab_rows).astype(jnp.int32).reshape(1)
    gain_row = final_gain.reshape(1, width)

    packed_width = width + rider // own * LANES
    norm_rooms = [pltpu.VMEM((tokens, width), BF16), pltpu.VMEM((tokens, LANES), F32)]
    rows_bytes = vocab_rows * width * 2

    wide = jnp.pad(embed_cotangent, ((0, 0), (0, 512)))
    everyone = exchange(jnp.broadcast_to(residual[None], (n_plane, own, width)), PLANE)
    everyone = everyone.reshape(tokens, width)
    everyone, wide = lax.optimization_barrier((everyone, wide))
    all_cotangent = lax.all_gather(wide, PLANE, axis=0, tiled=True)

    sums = call(
        sums_body,
        shape((n_section, 1, tokens), F32),
        product,
        rows_bytes,
        everyone, gain_row, table,
        scratch=norm_rooms,
    )
    sums = call(
        spread_body, shape((n_plane, 1, tokens), F32), tokens, 4 * tokens, exchange(sums, "section")
    )
    given = (
        first, exchange(sums, PLANE), targets.reshape(1, tokens), loss_mask.reshape(1, tokens),
        everyone, gain_row, table,
    )
    packed = call(
        partial_body,
        shape((n_plane, own, packed_width), BF16),
        2 * product,
        rows_bytes,
        *given,
        in_specs=[SMEM] + [VMEM] * 6,
        scratch=norm_rooms + [pltpu.VMEM((rider, LANES), F32)],
    )
    arrived = exchange(packed, PLANE)
    split = call(
        split_body,
        shape((n_section, 1, cut + LANES), F32),
        tokens * width,
        tokens * width * 2,
        arrived,
        scratch=[pltpu.VMEM((rider, LANES), F32)],
    )
    reduced = call(
        spread_body,
        shape((n_section, 1, cut + LANES), F32),
        own * width,
        own * width * 8,
        exchange(split, "section"),
    )
    grad_table = call(
        table_body,
        shape((vocab_rows, width), BF16),
        3 * product,
        2 * rows_bytes,
        *given, input_ids.reshape(1, tokens), all_cotangent,
        in_specs=[SMEM] + [VMEM] * 8,
        scratch=norm_rooms,
    )
    summed, grad_table = lax.optimization_barrier((exchange(reduced, "section"), grad_table))
    grad_residual, grad_gain = call(
        finish_body,
        (shape((own, width), BF16), shape((n_lanes, LANES), F32)),
        own * width * 10,
        own * width * 8,
        summed, residual, gain_row,
    )
    return (grad_residual, grad_gain.reshape(width), grad_table)


def solution(mesh):
    placed = (
        P(PLANE, None),
        P(),
        P(EVERY, None),
        P(),
        P(),
        P(),
        P(PLANE, None),
    )
    return jax.shard_map(
        on_device,
        mesh=mesh,
        in_specs=placed,
        out_specs=(P(PLANE, None), P(), P(EVERY, None)),
        check_vma=False,
    )
```

time: 658 us -> 166 us (0.25)
  waiting for transfers between devices: 449 us -> 32.7 us
  blocking collectives: 175 us -> 79.5 us
  starting transfers between devices: 0.16 us -> 19.1 us
  matrix products: 13.7 us -> 0 us
  Pallas kernels: 0 us -> 13.4 us
    psum x1 -> x0, waiting for transfers between devices: 196 us -> none  [on_device(): lax.psum(jnp.dot(dlogits, table, preferred_element_type=jnp.float32), 'se...]
    psum x2 -> x0, blocking collectives: 175 us -> none  [the longest x1 103 us: on_device(): totals = lax.psum(jnp.sum(expterm, axis=1), ('section', 'tensor', 'dp'))]
    all_gather x2 -> x1, waiting for transfers between devices: 172 us -> 0.02 us  [on_device(): all_cotangent = lax.all_gather(wide, PLANE, axis=0, tiled=True)]
    reduce_scatter x1 -> x0, waiting for transfers between devices: 80.4 us -> none  [on_device(): lax.psum_scatter(summed, ('tensor', 'dp'), scatter_dimension=0, tiled=True)]
    all_to_all x0 -> x3, blocking collectives: none -> 79.5 us  [exchange(): return lax.all_to_all(pieces, axes, 0, 0, tiled=True)]
    all_to_all x0 -> x3, waiting for transfers between devices: none -> 32.7 us  [exchange(): return lax.all_to_all(pieces, axes, 0, 0, tiled=True)]
    all_to_all x0 -> x3, starting transfers between devices: none -> 19.1 us  [exchange(): return lax.all_to_all(pieces, axes, 0, 0, tiled=True)]
    dot_general x4 -> x0, matrix products: 13.7 us -> none  [the longest x1 4.9 us: on_device(): lax.dot_general(onehot_in, all_cotangent, first_dims, preferred_element_t...]
  transfers between devices with their start and end apart: 4 -> 4, of which waited for: 4 -> 3; matrix products, arithmetic and copies ran while one was open for 1% -> 1% of each run, Pallas kernels for 0% -> 7%
where the time goes in v2:
time: 166 us; the launch traced here: 165 us
  blocking collectives  79.5 us (48%)
  waiting for transfers between devices  32.7 us (20%)
  starting transfers between devices  19.1 us (12%)
  between operations  14.1 us (8%)
  Pallas kernels  13.4 us (8%)
  local copies, waits for them, and re-layouts  6.43 us (4%)
    all_to_all x3, blocking collectives, exchange(): return lax.all_to_all(pieces, axes, 0, 0, tiled=True)  79.5 us
    all_to_all x3, waiting for transfers between devices, exchange(): return lax.all_to_all(pieces, axes, 0, 0, tiled=True)  32.7 us
    all_to_all x3, starting transfers between devices, exchange(): return lax.all_to_all(pieces, axes, 0, 0, tiled=True)  19.1 us
    pallas_call x7, Pallas kernels, call(): pl.pallas_call(body, out_shape=outs, in_specs=in_specs or [VMEM] * len(op...  13.4 us
  transfers between devices with their start and end apart: 4, of which 3 were waited for; matrix products, arithmetic and copies ran while one was open for 1% of the time, Pallas kernels for 7%

profile of v2, /device:TPU:2, one launch (start us, length us, event | category | flops | bytes accessed | tf_op | source)
XLA Modules:
  0.0 165.3 jit_solution(10379655949917543144)
XLA Ops:
  7.2 2.0 %broadcast_in_dim.2 = bf16[16,16,2304]{2,1,0:T(8,128)(2,1)} broadcast(bf16[16,2304]{1,0:T(8,128)(2,1)} %res_ref.1), dimensions={1,2} | broadcast | bytes 1253376 | tf_op jit(solution)/shard_map/broadcast_in_dim | solution.py:186
  9.1 9.5 %all-to-all-start = ((bf16[16,16,2304]{2,1,0:T(8,128)(2,1)}), bf16[16,16,2304]{2,1,0:T(8,128)(2,1)S(1)}, u32[]{:S(2)}, u32[]{:S(2)}) async-start(bf16[16,16,2304]{2,1,0:T(8,128)(2,1)} %broadcast_in_dim.2), calls=%async_computation | async-start | bytes 2359296 | tf_op jit(solution)/shard_map/all_to_all | solution.py:21
  18.7 0.0 all-gather.2.cloned.1.call-start
  18.7 1.5 pad.4
  20.2 14.7 %all-to-all-done = bf16[16,16,2304]{2,1,0:T(8,128)(2,1)S(1)} async-done(((bf16[16,16,2304]{2,1,0:T(8,128)(2,1)}), bf16[16,16,2304]{2,1,0:T(8,128)(2,1)S(1)}, u32[]{:S(2)}, u32[]{:S(2)}) %all-to-all-start) | async-done | bytes 1179680 | tf_op jit(solution)/shard_map/all_to_all | solution.py:21
  34.9 0.0 all-gather.2.cloned.1.call-update
  35.0 1.6 shard_map.94
  36.6 29.5 %all_to_all.30.in_ref = f32[32,1,256]{2,1,0:T(1,128)S(1)} all-to-all(f32[32,1,256]{2,1,0:T(1,128)S(1)} %shard_map.94), channel_id=1, replica_groups=mesh['section'=32,'tensor'=2,'dp'=8] {'section'}, dimensions={0} | all-to-all | bytes 65536 | tf_op jit(solution)/shard_map/all_to_all | solution.py:21
  66.1 0.6 shard_map.95
  66.8 5.0 %all-to-all-start.2 = ((f32[16,1,256]{2,1,0:T(1,128)}), f32[16,1,256]{2,1,0:T(1,128)S(1)}, u32[]{:S(2)}, u32[]{:S(2)}) async-start(f32[16,1,256]{2,1,0:T(1,128)} %shard_map.95), calls=%async_computation.2 | async-start | bytes 32768 | tf_op jit(solution)/shard_map/all_to_all | solution.py:21
  71.8 6.3 %all-to-all-done.2.arrived_ref = f32[16,1,256]{2,1,0:T(1,128)S(1)} async-done(((f32[16,1,256]{2,1,0:T(1,128)}), f32[16,1,256]{2,1,0:T(1,128)S(1)}, u32[]{:S(2)}, u32[]{:S(2)}) %all-to-all-start.2) | async-done | bytes 16416 | tf_op jit(solution)/shard_map/all_to_all | solution.py:21
  78.1 3.6 %shard_map.96 = bf16[16,16,2688]{2,1,0:T(8,128)(2,1)S(1)} custom-call(s32[1]{0:T(128)} %bitcast.first_ref, f32[16,1,256]{2,1,0:T(1,128)S(1)} %all-to-all-done.2.arrived_ref, s32[1,256]{1,0:T(1,128)S(1)} %bitcast.9, s32[1,256]{1,0:T(1,128)S(1)} %bitcast.11, bf16[256,2304]{1,0:T(8,128)(2,1)S(1)} %bitcast.7, f32[1,2304]{1,0:T(1,128)S(1)} %reshape.30.gain_ref, ...), custom_call_target="tpu_custom_call" | custom-call | flops 1179648000 | bytes 2304000 | tf_op jit(solution)/shard_map/pallas_call | solution.py:26
  81.7 28.1 %all_to_all.31.in_ref = bf16[16,16,2688]{2,1,0:T(8,128)(2,1)S(1)} all-to-all(bf16[16,16,2688]{2,1,0:T(8,128)(2,1)S(1)} %shard_map.96), channel_id=1, replica_groups=mesh['section'=32,'tensor'=2,'dp'=8] {'tensor','dp'}, dimensions={0} | all-to-all | bytes 2752512 | tf_op jit(solution)/shard_map/all_to_all | solution.py:21
  109.8 0.2 shard_map.97
  110.0 21.9 %all_to_all.32.in_ref = f32[32,1,1280]{2,1,0:T(1,128)S(1)} all-to-all(f32[32,1,1280]{2,1,0:T(1,128)S(1)} %shard_map.97), channel_id=1, replica_groups=mesh['section'=32,'tensor'=2,'dp'=8] {'section'}, dimensions={0} | all-to-all | bytes 327680 | tf_op jit(solution)/shard_map/all_to_all | solution.py:21
  131.9 0.1 shard_map.98
  132.0 0.7 copy-done.2
  132.7 4.6 %all-to-all-start.5 = ((f32[32,1,1280]{2,1,0:T(1,128)}), f32[32,1,1280]{2,1,0:T(1,128)}, u32[]{:S(2)}, u32[]{:S(2)}) async-start(f32[32,1,1280]{2,1,0:T(1,128)} %copy-done.2), calls=%async_computation.5 | async-start | bytes 327680 | tf_op jit(solution)/shard_map/all_to_all | solution.py:21
  137.2 0.0 all-gather.2.cloned.1.call-done.cotangent_ref
  137.3 1.4 copy-done.1
  138.6 5.5 %shard_map.99 = bf16[500,2304]{1,0:T(8,128)(2,1)} custom-call(s32[1]{0:T(128)} %bitcast.first_ref, f32[16,1,256]{2,1,0:T(1,128)S(1)} %all-to-all-done.2.arrived_ref, s32[1,256]{1,0:T(1,128)S(1)} %bitcast.10, s32[1,256]{1,0:T(1,128)S(1)} %bitcast.12, bf16[256,2304]{1,0:T(8,128)(2,1)S(1)} %bitcast.8, f32[1,2304]{1,0:T(1,128)S(1)} %reshape.30.gain_ref, ...), custom_call_target="tpu_custom_call" | custom-call | flops 1769472000 | bytes 4608000 | tf_op jit(solution)/shard_map/pallas_call | solution.py:26
  144.1 11.7 %all-to-all-done.5.in_ref = f32[32,1,1280]{2,1,0:T(1,128)} async-done(((f32[32,1,1280]{2,1,0:T(1,128)}), f32[32,1,1280]{2,1,0:T(1,128)}, u32[]{:S(2)}, u32[]{:S(2)}) %all-to-all-start.5) | async-done | bytes 163872 | tf_op jit(solution)/shard_map/all_to_all | solution.py:21
  155.8 0.9 copy-done.3
  156.7 1.8 %shard_map.100 = (bf16[16,2304]{1,0:T(8,128)(2,1)}, f32[18,128]{1,0:T(8,128)}) custom-call(f32[32,1,1280]{2,1,0:T(1,128)} %all-to-all-done.5.in_ref, bf16[16,2304]{1,0:T(8,128)(2,1)S(1)} %copy-done.3, f32[1,2304]{1,0:T(1,128)S(1)} %reshape.30.gain_ref), custom_call_target="tpu_custom_call" | custom-call | flops 368640 | bytes 294912 | tf_op jit(solution)/shard_map/pallas_call | solution.py:26
  (14 shorter events, 0.0 us)
Async XLA Ops:
  9.1 25.8 %copy-start.7 = (f32[2304]{0:T(1024)S(1)}, f32[2304]{0:T(1024)}, u32[]{:S(2)}) copy-start(f32[2304]{0:T(1024)} %param.8) | copy-start | bytes 27652
  9.1 25.8 %copy-start = (bf16[500,2304]{1,0:T(8,128)(2,1)S(1)}, bf16[500,2304]{1,0:T(8,128)(2,1)}, u32[]{:S(2)}) copy-start(bf16[500,2304]{1,0:T(8,128)(2,1)} %table_ref.5) | copy-start | bytes 6912004
  9.1 25.8 %all-to-all-start = ((bf16[16,16,2304]{2,1,0:T(8,128)(2,1)}), bf16[16,16,2304]{2,1,0:T(8,128)(2,1)S(1)}, u32[]{:S(2)}, u32[]{:S(2)}) async-start(bf16[16,16,2304]{2,1,0:T(8,128)(2,1)} %broadcast_in_dim.2), calls=%async_computation | async-start | bytes 2359296 | tf_op jit(solution)/shard_map/all_to_all | solution.py:21
  18.7 118.6 %all-gather.2.cloned.1.call-start = ((), (), s32[]{:S(2)}) async-start(), calls=%async_computation.6 | async-start | bytes 1531904 | tf_op jit(solution)/shard_map/all_gather | solution.py:189
  35.0 43.1 %copy-start.4 = (s32[256]{0:T(256)S(1)}, s32[256]{0:T(256)}, u32[]{:S(2)}) copy-start(s32[256]{0:T(256)} %param.10) | copy-start | bytes 3076
  35.0 43.1 %copy-start.5 = (s32[256]{0:T(256)S(1)}, s32[256]{0:T(256)}, u32[]{:S(2)}) copy-start(s32[256]{0:T(256)} %param.12) | copy-start | bytes 3076
  66.8 11.3 %all-to-all-start.2 = ((f32[16,1,256]{2,1,0:T(1,128)}), f32[16,1,256]{2,1,0:T(1,128)S(1)}, u32[]{:S(2)}, u32[]{:S(2)}) async-start(f32[16,1,256]{2,1,0:T(1,128)} %shard_map.95), calls=%async_computation.2 | async-start | bytes 32768 | tf_op jit(solution)/shard_map/all_to_all | solution.py:21
  109.8 27.5 %copy-start.6 = (s32[256]{0:T(256)S(1)}, s32[256]{0:T(256)}, u32[]{:S(2)}) copy-start(s32[256]{0:T(256)} %param.11) | copy-start | bytes 3076
  132.0 0.7 copy-start.2
  132.7 23.1 %all-to-all-start.5 = ((f32[32,1,1280]{2,1,0:T(1,128)}), f32[32,1,1280]{2,1,0:T(1,128)}, u32[]{:S(2)}, u32[]{:S(2)}) async-start(f32[32,1,1280]{2,1,0:T(1,128)} %copy-done.2), calls=%async_computation.5 | async-start | bytes 327680 | tf_op jit(solution)/shard_map/all_to_all | solution.py:21
  137.3 1.4 copy-start.1
  155.8 0.9 copy-start.3
Sparse Core Ops, SparseCore 0:
  35.1 97.3 all-gather.1

commit v3 on v2

--- a/solution.py
+++ b/solution.py
@@ -10,6 +10,7 @@
 PLANE = ("tensor", "dp")
 EVERY = ("section", "tensor", "dp")
 LANES = 128
+SLOTS = 3
 VMEM_LIMIT = 24 * 1024 * 1024
 F32 = jnp.float32
 BF16 = jnp.bfloat16
@@ -165,7 +166,273 @@
         out_ref[:, columns] = (head + scale * inputs).astype(BF16)
 
 
-def on_device(residual, final_gain, table, targets, input_ids, loss_mask, embed_cotangent):
+def plan_body(ids_ref, me_ref, rows_ref, codes_ref, most_ref):
+    _, own, groups = ids_ref.shape
+    section, place, vocab_rows = me_ref[0], me_ref[1], me_ref[2]
+    device = section * groups + place
+    most = jnp.int32(0)
+    for which in range(2):
+        ids = ids_ref[which]
+        token = lax.broadcasted_iota(jnp.int32, ids.shape, 0)
+        group = lax.broadcasted_iota(jnp.int32, ids.shape, 1)
+        owner = lax.div(ids, vocab_rows)
+        again = jnp.zeros(ids.shape, jnp.int32)
+        for j in range(own):
+            again = again + jnp.where((ids == ids[j : j + 1]) & (token > j), 1, 0)
+        first = jnp.where(again == 0, 1, 0)
+        slot = jnp.zeros(ids.shape, jnp.int32)
+        for j in range(own):
+            under = (owner == owner[j : j + 1]) & (ids[j : j + 1] < ids) & (first[j : j + 1] == 1)
+            slot = slot + jnp.where(under, 1, 0)
+        most = jnp.maximum(most, jnp.max(slot))
+        rows_ref[which] = jnp.full(rows_ref.shape[1:], -1, jnp.int32)
+        mine = (owner == device) & (first == 1)
+        for k in range(SLOTS):
+            local = jnp.where(mine & (slot == k), ids - device * vocab_rows + 1, 0)
+            rows_ref[which, :, k * groups : (k + 1) * groups] = (
+                jnp.sum(local, axis=0, keepdims=True) - 1
+            )
+        near = owner - section * groups
+        code = jnp.where((near >= 0) & (near < groups), slot * groups + near, -1)
+        code = jnp.sum(jnp.where(group == place, code, 0), axis=1, keepdims=True)
+        codes_ref[which] = jnp.broadcast_to(code, codes_ref.shape[1:])
+    most_ref[0] = most
+
+
+def three_terms(x):
+    high = x.astype(BF16).astype(F32)
+    middle = (x - high).astype(BF16).astype(F32)
+    return high, middle, x - high - middle
+
+
+def slot_layout(own, width, tokens):
+    n_lanes = width // LANES
+    token_tiles = -(-tokens // LANES)
+    scalars = 2 * SLOTS * n_lanes
+    tiles = -(-(scalars + 6 * token_tiles) // own)
+    return n_lanes, token_tiles, scalars, tiles
+
+
+def compact_body(
+    res_ref, gain_ref, table_ref, target_row_ref, mask_ref, slot_rows_ref, codes_ref, cotangent_ref,
+    packed_ref, hidden_ref, inverse_ref, tokens_ref, room_ref,
+):
+    n_plane, own, packed_width = packed_ref.shape
+    tokens, width = res_ref.shape
+    vocab_rows = table_ref.shape[0]
+    n_lanes, token_tiles, scalars, tiles = slot_layout(own, width, tokens)
+    capped = capped_scores(res_ref, gain_ref, table_ref, hidden_ref, inverse_ref)
+    rows = lax.broadcasted_iota(jnp.int32, capped.shape, 0)
+    hit = target_row_ref[...] == rows
+    expterm = jnp.exp(capped)
+    bend = capped * (1.0 / 30.0)
+    weight = mask_ref[...].astype(F32) * (1.0 - bend * bend)
+    unscaled = jnp.where(hit, 0.0, weight * expterm).astype(BF16)
+    pieces = [
+        jnp.sum(expterm, axis=0, keepdims=True),
+        jnp.sum(jnp.where(hit, capped, 0.0), axis=0, keepdims=True),
+    ]
+    stride = tiles * own
+
+    def put(at, value):
+        room_ref[pl.ds(at, n_plane, stride=stride), :] = value
+
+    used = scalars + 6 * token_tiles
+    for at in range(used, stride):
+        put(at, jnp.zeros((n_plane, LANES), F32))
+    tokens_ref[...] = jnp.zeros_like(tokens_ref)
+    for which in range(2):
+        for term, value in enumerate(three_terms(pieces[which])):
+            tokens_ref[:, :tokens] = value
+            for t in range(token_tiles):
+                at = scalars + (which * 3 + term) * token_tiles + t
+                row = tokens_ref[:, t * LANES : (t + 1) * LANES]
+                put(at, jnp.broadcast_to(row, (n_plane, LANES)))
+
+    n_slots = SLOTS * n_plane
+    slot_iota = lax.broadcasted_iota(jnp.int32, (vocab_rows, n_slots), 0)
+    pick = (slot_rows_ref[0, :, :n_slots] == slot_iota).astype(F32).astype(BF16)
+    own_iota = lax.broadcasted_iota(jnp.int32, (own, n_slots), 1)
+    give = (codes_ref[1, :, :n_slots] == own_iota).astype(F32).astype(BF16)
+    dims = (((0,), (0,)), ((), ()))
+    tile = 2 * LANES
+    for n in range(width // tile):
+        columns = slice(n * tile, (n + 1) * tile)
+        part = lax.dot_general(unscaled, table_ref[:, columns], dims, preferred_element_type=F32)
+        packed_ref[:, :, columns] = part.astype(BF16).reshape(n_plane, own, tile)
+        moved = (
+            lax.dot_general(pick, table_ref[:, columns], dims, preferred_element_type=F32),
+            lax.dot_general(give, cotangent_ref[:, columns], dims, preferred_element_type=F32),
+        )
+        for which in range(2):
+            for k in range(SLOTS):
+                for half in range(2):
+                    at = (which * SLOTS + k) * n_lanes + 2 * n + half
+                    put(at, moved[which][k * n_plane : (k + 1) * n_plane, half * LANES : (half + 1) * LANES])
+    for p in range(n_plane):
+        for t in range(tiles):
+            start = p * stride + t * own
+            packed_ref[p, :, width + t * LANES : width + (t + 1) * LANES] = (
+                room_ref[start : start + own, :].astype(BF16)
+            )
+
+
+def unpack_body(
+    in_ref, place_ref, codes_ref, out_ref, rows_out_ref, room_ref, moved_ref, rest_ref
+):
+    n_plane, own, packed_width = in_ref.shape
+    tokens = n_plane * own
+    n_section = out_ref.shape[0]
+    halves = n_section // own
+    width = rows_out_ref.shape[1]
+    cut = width // halves
+    n_lanes, token_tiles, scalars, tiles = slot_layout(own, width, tokens)
+    stride = tiles * own
+    total = in_ref[0, :, :width].astype(F32)
+    for p in range(1, n_plane):
+        total = total + in_ref[p, :, :width].astype(F32)
+    for p in range(n_plane):
+        for t in range(tiles):
+            start = p * stride + t * own
+            room_ref[start : start + own, :] = in_ref[
+                p, :, width + t * LANES : width + (t + 1) * LANES
+            ].astype(F32)
+
+    def take(at):
+        return room_ref[pl.ds(at, n_plane, stride=stride), :]
+
+    for which in range(2):
+        for k in range(SLOTS):
+            for j in range(n_lanes):
+                moved_ref[
+                    which, k * n_plane : (k + 1) * n_plane, j * LANES : (j + 1) * LANES
+                ] = take((which * SLOTS + k) * n_lanes + j)
+    rows_out_ref[...] = moved_ref[1].astype(BF16)
+    n_slots = SLOTS * n_plane
+    own_iota = lax.broadcasted_iota(jnp.int32, (own, n_slots), 1)
+    choose = (codes_ref[0, :, :n_slots] == own_iota).astype(F32).astype(BF16)
+    target_rows = jnp.dot(choose, moved_ref[0].astype(BF16), preferred_element_type=F32)
+    for h in range(halves):
+        for i in range(own):
+            s = h * own + i
+            rest_ref[2 * s : 2 * s + 1, :cut] = total[i : i + 1, h * cut : (h + 1) * cut]
+            rest_ref[2 * s + 1 : 2 * s + 2, :cut] = target_rows[i : i + 1, h * cut : (h + 1) * cut]
+
+    def summed(which):
+        tiles_of = []
+        for t in range(token_tiles):
+            terms = [
+                jnp.sum(take(scalars + (which * 3 + term) * token_tiles + t), axis=0, keepdims=True)
+                for term in range(3)
+            ]
+            tiles_of.append(terms[0] + terms[1] + terms[2])
+        return tiles_of
+
+    lane = lax.broadcasted_iota(jnp.int32, (own, LANES), 1)
+    token = lax.broadcasted_iota(jnp.int32, (own, LANES), 0) + place_ref[0] * own
+    score = jnp.zeros((own, 1), F32)
+    for t, value in enumerate(summed(1)):
+        score = score + jnp.sum(
+            jnp.where(lane + t * LANES == token, jnp.broadcast_to(value, lane.shape), 0.0),
+            axis=1,
+            keepdims=True,
+        )
+    high, middle, low = three_terms(score)
+    scores = jnp.where(lane == 0, high, jnp.where(lane == 1, middle, jnp.where(lane == 2, low, 0.0)))
+    sums = [three_terms(value) for value in summed(0)]
+    extra = [sums[t][term] for term in range(3) for t in range(token_tiles)]
+    per_row = (len(extra) + 2) // 2
+    for s in range(n_section):
+        i = s % own
+        for n, value in enumerate(extra + [scores[i : i + 1]]):
+            row, column = 2 * s + n // per_row, cut + n % per_row * LANES
+            rest_ref[row : row + 1, column : column + LANES] = value
+        for n in range(len(extra) + 1, 2 * per_row):
+            row, column = 2 * s + n // per_row, cut + n % per_row * LANES
+            rest_ref[row : row + 1, column : column + LANES] = jnp.zeros((1, LANES), F32)
+    for s in range(n_section):
+        out_ref[s] = rest_ref[2 * s : 2 * s + 2, :].astype(BF16)
+
+
+def combine_body(in_ref, me_ref, mask_ref, out_ref, totals_ref, tokens_ref):
+    n_section, _, piece_width = in_ref.shape
+    cut = out_ref.shape[2]
+    tokens = totals_ref.shape[1]
+    own = me_ref[3]
+    total = in_ref[0].astype(F32)
+    for s in range(1, n_section):
+        total = total + in_ref[s].astype(F32)
+    token_tiles = -(-tokens // LANES)
+    per_row = (piece_width - cut) // LANES
+
+    def tile_of(n):
+        row, column = n // per_row, cut + n % per_row * LANES
+        return total[row : row + 1, column : column + LANES]
+
+    for t in range(token_tiles):
+        tokens_ref[:, t * LANES : (t + 1) * LANES] = (
+            tile_of(t) + tile_of(token_tiles + t) + tile_of(2 * token_tiles + t)
+        )
+    totals = tokens_ref[:, :tokens]
+    totals_ref[...] = totals
+    token = me_ref[1] * own + lax.rem(me_ref[0], own)
+    here = lax.broadcasted_iota(jnp.int32, totals.shape, 1) == token
+    whole = jnp.sum(jnp.where(here, totals, 0.0), axis=1, keepdims=True)
+    weight = jnp.sum(jnp.where(here, mask_ref[...].astype(F32), 0.0), axis=1, keepdims=True)
+    score = jnp.sum(tile_of(3 * token_tiles), axis=1, keepdims=True)
+    bend = score * (1.0 / 30.0)
+    at_target = weight * (jnp.exp(score) / whole - 1.0) * (1.0 - bend * bend)
+    at_target = at_target.astype(BF16).astype(F32)
+    grad = total[0:1, :cut] / whole + at_target * total[1:2, :cut]
+    for s in range(out_ref.shape[0]):
+        out_ref[s] = grad
+
+
+def close_body(in_ref, res_ref, gain_ref, grad_ref, gain_out_ref):
+    n_section = in_ref.shape[0]
+    own, width = res_ref.shape
+    halves = n_section // own
+    x = res_ref[...].astype(F32)
+    inverse = 1.0 / jnp.sqrt(jnp.mean(x * x, axis=1, keepdims=True) + 1e-06)
+    normed = x * inverse
+    grad_hidden = jnp.concatenate(
+        [in_ref[h * own : (h + 1) * own, 0, :] for h in range(halves)], axis=1
+    )
+    gain = jnp.sum(grad_hidden * normed, axis=0, keepdims=True)
+    for p in range(gain_out_ref.shape[0]):
+        gain_out_ref[p] = gain
+    scaled = grad_hidden * gain_ref[...]
+    along = jnp.mean(scaled * normed, axis=1, keepdims=True)
+    grad_ref[...] = ((scaled - normed * along) * inverse).astype(BF16)
+
+
+def compact_table_body(
+    target_row_ref, totals_ref, mask_ref, res_ref, gain_ref, table_ref, slot_rows_ref, moved_ref,
+    out_ref, hidden_ref, inverse_ref,
+):
+    vocab_rows, width = out_ref.shape
+    capped = capped_scores(res_ref, gain_ref, table_ref, hidden_ref, inverse_ref)
+    rows = lax.broadcasted_iota(jnp.int32, capped.shape, 0)
+    hit = (target_row_ref[...] == rows).astype(F32)
+    share = jnp.exp(capped) * (1.0 / totals_ref[...])
+    bend = capped * (1.0 / 30.0)
+    dlogits = (mask_ref[...].astype(F32) * (share - hit) * (1.0 - bend * bend)).astype(BF16)
+    n_slots = moved_ref.shape[0]
+    slot_iota = lax.broadcasted_iota(jnp.int32, (vocab_rows, n_slots), 0)
+    onehot = (slot_rows_ref[1, :, :n_slots] == slot_iota).astype(F32).astype(BF16)
+    scale = math.sqrt(width)
+    tile = 2 * LANES
+    for n in range(width // tile):
+        columns = slice(n * tile, (n + 1) * tile)
+        head = jnp.dot(dlogits, hidden_ref[:, columns], preferred_element_type=F32)
+        inputs = jnp.dot(onehot, moved_ref[:, columns], preferred_element_type=F32)
+        out_ref[:, columns] = (head + scale * inputs).astype(BF16)
+
+
+def general(
+    everyone, plan, residual, final_gain, table, targets, input_ids, loss_mask, embed_cotangent
+):
+    del plan
     own, width = residual.shape
     vocab_rows = table.shape[0]
     n_plane, n_section = lax.axis_size(PLANE), lax.axis_size("section")
@@ -183,9 +450,6 @@
     rows_bytes = vocab_rows * width * 2
 
     wide = jnp.pad(embed_cotangent, ((0, 0), (0, 512)))
-    everyone = exchange(jnp.broadcast_to(residual[None], (n_plane, own, width)), PLANE)
-    everyone = everyone.reshape(tokens, width)
-    everyone, wide = lax.optimization_barrier((everyone, wide))
     all_cotangent = lax.all_gather(wide, PLANE, axis=0, tiled=True)
 
     sums = call(
@@ -246,6 +510,115 @@
         summed, residual, gain_row,
     )
     return (grad_residual, grad_gain.reshape(width), grad_table)
+
+
+def compact(
+    everyone, plan, residual, final_gain, table, targets, input_ids, loss_mask, embed_cotangent
+):
+    del input_ids
+    slot_rows, codes, me = plan
+    own, width = residual.shape
+    vocab_rows = table.shape[0]
+    n_plane, n_section = lax.axis_size(PLANE), lax.axis_size("section")
+    tokens = own * n_plane
+    cut = own * width // n_section
+    product = 2 * tokens * vocab_rows * width
+    rows_bytes = vocab_rows * width * 2
+    shape = jax.ShapeDtypeStruct
+    _, token_tiles, _, tiles = slot_layout(own, width, tokens)
+    packed_width = width + tiles * LANES
+    piece_width = cut + (3 * token_tiles + 2) // 2 * LANES
+    norm_rooms = [pltpu.VMEM((tokens, width), BF16), pltpu.VMEM((tokens, LANES), F32)]
+    gain_row = final_gain.reshape(1, width)
+    mask = loss_mask.reshape(1, tokens)
+    target_row = targets.reshape(1, tokens) - (me[0] * n_plane + me[1]) * vocab_rows
+
+    packed = call(
+        compact_body,
+        shape((n_plane, own, packed_width), BF16),
+        2 * product,
+        rows_bytes,
+        everyone, gain_row, table, target_row, mask, slot_rows, codes, embed_cotangent,
+        scratch=norm_rooms + [
+            pltpu.VMEM((1, token_tiles * LANES), F32),
+            pltpu.VMEM((n_plane * tiles * own, LANES), F32),
+        ],
+    )
+    pieces, moved = call(
+        unpack_body,
+        (
+            shape((n_section, 2, piece_width), BF16),
+            shape((SLOTS * n_plane, width), BF16),
+        ),
+        tokens * width,
+        tokens * packed_width * 2,
+        exchange(packed, PLANE), me[1:2], codes,
+        in_specs=[VMEM, SMEM, VMEM],
+        scratch=[
+            pltpu.VMEM((n_plane * tiles * own, LANES), F32),
+            pltpu.VMEM((2, SLOTS * n_plane, width), F32),
+            pltpu.VMEM((2 * n_section, piece_width), F32),
+        ],
+    )
+    half_token, totals = call(
+        combine_body,
+        (shape((n_section, 1, cut), F32), shape((1, tokens), F32)),
+        own * width,
+        own * width * 8,
+        exchange(pieces, "section"), me, mask,
+        in_specs=[VMEM, SMEM, VMEM],
+        scratch=[pltpu.VMEM((1, token_tiles * LANES), F32)],
+    )
+    grad_table = call(
+        compact_table_body,
+        shape((vocab_rows, width), BF16),
+        3 * product,
+        2 * rows_bytes,
+        target_row, totals, mask, everyone, gain_row, table, slot_rows, moved,
+        scratch=norm_rooms,
+    )
+    summed, grad_table = lax.optimization_barrier((exchange(half_token, "section"), grad_table))
+    grad_residual, gain_part = call(
+        close_body,
+        (shape((own, width), BF16), shape((n_plane, 1, width), F32)),
+        own * width * 10,
+        own * width * 8,
+        summed, residual, gain_row,
+    )
+    grad_gain = jnp.sum(exchange(gain_part, PLANE), axis=(0, 1))
+    return (grad_residual, grad_gain, grad_table)
+
+
+def on_device(residual, final_gain, table, targets, input_ids, loss_mask, embed_cotangent):
+    own, width = residual.shape
+    n_plane = lax.axis_size(PLANE)
+    shape = jax.ShapeDtypeStruct
+    ids = jnp.stack([targets.reshape(n_plane, own).T, input_ids.reshape(n_plane, own).T])
+    place = lax.axis_index(PLANE)
+    me = jnp.stack([lax.axis_index("section"), place, table.shape[0], own]).astype(jnp.int32)
+    lanes = -(-SLOTS * n_plane // LANES) * LANES
+    everyone = exchange(jnp.broadcast_to(residual[None], (n_plane, own, width)), PLANE)
+    everyone = everyone.reshape(n_plane * own, width)
+    slot_rows, codes, most = call(
+        plan_body,
+        (
+            shape((2, 1, lanes), jnp.int32),
+            shape((2, own, lanes), jnp.int32),
+            shape((1,), jnp.int32),
+        ),
+        1000,
+        1000,
+        ids, me,
+        in_specs=[VMEM, SMEM],
+        out_specs=(VMEM, VMEM, SMEM),
+    )
+    return lax.cond(
+        most[0] < SLOTS,
+        compact,
+        general,
+        everyone, (slot_rows, codes, me), residual, final_gain, table, targets, input_ids, loss_mask,
+        embed_cotangent,
+    )
 
 
 def solution(mesh):

time: 166 us -> 151 us (0.910)
  the two profiles are of different devices: /device:TPU:2 before, /device:TPU:1 now
where the time goes in v3:
time: 151 us; the launch traced here: 150 us
  blocking collectives  79.3 us (53%)
  waiting for transfers between devices  22 us (15%)
  Pallas kernels  17.5 us (12%)
  between operations  14.8 us (10%)
  starting transfers between devices  12.6 us (8%)
  local copies, waits for them, and re-layouts  3.06 us (2%)
    all_to_all x3, blocking collectives, exchange(): return lax.all_to_all(pieces, axes, 0, 0, tiled=True)  79.3 us
    all_to_all x2, waiting for transfers between devices, exchange(): return lax.all_to_all(pieces, axes, 0, 0, tiled=True)  22 us
    pallas_call x6, Pallas kernels, call(): pl.pallas_call(body, out_shape=outs, in_specs=in_specs or [VMEM] * len(op...  17.5 us
    all_to_all x2, starting transfers between devices, exchange(): return lax.all_to_all(pieces, axes, 0, 0, tiled=True)  12.6 us
  transfers between devices with their start and end apart: 2, of which 2 were waited for; matrix products, arithmetic and copies ran while one was open for 0% of the time, Pallas kernels for 6%

profile of v3, /device:TPU:1, one launch (start us, length us, event | category | flops | bytes accessed | tf_op | source)
XLA Modules:
  0.0 149.8 jit_solution(14908569067598507459)
XLA Ops:
  7.2 2.1 %broadcast_in_dim.2 = bf16[16,16,2304]{2,1,0:T(8,128)(2,1)} broadcast(bf16[16,2304]{1,0:T(8,128)(2,1)} %param.9), dimensions={1,2} | broadcast | bytes 1253376 | tf_op jit(solution)/shard_map/broadcast_in_dim | solution.py:600
  9.4 7.6 %all-to-all-start.9 = ((bf16[16,16,2304]{2,1,0:T(8,128)(2,1)}), bf16[16,16,2304]{2,1,0:T(8,128)(2,1)}, u32[]{:S(2)}, u32[]{:S(2)}) async-start(bf16[16,16,2304]{2,1,0:T(8,128)(2,1)} %broadcast_in_dim.2), calls=%async_computation.9 | async-start | bytes 2359296 | tf_op jit(solution)/shard_map/all_to_all | solution.py:22
  17.0 0.1 reshape.47
  17.1 0.1 copy.13
  17.2 0.0 copy-done.5
  17.2 0.1 reshape.46
  17.2 0.1 copy.12
  17.3 0.1 pad_add_fusion.1.me_ref
  17.4 1.5 %shard_map.96 = (s32[2,1,128]{2,1,0:T(1,128)S(1)}, s32[2,16,128]{2,1,0:T(8,128)S(1)}, s32[1]{0:T(128)}) custom-call(s32[2,16,16]{2,1,0:T(8,128)S(1)} %pad_add_fusion.ids_ref, s32[4]{0:T(128)S(1)} %pad_add_fusion.1.me_ref), custom_call_target="tpu_custom_call" | custom-call | flops 1000 | bytes 1000 | tf_op jit(solution)/shard_map/pallas_call | solution.py:27
  19.6 11.8 %all-to-all-done.9 = bf16[16,16,2304]{2,1,0:T(8,128)(2,1)} async-done(((bf16[16,16,2304]{2,1,0:T(8,128)(2,1)}), bf16[16,16,2304]{2,1,0:T(8,128)(2,1)}, u32[]{:S(2)}, u32[]{:S(2)}) %all-to-all-start.9) | async-done | bytes 1179680 | tf_op jit(solution)/shard_map/all_to_all | solution.py:22
  31.5 110.8 %conditional.1 = (bf16[16,2304]{1,0:T(8,128)(2,1)}, bf16[500,2304]{1,0:T(8,128)(2,1)}, f32[2304]{0:T(1024)S(1)}) conditional(s32[]{:T(128)} %bitcast.13, (f32[2304]{0:T(1024)S(1)}, bf16[256,2304]{1,0:T(8,128)(2,1)}, bf16[500,2304]{1,0:T(8,128)(2,1)S(1)}, s32[256]{0:T(256)S(1)}, s32[256]{0:T(256)S(1)}, /*index=5*/s32[256]{0:T(256)S(1)}, ...), branch_computations={%region_0.1_spmd, %region_1.3_spmd} | conditional | flops 3539939584 | bytes 25218350 | solution.py:615
  31.5 5.9 %branch_1_fun.5 = bf16[16,16,3328]{2,1,0:T(8,128)(2,1)S(1)} custom-call(bf16[256,2304]{1,0:T(8,128)(2,1)} %get-tuple-element.54.res_ref, f32[1,2304]{1,0:T(1,128)S(1)} %reshape.41.gain_ref, bf16[500,2304]{1,0:T(8,128)(2,1)S(1)} %get-tuple-element.56.table_ref, s32[1,256]{1,0:T(1,128)S(1)} %bitcast.17, s32[1,256]{1,0:T(1,128)S(1)} %bitcast.25, ...), custom_call_target="tpu_custom_call" | custom-call | flops 1179648000 | bytes 2304000 | tf_op jit(solution)/shard_map/cond/branch_1_fun/pallas_call | solution.py:27
  37.4 29.8 %all_to_all.44.in_ref = bf16[16,16,3328]{2,1,0:T(8,128)(2,1)S(1)} all-to-all(bf16[16,16,3328]{2,1,0:T(8,128)(2,1)S(1)} %branch_1_fun.5), channel_id=1, replica_groups=mesh['section'=32,'tensor'=2,'dp'=8] {'tensor','dp'}, dimensions={0} | all-to-all | bytes 3407872 | tf_op jit(solution)/shard_map/cond/branch_1_fun/all_to_all | solution.py:22
  67.2 1.0 branch_1_fun.6
  68.3 38.8 %all_to_all.45.in_ref = bf16[32,2,1664]{2,1,0:T(2,128)(2,1)S(1)} all-to-all(bf16[32,2,1664]{2,1,0:T(2,128)(2,1)S(1)} %get-tuple-element.65), channel_id=1, replica_groups=mesh['section'=32,'tensor'=2,'dp'=8] {'section'}, dimensions={0} | all-to-all | bytes 425984 | tf_op jit(solution)/shard_map/cond/branch_1_fun/all_to_all | solution.py:22
  107.1 1.4 branch_1_fun.7
  108.5 5.0 %all-to-all-start.7 = ((f32[32,1,1152]{2,1,0:T(1,128)}), f32[32,1,1152]{2,1,0:T(1,128)S(1)}, u32[]{:S(2)}, u32[]{:S(2)}) async-start(f32[32,1,1152]{2,1,0:T(1,128)} %get-tuple-element.67), calls=%async_computation.7 | async-start | bytes 294912 | tf_op jit(solution)/shard_map/cond/branch_1_fun/all_to_all | solution.py:22
  113.5 6.7 %branch_1_fun.8 = bf16[500,2304]{1,0:T(8,128)(2,1)} custom-call(s32[1,256]{1,0:T(1,128)S(1)} %bitcast.18, f32[1,256]{1,0:T(1,128)S(1)} %get-tuple-element.68.totals_ref, s32[1,256]{1,0:T(1,128)S(1)} %bitcast.27, bf16[256,2304]{1,0:T(8,128)(2,1)} %get-tuple-element.54.res_ref, f32[1,2304]{1,0:T(1,128)S(1)} %reshape.41.gain_ref, ...), custom_call_target="tpu_custom_call" | custom-call | flops 1769472000 | bytes 4608000 | tf_op jit(solution)/shard_map/cond/branch_1_fun/pallas_call | solution.py:27
  120.2 10.2 %all-to-all-done.7.in_ref = f32[32,1,1152]{2,1,0:T(1,128)S(1)} async-done(((f32[32,1,1152]{2,1,0:T(1,128)}), f32[32,1,1152]{2,1,0:T(1,128)S(1)}, u32[]{:S(2)}, u32[]{:S(2)}) %all-to-all-start.7) | async-done | bytes 147488 | tf_op jit(solution)/shard_map/cond/branch_1_fun/all_to_all | solution.py:22
  130.4 0.9 branch_1_fun.9
  131.3 10.7 %all_to_all.46 = f32[16,1,2304]{2,1,0:T(1,128)S(1)} all-to-all(f32[16,1,2304]{2,1,0:T(1,128)S(1)} %get-tuple-element.73), channel_id=1, replica_groups=mesh['section'=32,'tensor'=2,'dp'=8] {'tensor','dp'}, dimensions={0} | all-to-all | bytes 294912 | tf_op jit(solution)/shard_map/cond/branch_1_fun/all_to_all | solution.py:22
  142.0 0.1 reduce_sum.8
  142.3 0.0 copy-start.8
  142.3 0.6 copy-done.8
  (16 shorter events, 0.0 us)
Async XLA Ops:
  7.2 24.3 %copy-start.2 = (bf16[16,2304]{1,0:T(8,128)(2,1)S(1)}, bf16[16,2304]{1,0:T(8,128)(2,1)}, u32[]{:S(2)}) copy-start(bf16[16,2304]{1,0:T(8,128)(2,1)} %param.9) | copy-start | bytes 221188
  7.2 9.8 %copy-start.7 = (s32[256]{0:T(256)S(1)}, s32[256]{0:T(256)}, u32[]{:S(2)}) copy-start(s32[256]{0:T(256)} %param.13) | copy-start | bytes 3076
  7.2 10.0 %copy-start.5 = (s32[256]{0:T(256)S(1)}, s32[256]{0:T(256)}, u32[]{:S(2)}) copy-start(s32[256]{0:T(256)} %param.12) | copy-start | bytes 3076
  7.2 24.3 %copy-start.4 = (f32[2304]{0:T(1024)S(1)}, f32[2304]{0:T(1024)}, u32[]{:S(2)}) copy-start(f32[2304]{0:T(1024)} %param.10) | copy-start | bytes 27652
  7.2 24.2 %copy-start.1 = (bf16[500,2304]{1,0:T(8,128)(2,1)S(1)}, bf16[500,2304]{1,0:T(8,128)(2,1)}, u32[]{:S(2)}) copy-start(bf16[500,2304]{1,0:T(8,128)(2,1)} %param.11) | copy-start | bytes 6912004
  7.2 24.2 %copy-start.6 = (s32[256]{0:T(256)S(1)}, s32[256]{0:T(256)}, u32[]{:S(2)}) copy-start(s32[256]{0:T(256)} %param.14) | copy-start | bytes 3076
  7.2 24.2 %copy-start.3 = (bf16[16,2304]{1,0:T(8,128)(2,1)S(1)}, bf16[16,2304]{1,0:T(8,128)(2,1)}, u32[]{:S(2)}) copy-start(bf16[16,2304]{1,0:T(8,128)(2,1)} %param.15) | copy-start | bytes 221188
  9.4 22.1 %all-to-all-start.9 = ((bf16[16,16,2304]{2,1,0:T(8,128)(2,1)}), bf16[16,16,2304]{2,1,0:T(8,128)(2,1)}, u32[]{:S(2)}, u32[]{:S(2)}) async-start(bf16[16,16,2304]{2,1,0:T(8,128)(2,1)} %broadcast_in_dim.2), calls=%async_computation.9 | async-start | bytes 2359296 | tf_op jit(solution)/shard_map/all_to_all | solution.py:22
  108.5 21.9 %all-to-all-start.7 = ((f32[32,1,1152]{2,1,0:T(1,128)}), f32[32,1,1152]{2,1,0:T(1,128)S(1)}, u32[]{:S(2)}, u32[]{:S(2)}) async-start(f32[32,1,1152]{2,1,0:T(1,128)} %get-tuple-element.67), calls=%async_computation.7 | async-start | bytes 294912 | tf_op jit(solution)/shard_map/cond/branch_1_fun/all_to_all | solution.py:22
  142.3 0.6 copy-start.8

commit v4 on v3

--- a/solution.py
+++ b/solution.py
@@ -8,13 +8,16 @@
 from jax.sharding import PartitionSpec as P
 
 PLANE = ("tensor", "dp")
-EVERY = ("section", "tensor", "dp")
+SECTION = ("z", "core")
+CHIPS = ("core", "tensor", "dp")
+EVERY = ("z", "core", "tensor", "dp")
 LANES = 128
 SLOTS = 3
 VMEM_LIMIT = 24 * 1024 * 1024
 F32 = jnp.float32
 BF16 = jnp.bfloat16
 VMEM = pl.BlockSpec(memory_space=pltpu.VMEM)
+ANY = pl.BlockSpec(memory_space=pl.ANY)
 SMEM = pl.BlockSpec(memory_space=pltpu.SMEM)
 
 
@@ -35,7 +38,7 @@
     )(*operands)
 
 
-def capped_scores(res_ref, gain_ref, table_ref, hidden_ref, inverse_ref):
+def norm_rows(res_ref, gain_ref, hidden_ref, inverse_ref):
     tokens = res_ref.shape[0]
     step = 16
 
@@ -48,10 +51,18 @@
         return carry
 
     lax.fori_loop(0, tokens // step, norm, 0, unroll=4)
+
+
+def scores_of(table_ref, hidden_ref):
     scores = lax.dot_general(
         table_ref[...], hidden_ref[...], (((1,), (1,)), ((), ())), preferred_element_type=F32
     )
     return 30.0 * jnp.tanh(scores * (1.0 / 30.0))
+
+
+def capped_scores(res_ref, gain_ref, table_ref, hidden_ref, inverse_ref):
+    norm_rows(res_ref, gain_ref, hidden_ref, inverse_ref)
+    return scores_of(table_ref, hidden_ref)
 
 
 def logit_grads(capped, first_ref, arrived_ref, targets_ref, mask_ref):
@@ -208,20 +219,67 @@
 def slot_layout(own, width, tokens):
     n_lanes = width // LANES
     token_tiles = -(-tokens // LANES)
-    scalars = 2 * SLOTS * n_lanes
-    tiles = -(-(scalars + 6 * token_tiles) // own)
-    return n_lanes, token_tiles, scalars, tiles
+    scalar_tiles = -(-6 * token_tiles // own)
+    slot_tiles = -(-2 * SLOTS * n_lanes // own)
+    return n_lanes, token_tiles, scalar_tiles, slot_tiles
+
+
+def slots_body(table_ref, slot_rows_ref, codes_ref, cotangent_ref, out_ref, room_ref):
+    n_plane, own, _ = out_ref.shape
+    vocab_rows, width = table_ref.shape
+    n_lanes, _, _, tiles = slot_layout(own, width, own * n_plane)
+    stride = tiles * own
+
+    def put(at, value):
+        room_ref[pl.ds(at, n_plane, stride=stride), :] = value
+
+    for at in range(2 * SLOTS * n_lanes, stride):
+        put(at, jnp.zeros((n_plane, LANES), F32))
+    n_slots = SLOTS * n_plane
+    slot_iota = lax.broadcasted_iota(jnp.int32, (vocab_rows, n_slots), 0)
+    pick = (slot_rows_ref[0, :, :n_slots] == slot_iota).astype(F32).astype(BF16)
+    own_iota = lax.broadcasted_iota(jnp.int32, (own, n_slots), 1)
+    give = (codes_ref[1, :, :n_slots] == own_iota).astype(F32).astype(BF16)
+    dims = (((0,), (0,)), ((), ()))
+    tile = 2 * LANES
+    for n in range(width // tile):
+        columns = slice(n * tile, (n + 1) * tile)
+        moved = (
+            lax.dot_general(pick, table_ref[:, columns], dims, preferred_element_type=F32),
+            lax.dot_general(give, cotangent_ref[:, columns], dims, preferred_element_type=F32),
+        )
+        for which in range(2):
+            for k in range(SLOTS):
+                block = moved[which][k * n_plane : (k + 1) * n_plane]
+                for half in range(2):
+                    at = (which * SLOTS + k) * n_lanes + 2 * n + half
+                    put(at, block[:, half * LANES : (half + 1) * LANES])
+    for p in range(n_plane):
+        for t in range(tiles):
+            start = p * stride + t * own
+            out_ref[p, :, t * LANES : (t + 1) * LANES] = (
+                room_ref[start : start + own, :].astype(BF16)
+            )
 
 
 def compact_body(
-    res_ref, gain_ref, table_ref, target_row_ref, mask_ref, slot_rows_ref, codes_ref, cotangent_ref,
-    packed_ref, hidden_ref, inverse_ref, tokens_ref, room_ref,
+    res_hbm, table_hbm, slots_hbm, gain_ref, target_row_ref, mask_ref,
+    packed_ref, res_ref, table_ref, slots_ref, hidden_ref, inverse_ref, tokens_ref, room_ref, sems,
 ):
+    copies = [
+        pltpu.make_async_copy(res_hbm, res_ref, sems.at[0]),
+        pltpu.make_async_copy(table_hbm, table_ref, sems.at[1]),
+        pltpu.make_async_copy(slots_hbm, slots_ref, sems.at[2]),
+    ]
+    for copy in copies:
+        copy.start()
     n_plane, own, packed_width = packed_ref.shape
     tokens, width = res_ref.shape
-    vocab_rows = table_ref.shape[0]
-    n_lanes, token_tiles, scalars, tiles = slot_layout(own, width, tokens)
-    capped = capped_scores(res_ref, gain_ref, table_ref, hidden_ref, inverse_ref)
+    n_lanes, token_tiles, scalar_tiles, _ = slot_layout(own, width, tokens)
+    copies[0].wait()
+    norm_rows(res_ref, gain_ref, hidden_ref, inverse_ref)
+    copies[1].wait()
+    capped = scores_of(table_ref, hidden_ref)
     rows = lax.broadcasted_iota(jnp.int32, capped.shape, 0)
     hit = target_row_ref[...] == rows
     expterm = jnp.exp(capped)
@@ -232,49 +290,27 @@
         jnp.sum(expterm, axis=0, keepdims=True),
         jnp.sum(jnp.where(hit, capped, 0.0), axis=0, keepdims=True),
     ]
-    stride = tiles * own
-
-    def put(at, value):
-        room_ref[pl.ds(at, n_plane, stride=stride), :] = value
-
-    used = scalars + 6 * token_tiles
-    for at in range(used, stride):
-        put(at, jnp.zeros((n_plane, LANES), F32))
     tokens_ref[...] = jnp.zeros_like(tokens_ref)
+    room_ref[...] = jnp.zeros_like(room_ref)
     for which in range(2):
         for term, value in enumerate(three_terms(pieces[which])):
             tokens_ref[:, :tokens] = value
             for t in range(token_tiles):
-                at = scalars + (which * 3 + term) * token_tiles + t
-                row = tokens_ref[:, t * LANES : (t + 1) * LANES]
-                put(at, jnp.broadcast_to(row, (n_plane, LANES)))
-
-    n_slots = SLOTS * n_plane
-    slot_iota = lax.broadcasted_iota(jnp.int32, (vocab_rows, n_slots), 0)
-    pick = (slot_rows_ref[0, :, :n_slots] == slot_iota).astype(F32).astype(BF16)
-    own_iota = lax.broadcasted_iota(jnp.int32, (own, n_slots), 1)
-    give = (codes_ref[1, :, :n_slots] == own_iota).astype(F32).astype(BF16)
-    dims = (((0,), (0,)), ((), ()))
+                at = (which * 3 + term) * token_tiles + t
+                room_ref[at : at + 1, :] = tokens_ref[:, t * LANES : (t + 1) * LANES]
+    for t in range(scalar_tiles):
+        block = room_ref[t * own : (t + 1) * own, :].astype(BF16)
+        for p in range(n_plane):
+            packed_ref[p, :, width + t * LANES : width + (t + 1) * LANES] = block
     tile = 2 * LANES
     for n in range(width // tile):
         columns = slice(n * tile, (n + 1) * tile)
-        part = lax.dot_general(unscaled, table_ref[:, columns], dims, preferred_element_type=F32)
+        part = lax.dot_general(
+            unscaled, table_ref[:, columns], (((0,), (0,)), ((), ())), preferred_element_type=F32
+        )
         packed_ref[:, :, columns] = part.astype(BF16).reshape(n_plane, own, tile)
-        moved = (
-            lax.dot_general(pick, table_ref[:, columns], dims, preferred_element_type=F32),
-            lax.dot_general(give, cotangent_ref[:, columns], dims, preferred_element_type=F32),
-        )
-        for which in range(2):
-            for k in range(SLOTS):
-                for half in range(2):
-                    at = (which * SLOTS + k) * n_lanes + 2 * n + half
-                    put(at, moved[which][k * n_plane : (k + 1) * n_plane, half * LANES : (half + 1) * LANES])
-    for p in range(n_plane):
-        for t in range(tiles):
-            start = p * stride + t * own
-            packed_ref[p, :, width + t * LANES : width + (t + 1) * LANES] = (
-                room_ref[start : start + own, :].astype(BF16)
-            )
+    copies[2].wait()
+    packed_ref[:, :, width + scalar_tiles * LANES :] = slots_ref[...]
 
 
 def unpack_body(
@@ -286,7 +322,8 @@
     halves = n_section // own
     width = rows_out_ref.shape[1]
     cut = width // halves
-    n_lanes, token_tiles, scalars, tiles = slot_layout(own, width, tokens)
+    n_lanes, token_tiles, scalar_tiles, slot_tiles = slot_layout(own, width, tokens)
+    tiles = scalar_tiles + slot_tiles
     stride = tiles * own
     total = in_ref[0, :, :width].astype(F32)
     for p in range(1, n_plane):
@@ -306,7 +343,7 @@
             for j in range(n_lanes):
                 moved_ref[
                     which, k * n_plane : (k + 1) * n_plane, j * LANES : (j + 1) * LANES
-                ] = take((which * SLOTS + k) * n_lanes + j)
+                ] = take(scalar_tiles * own + (which * SLOTS + k) * n_lanes + j)
     rows_out_ref[...] = moved_ref[1].astype(BF16)
     n_slots = SLOTS * n_plane
     own_iota = lax.broadcasted_iota(jnp.int32, (own, n_slots), 1)
@@ -314,7 +351,7 @@
     target_rows = jnp.dot(choose, moved_ref[0].astype(BF16), preferred_element_type=F32)
     for h in range(halves):
         for i in range(own):
-            s = h * own + i
+            s = i * halves + h
             rest_ref[2 * s : 2 * s + 1, :cut] = total[i : i + 1, h * cut : (h + 1) * cut]
             rest_ref[2 * s + 1 : 2 * s + 2, :cut] = target_rows[i : i + 1, h * cut : (h + 1) * cut]
 
@@ -322,7 +359,7 @@
         tiles_of = []
         for t in range(token_tiles):
             terms = [
-                jnp.sum(take(scalars + (which * 3 + term) * token_tiles + t), axis=0, keepdims=True)
+                jnp.sum(take((which * 3 + term) * token_tiles + t), axis=0, keepdims=True)
                 for term in range(3)
             ]
             tiles_of.append(terms[0] + terms[1] + terms[2])
@@ -343,7 +380,7 @@
     extra = [sums[t][term] for term in range(3) for t in range(token_tiles)]
     per_row = (len(extra) + 2) // 2
     for s in range(n_section):
-        i = s % own
+        i = s // halves
         for n, value in enumerate(extra + [scores[i : i + 1]]):
             row, column = 2 * s + n // per_row, cut + n % per_row * LANES
             rest_ref[row : row + 1, column : column + LANES] = value
@@ -358,7 +395,8 @@
     n_section, _, piece_width = in_ref.shape
     cut = out_ref.shape[2]
     tokens = totals_ref.shape[1]
-    own = me_ref[3]
+    own = out_ref.shape[0]
+    halves = n_section // own
     total = in_ref[0].astype(F32)
     for s in range(1, n_section):
         total = total + in_ref[s].astype(F32)
@@ -375,7 +413,7 @@
         )
     totals = tokens_ref[:, :tokens]
     totals_ref[...] = totals
-    token = me_ref[1] * own + lax.rem(me_ref[0], own)
+    token = me_ref[1] * own + lax.div(me_ref[0], halves)
     here = lax.broadcasted_iota(jnp.int32, totals.shape, 1) == token
     whole = jnp.sum(jnp.where(here, totals, 0.0), axis=1, keepdims=True)
     weight = jnp.sum(jnp.where(here, mask_ref[...].astype(F32), 0.0), axis=1, keepdims=True)
@@ -388,20 +426,27 @@
         out_ref[s] = grad
 
 
-def close_body(in_ref, res_ref, gain_ref, grad_ref, gain_out_ref):
-    n_section = in_ref.shape[0]
-    own, width = res_ref.shape
-    halves = n_section // own
+def normed_rows(res_ref):
     x = res_ref[...].astype(F32)
     inverse = 1.0 / jnp.sqrt(jnp.mean(x * x, axis=1, keepdims=True) + 1e-06)
-    normed = x * inverse
-    grad_hidden = jnp.concatenate(
-        [in_ref[h * own : (h + 1) * own, 0, :] for h in range(halves)], axis=1
-    )
-    gain = jnp.sum(grad_hidden * normed, axis=0, keepdims=True)
-    for p in range(gain_out_ref.shape[0]):
-        gain_out_ref[p] = gain
-    scaled = grad_hidden * gain_ref[...]
+    return x * inverse, inverse
+
+
+def gain_body(in_ref, core_ref, res_ref, out_ref):
+    own, _, cut = in_ref.shape
+    normed, _ = normed_rows(res_ref)
+    half = jnp.where(core_ref[0] == 0, normed[:, :cut], normed[:, cut:])
+    gain = jnp.sum(in_ref[:, 0, :] * half, axis=0, keepdims=True)
+    for i in range(out_ref.shape[0]):
+        out_ref[i] = gain
+
+
+def close_body(in_ref, other_ref, core_ref, res_ref, gain_ref, grad_ref):
+    mine, other = in_ref[:, 0, :], other_ref[:, 0, :]
+    at_left = core_ref[0] == 0
+    left, right = jnp.where(at_left, mine, other), jnp.where(at_left, other, mine)
+    normed, inverse = normed_rows(res_ref)
+    scaled = jnp.concatenate([left, right], axis=1) * gain_ref[...]
     along = jnp.mean(scaled * normed, axis=1, keepdims=True)
     grad_ref[...] = ((scaled - normed * along) * inverse).astype(BF16)
 
@@ -435,7 +480,7 @@
     del plan
     own, width = residual.shape
     vocab_rows = table.shape[0]
-    n_plane, n_section = lax.axis_size(PLANE), lax.axis_size("section")
+    n_plane, n_section = lax.axis_size(PLANE), lax.axis_size(SECTION)
     tokens = own * n_plane
     cut = own * width // n_section
     n_lanes = width // LANES
@@ -461,7 +506,7 @@
         scratch=norm_rooms,
     )
     sums = call(
-        spread_body, shape((n_plane, 1, tokens), F32), tokens, 4 * tokens, exchange(sums, "section")
+        spread_body, shape((n_plane, 1, tokens), F32), tokens, 4 * tokens, exchange(sums, SECTION)
     )
     given = (
         first, exchange(sums, PLANE), targets.reshape(1, tokens), loss_mask.reshape(1, tokens),
@@ -490,7 +535,7 @@
         shape((n_section, 1, cut + LANES), F32),
         own * width,
         own * width * 8,
-        exchange(split, "section"),
+        exchange(split, SECTION),
     )
     grad_table = call(
         table_body,
@@ -501,7 +546,7 @@
         in_specs=[SMEM] + [VMEM] * 8,
         scratch=norm_rooms,
     )
-    summed, grad_table = lax.optimization_barrier((exchange(reduced, "section"), grad_table))
+    summed, grad_table = lax.optimization_barrier((exchange(reduced, SECTION), grad_table))
     grad_residual, grad_gain = call(
         finish_body,
         (shape((own, width), BF16), shape((n_lanes, LANES), F32)),
@@ -515,17 +560,18 @@
 def compact(
     everyone, plan, residual, final_gain, table, targets, input_ids, loss_mask, embed_cotangent
 ):
-    del input_ids
-    slot_rows, codes, me = plan
+    del input_ids, embed_cotangent
+    slot_rows, codes, slots, me = plan
     own, width = residual.shape
     vocab_rows = table.shape[0]
-    n_plane, n_section = lax.axis_size(PLANE), lax.axis_size("section")
+    n_plane, n_section = lax.axis_size(PLANE), lax.axis_size(SECTION)
     tokens = own * n_plane
     cut = own * width // n_section
     product = 2 * tokens * vocab_rows * width
     rows_bytes = vocab_rows * width * 2
     shape = jax.ShapeDtypeStruct
-    _, token_tiles, _, tiles = slot_layout(own, width, tokens)
+    _, token_tiles, scalar_tiles, slot_tiles = slot_layout(own, width, tokens)
+    tiles = scalar_tiles + slot_tiles
     packed_width = width + tiles * LANES
     piece_width = cut + (3 * token_tiles + 2) // 2 * LANES
     norm_rooms = [pltpu.VMEM((tokens, width), BF16), pltpu.VMEM((tokens, LANES), F32)]
@@ -538,10 +584,16 @@
         shape((n_plane, own, packed_width), BF16),
         2 * product,
         rows_bytes,
-        everyone, gain_row, table, target_row, mask, slot_rows, codes, embed_cotangent,
-        scratch=norm_rooms + [
+        everyone, table, slots, gain_row, target_row, mask,
+        in_specs=[ANY] * 3 + [VMEM] * 3,
+        scratch=[
+            pltpu.VMEM((tokens, width), BF16),
+            pltpu.VMEM((vocab_rows, width), BF16),
+            pltpu.VMEM((n_plane, own, slot_tiles * LANES), BF16),
+        ] + norm_rooms + [
             pltpu.VMEM((1, token_tiles * LANES), F32),
-            pltpu.VMEM((n_plane * tiles * own, LANES), F32),
+            pltpu.VMEM((scalar_tiles * own, LANES), F32),
+            pltpu.SemaphoreType.DMA((3,)),
         ],
     )
     pieces, moved = call(
@@ -562,10 +614,10 @@
     )
     half_token, totals = call(
         combine_body,
-        (shape((n_section, 1, cut), F32), shape((1, tokens), F32)),
+        (shape((own, 1, cut), F32), shape((1, tokens), F32)),
         own * width,
         own * width * 8,
-        exchange(pieces, "section"), me, mask,
+        exchange(pieces, SECTION), me, mask,
         in_specs=[VMEM, SMEM, VMEM],
         scratch=[pltpu.VMEM((1, token_tiles * LANES), F32)],
     )
@@ -577,16 +629,28 @@
         target_row, totals, mask, everyone, gain_row, table, slot_rows, moved,
         scratch=norm_rooms,
     )
-    summed, grad_table = lax.optimization_barrier((exchange(half_token, "section"), grad_table))
-    grad_residual, gain_part = call(
+    mine, grad_table = lax.optimization_barrier((exchange(half_token, "z"), grad_table))
+    core = lax.axis_index("core").astype(jnp.int32).reshape(1)
+    n_chips = lax.axis_size(CHIPS)
+    other = lax.ppermute(mine, "core", [(0, 1), (1, 0)])
+    gain_part = call(
+        gain_body,
+        shape((n_chips, 1, cut), F32),
+        own * width * 4,
+        own * width * 8,
+        mine, core, residual,
+        in_specs=[VMEM, SMEM, VMEM],
+    )
+    grad_residual = call(
         close_body,
-        (shape((own, width), BF16), shape((n_plane, 1, width), F32)),
+        shape((own, width), BF16),
         own * width * 10,
         own * width * 8,
-        summed, residual, gain_row,
-    )
-    grad_gain = jnp.sum(exchange(gain_part, PLANE), axis=(0, 1))
-    return (grad_residual, grad_gain, grad_table)
+        mine, other, core, residual, gain_row,
+        in_specs=[VMEM, VMEM, SMEM, VMEM, VMEM],
+    )
+    grad_gain = exchange(gain_part, CHIPS).reshape(n_chips // n_plane, n_plane, cut)
+    return (grad_residual, jnp.sum(grad_gain, axis=1).reshape(width), grad_table)
 
 
 def on_device(residual, final_gain, table, targets, input_ids, loss_mask, embed_cotangent):
@@ -595,7 +659,7 @@
     shape = jax.ShapeDtypeStruct
     ids = jnp.stack([targets.reshape(n_plane, own).T, input_ids.reshape(n_plane, own).T])
     place = lax.axis_index(PLANE)
-    me = jnp.stack([lax.axis_index("section"), place, table.shape[0], own]).astype(jnp.int32)
+    me = jnp.stack([lax.axis_index(SECTION), place, table.shape[0], own]).astype(jnp.int32)
     lanes = -(-SLOTS * n_plane // LANES) * LANES
     everyone = exchange(jnp.broadcast_to(residual[None], (n_plane, own, width)), PLANE)
     everyone = everyone.reshape(n_plane * own, width)
@@ -612,16 +676,28 @@
         in_specs=[VMEM, SMEM],
         out_specs=(VMEM, VMEM, SMEM),
     )
+    slot_tiles = slot_layout(own, width, own * n_plane)[3]
+    slots = call(
+        slots_body,
+        shape((n_plane, own, slot_tiles * LANES), BF16),
+        1000,
+        1000,
+        table, slot_rows, codes, embed_cotangent,
+        scratch=[pltpu.VMEM((n_plane * slot_tiles * own, LANES), F32)],
+    )
     return lax.cond(
         most[0] < SLOTS,
         compact,
         general,
-        everyone, (slot_rows, codes, me), residual, final_gain, table, targets, input_ids, loss_mask,
+        everyone, (slot_rows, codes, slots, me), residual, final_gain, table, targets, input_ids, loss_mask,
         embed_cotangent,
     )
 
 
 def solution(mesh):
+    cores = 2
+    devices = mesh.devices.reshape(-1, cores, *mesh.devices.shape[1:])
+    fine = jax.sharding.Mesh(devices, EVERY)
     placed = (
         P(PLANE, None),
         P(),
@@ -633,7 +709,7 @@
     )
     return jax.shard_map(
         on_device,
-        mesh=mesh,
+        mesh=fine,
         in_specs=placed,
         out_specs=(P(PLANE, None), P(), P(EVERY, None)),
         check_vma=False,

time: 151 us -> 146 us (0.967)
  blocking collectives: 79.3 us -> 68.6 us
  starting transfers between devices: 12.6 us -> 20.1 us
    all_to_all x3 -> x2, blocking collectives: 79.3 us -> 68.6 us  [exchange(): return lax.all_to_all(pieces, axes, 0, 0, tiled=True)]
    all_to_all x2 -> x3, starting transfers between devices: 12.6 us -> 17.9 us  [exchange(): return lax.all_to_all(pieces, axes, 0, 0, tiled=True)]
    ppermute x0 -> x1, starting transfers between devices: none -> 2.14 us  [compact(): other = lax.ppermute(mine, 'core', [(0, 1), (1, 0)])]
    all_to_all x2 -> x3, waiting for transfers between devices: 22 us -> 20.2 us  [exchange(): return lax.all_to_all(pieces, axes, 0, 0, tiled=True)]
    pallas_call x6 -> x8, Pallas kernels: 17.5 us -> 17.4 us  [call(): pl.pallas_call(body, out_shape=outs, in_specs=in_specs or [VMEM] * len(op...]
  transfers between devices with their start and end apart: 2 -> 4, of which waited for: 2 -> 4; matrix products, arithmetic and copies ran while one was open for 0% -> 0% of each run, Pallas kernels for 6% -> 6%
where the time goes in v4:
time: 146 us
  blocking collectives  68.6 us (47%)
  waiting for transfers between devices  21.2 us (15%)
  starting transfers between devices  20.1 us (14%)
  Pallas kernels  17.4 us (12%)
  between operations  14.8 us (10%)
  local copies, waits for them, and re-layouts  3.11 us (2%)
    all_to_all x2, blocking collectives, exchange(): return lax.all_to_all(pieces, axes, 0, 0, tiled=True)  68.6 us
    all_to_all x3, waiting for transfers between devices, exchange(): return lax.all_to_all(pieces, axes, 0, 0, tiled=True)  20.2 us
    all_to_all x3, starting transfers between devices, exchange(): return lax.all_to_all(pieces, axes, 0, 0, tiled=True)  17.9 us
    pallas_call x8, Pallas kernels, call(): pl.pallas_call(body, out_shape=outs, in_specs=in_specs or [VMEM] * len(op...  17.4 us
  transfers between devices with their start and end apart: 4, of which 4 were waited for; matrix products, arithmetic and copies ran while one was open for 0% of the time, Pallas kernels for 6%

profile of v4, /device:TPU:1, one launch (start us, length us, event | category | flops | bytes accessed | tf_op | source)
XLA Modules:
  0.0 145.7 jit_solution(16595915183877459633)
XLA Ops:
  7.2 2.1 %broadcast_in_dim.2 = bf16[16,16,2304]{2,1,0:T(8,128)(2,1)} broadcast(bf16[16,2304]{1,0:T(8,128)(2,1)} %param.9), dimensions={1,2} | broadcast | bytes 1253376 | tf_op jit(solution)/shard_map/broadcast_in_dim | solution.py:664
  9.3 7.6 %all-to-all-start.9 = ((bf16[16,16,2304]{2,1,0:T(8,128)(2,1)}), bf16[16,16,2304]{2,1,0:T(8,128)(2,1)}, u32[]{:S(2)}, u32[]{:S(2)}) async-start(bf16[16,16,2304]{2,1,0:T(8,128)(2,1)} %broadcast_in_dim.2), calls=%async_computation.9 | async-start | bytes 2359296 | tf_op jit(solution)/shard_map/all_to_all | solution.py:25
  17.0 0.1 reshape.56
  17.2 0.1 reshape.55
  17.3 0.1 pad_add_fusion.1.me_ref
  17.4 1.5 %shard_map.96 = (s32[2,1,128]{2,1,0:T(1,128)S(1)}, s32[2,16,128]{2,1,0:T(8,128)S(1)}, s32[1]{0:T(128)}) custom-call(s32[2,16,16]{2,1,0:T(8,128)S(1)} %pad_add_fusion.ids_ref, s32[4]{0:T(128)S(1)} %pad_add_fusion.1.me_ref), custom_call_target="tpu_custom_call" | custom-call | flops 1000 | bytes 1000 | tf_op jit(solution)/shard_map/pallas_call | solution.py:30
  19.0 0.7 shard_map.97
  20.3 11.1 %all-to-all-done.9 = bf16[16,16,2304]{2,1,0:T(8,128)(2,1)} async-done(((bf16[16,16,2304]{2,1,0:T(8,128)(2,1)}), bf16[16,16,2304]{2,1,0:T(8,128)(2,1)}, u32[]{:S(2)}, u32[]{:S(2)}) %all-to-all-start.9) | async-done | bytes 1179680 | tf_op jit(solution)/shard_map/all_to_all | solution.py:25
  31.4 106.8 %conditional.1 = (bf16[16,2304]{1,0:T(8,128)(2,1)S(1)}, bf16[500,2304]{1,0:T(8,128)(2,1)}, f32[2304]{0:T(1024)S(1)}) conditional(s32[]{:T(128)} %bitcast.14, (f32[2304]{0:T(1024)S(1)}, bf16[256,2304]{1,0:T(8,128)(2,1)}, bf16[500,2304]{1,0:T(8,128)(2,1)S(1)}, s32[256]{0:T(256)S(1)}, s32[256]{0:T(256)S(1)}, /*index=5*/s32[256]{0:T(256)S(1)}, ...), branch_computations={%region_0.1_spmd, %region_1.3_spmd} | conditional | flops 3539939584 | bytes 25218406 | solution.py:688
  31.5 5.0 %branch_1_fun.6 = bf16[16,16,3328]{2,1,0:T(8,128)(2,1)S(1)} custom-call(bf16[256,2304]{1,0:T(8,128)(2,1)} %get-tuple-element.54.res_hbm.res_ref, bf16[500,2304]{1,0:T(8,128)(2,1)S(1)} %get-tuple-element.55.table_hbm.table_ref, bf16[16,16,896]{2,1,0:T(8,128)(2,1)S(1)} %get-tuple-element.56.slots_hbm, f32[1,2304]{1,0:T(1,128)S(1)} %reshape.47.gain_ref, ...), custom_call_target="tpu_custom_call" | custom-call | flops 1179648000 | bytes 2304000 | tf_op jit(solution)/shard_map/cond/branch_1_fun/pallas_call | solution.py:30
  36.5 29.8 %all_to_all.44.in_ref = bf16[16,16,3328]{2,1,0:T(8,128)(2,1)S(1)} all-to-all(bf16[16,16,3328]{2,1,0:T(8,128)(2,1)S(1)} %branch_1_fun.6), channel_id=1, replica_groups=mesh['z'=16,'core'=2,'tensor'=2,'dp'=8] {'tensor','dp'}, dimensions={0} | all-to-all | bytes 3407872 | tf_op jit(solution)/shard_map/cond/branch_1_fun/all_to_all | solution.py:25
  66.2 1.0 branch_1_fun.7
  67.3 38.8 %all_to_all.45.in_ref = bf16[32,2,1664]{2,1,0:T(2,128)(2,1)S(1)} all-to-all(bf16[32,2,1664]{2,1,0:T(2,128)(2,1)S(1)} %get-tuple-element.64), channel_id=1, replica_groups=mesh['z'=16,'core'=2,'tensor'=2,'dp'=8] {'z','core'}, dimensions={0} | all-to-all | bytes 425984 | tf_op jit(solution)/shard_map/cond/branch_1_fun/all_to_all | solution.py:25
  106.1 1.4 branch_1_fun.8
  107.5 3.5 %all-to-all-start.7 = ((f32[16,1,1152]{2,1,0:T(1,128)}), f32[16,1,1152]{2,1,0:T(1,128)S(1)}, u32[]{:S(2)}, u32[]{:S(2)}) async-start(f32[16,1,1152]{2,1,0:T(1,128)} %get-tuple-element.66), calls=%async_computation.7 | async-start | bytes 147456 | tf_op jit(solution)/shard_map/cond/branch_1_fun/all_to_all | solution.py:25
  111.0 6.7 %branch_1_fun.9 = bf16[500,2304]{1,0:T(8,128)(2,1)} custom-call(s32[1,256]{1,0:T(1,128)S(1)} %bitcast.20, f32[1,256]{1,0:T(1,128)S(1)} %get-tuple-element.67.totals_ref, s32[1,256]{1,0:T(1,128)S(1)} %bitcast.28, bf16[256,2304]{1,0:T(8,128)(2,1)} %get-tuple-element.54.res_hbm.res_ref, f32[1,2304]{1,0:T(1,128)S(1)} %reshape.47.gain_ref, ...), custom_call_target="tpu_custom_call" | custom-call | flops 1769472000 | bytes 4608000 | tf_op jit(solution)/shard_map/cond/branch_1_fun/pallas_call | solution.py:30
  117.7 4.9 %all-to-all-done.7.in_ref = f32[16,1,1152]{2,1,0:T(1,128)S(1)} async-done(((f32[16,1,1152]{2,1,0:T(1,128)}), f32[16,1,1152]{2,1,0:T(1,128)S(1)}, u32[]{:S(2)}, u32[]{:S(2)}) %all-to-all-start.7) | async-done | bytes 73760 | tf_op jit(solution)/shard_map/cond/branch_1_fun/all_to_all | solution.py:25
  122.6 0.8 branch_1_fun.11
  123.4 6.8 %all-to-all-start.8 = ((f32[32,1,1152]{2,1,0:T(1,128)}), f32[32,1,1152]{2,1,0:T(1,128)S(1)}, u32[]{:S(2)}, u32[]{:S(2)}) async-start(f32[32,1,1152]{2,1,0:T(1,128)} %branch_1_fun.11), calls=%async_computation.8 | async-start | bytes 294912 | tf_op jit(solution)/shard_map/cond/branch_1_fun/all_to_all | solution.py:25
  130.2 2.1 %collective-permute-start = (f32[16,1,1152]{2,1,0:T(1,128)S(1)}, f32[16,1,1152]{2,1,0:T(1,128)S(1)}, u32[]{:S(2)}, u32[]{:S(2)}) collective-permute-start(f32[16,1,1152]{2,1,0:T(1,128)S(1)} %all-to-all-done.7.in_ref), channel_id=1, source_target_pairs={{0,16},{16,0},{1,17},{17,1},{2,18},{18,2},{3,19},{19,3},{4,20},{20... | collective-permute-start | bytes 221192 | tf_op jit(solution)/shard_map/cond/branch_1_fun/ppermute | solution.py:635
  132.4 1.0 collective-permute-done.other_ref
  133.4 0.2 branch_1_fun.10
  133.6 4.3 %all-to-all-done.8 = f32[32,1,1152]{2,1,0:T(1,128)S(1)} async-done(((f32[32,1,1152]{2,1,0:T(1,128)}), f32[32,1,1152]{2,1,0:T(1,128)S(1)}, u32[]{:S(2)}, u32[]{:S(2)}) %all-to-all-start.8) | async-done | bytes 147488 | tf_op jit(solution)/shard_map/cond/branch_1_fun/all_to_all | solution.py:25
  138.2 0.6 copy-done.8
  (25 shorter events, 0.3 us)
Async XLA Ops:
  7.2 9.8 %copy-start.7 = (s32[256]{0:T(256)S(1)}, s32[256]{0:T(256)}, u32[]{:S(2)}) copy-start(s32[256]{0:T(256)} %param.13) | copy-start | bytes 3076
  7.2 10.0 %copy-start.6 = (s32[256]{0:T(256)S(1)}, s32[256]{0:T(256)}, u32[]{:S(2)}) copy-start(s32[256]{0:T(256)} %param.12) | copy-start | bytes 3076
  7.2 11.8 %copy-start.1 = (bf16[500,2304]{1,0:T(8,128)(2,1)S(1)}, bf16[500,2304]{1,0:T(8,128)(2,1)}, u32[]{:S(2)}) copy-start(bf16[500,2304]{1,0:T(8,128)(2,1)} %table_ref.1) | copy-start | bytes 6912004
  7.2 11.8 %copy-start.3 = (bf16[16,2304]{1,0:T(8,128)(2,1)S(1)}, bf16[16,2304]{1,0:T(8,128)(2,1)}, u32[]{:S(2)}) copy-start(bf16[16,2304]{1,0:T(8,128)(2,1)} %cotangent_ref.1) | copy-start | bytes 221188
  9.3 22.1 %all-to-all-start.9 = ((bf16[16,16,2304]{2,1,0:T(8,128)(2,1)}), bf16[16,16,2304]{2,1,0:T(8,128)(2,1)}, u32[]{:S(2)}, u32[]{:S(2)}) async-start(bf16[16,16,2304]{2,1,0:T(8,128)(2,1)} %broadcast_in_dim.2), calls=%async_computation.9 | async-start | bytes 2359296 | tf_op jit(solution)/shard_map/all_to_all | solution.py:25
  17.0 14.4 %copy-start.2 = (bf16[16,2304]{1,0:T(8,128)(2,1)S(1)}, bf16[16,2304]{1,0:T(8,128)(2,1)}, u32[]{:S(2)}) copy-start(bf16[16,2304]{1,0:T(8,128)(2,1)} %param.9) | copy-start | bytes 221188
  17.0 14.4 %copy-start.4 = (f32[2304]{0:T(1024)S(1)}, f32[2304]{0:T(1024)}, u32[]{:S(2)}) copy-start(f32[2304]{0:T(1024)} %param.10) | copy-start | bytes 27652
  17.0 14.4 %copy-start.5 = (s32[256]{0:T(256)S(1)}, s32[256]{0:T(256)}, u32[]{:S(2)}) copy-start(s32[256]{0:T(256)} %param.14) | copy-start | bytes 3076
  107.5 15.1 %all-to-all-start.7 = ((f32[16,1,1152]{2,1,0:T(1,128)}), f32[16,1,1152]{2,1,0:T(1,128)S(1)}, u32[]{:S(2)}, u32[]{:S(2)}) async-start(f32[16,1,1152]{2,1,0:T(1,128)} %get-tuple-element.66), calls=%async_computation.7 | async-start | bytes 147456 | tf_op jit(solution)/shard_map/cond/branch_1_fun/all_to_all | solution.py:25
  123.4 14.5 %all-to-all-start.8 = ((f32[32,1,1152]{2,1,0:T(1,128)}), f32[32,1,1152]{2,1,0:T(1,128)S(1)}, u32[]{:S(2)}, u32[]{:S(2)}) async-start(f32[32,1,1152]{2,1,0:T(1,128)} %branch_1_fun.11), calls=%async_computation.8 | async-start | bytes 294912 | tf_op jit(solution)/shard_map/cond/branch_1_fun/all_to_all | solution.py:25
  130.2 3.2 %collective-permute-start = (f32[16,1,1152]{2,1,0:T(1,128)S(1)}, f32[16,1,1152]{2,1,0:T(1,128)S(1)}, u32[]{:S(2)}, u32[]{:S(2)}) collective-permute-start(f32[16,1,1152]{2,1,0:T(1,128)S(1)} %all-to-all-done.7.in_ref), channel_id=1, source_target_pairs={{0,16},{16,0},{1,17},{17,1},{2,18},{18,2},{3,19},{19,3},{4,20},{20... | collective-permute-start | bytes 221192 | tf_op jit(solution)/shard_map/cond/branch_1_fun/ppermute | solution.py:635
  138.2 0.6 copy-start.8
  138.2 0.6 copy-start.9

commit v5 on v4

--- a/solution.py
+++ b/solution.py
@@ -50,13 +50,21 @@
         hidden_ref[rows, :] = (x * inverse * gain_ref[...]).astype(BF16)
         return carry
 
-    lax.fori_loop(0, tokens // step, norm, 0, unroll=4)
+    lax.fori_loop(0, tokens // step, norm, 0, unroll=16)
 
 
 def scores_of(table_ref, hidden_ref):
-    scores = lax.dot_general(
-        table_ref[...], hidden_ref[...], (((1,), (1,)), ((), ())), preferred_element_type=F32
-    )
+    vocab_rows, block = table_ref.shape[0], 256
+    scores = [
+        lax.dot_general(
+            table_ref[start : min(start + block, vocab_rows), :],
+            hidden_ref[...],
+            (((1,), (1,)), ((), ())),
+            preferred_element_type=F32,
+        )
+        for start in range(0, vocab_rows, block)
+    ]
+    scores = jnp.concatenate(scores, axis=0)
     return 30.0 * jnp.tanh(scores * (1.0 / 30.0))
 
 
@@ -177,15 +185,19 @@
         out_ref[:, columns] = (head + scale * inputs).astype(BF16)
 
 
-def plan_body(ids_ref, me_ref, rows_ref, codes_ref, most_ref):
+def plan_body(ids_ref, me_ref, rows_ref, codes_ref, pairs_ref):
     _, own, groups = ids_ref.shape
     section, place, vocab_rows = me_ref[0], me_ref[1], me_ref[2]
     device = section * groups + place
-    most = jnp.int32(0)
+    token = lax.broadcasted_iota(jnp.int32, (own, groups), 0)
+    group = lax.broadcasted_iota(jnp.int32, (own, groups), 1)
+
+    def column(x):
+        return jnp.sum(jnp.where(group == place, x, 0), axis=1, keepdims=True)
+
+    ahead_sent = ahead_here = jnp.zeros((1, groups), jnp.int32)
     for which in range(2):
         ids = ids_ref[which]
-        token = lax.broadcasted_iota(jnp.int32, ids.shape, 0)
-        group = lax.broadcasted_iota(jnp.int32, ids.shape, 1)
         owner = lax.div(ids, vocab_rows)
         again = jnp.zeros(ids.shape, jnp.int32)
         for j in range(own):
@@ -195,19 +207,31 @@
         for j in range(own):
             under = (owner == owner[j : j + 1]) & (ids[j : j + 1] < ids) & (first[j : j + 1] == 1)
             slot = slot + jnp.where(under, 1, 0)
-        most = jnp.maximum(most, jnp.max(slot))
+        near = column(owner) - section * groups
+        inside = (near >= 0) & (near < groups)
+        mine = (owner == device) & (first == 1)
+        if which == 0:
+            offset = jnp.zeros((own, 1), jnp.int32)
+            pair = owner * groups + group
+        else:
+            offset = jnp.sum(jnp.where(group == near, ahead_sent, 0), axis=1, keepdims=True)
+            slot_here = slot + ahead_here
+            over = lax.div(owner, groups) * groups
+            pair = (over + group) * groups + owner - over
+        pairs_ref[which] = jnp.where(first == 1, pair, -1)
+        code = jnp.where(inside, (column(slot) + offset) * groups + near, -1)
+        codes_ref[which] = jnp.broadcast_to(code, codes_ref.shape[1:])
         rows_ref[which] = jnp.full(rows_ref.shape[1:], -1, jnp.int32)
-        mine = (owner == device) & (first == 1)
         for k in range(SLOTS):
-            local = jnp.where(mine & (slot == k), ids - device * vocab_rows + 1, 0)
+            taken = mine & ((slot if which == 0 else slot_here) == k)
+            local = jnp.where(taken, ids - device * vocab_rows + 1, 0)
             rows_ref[which, :, k * groups : (k + 1) * groups] = (
                 jnp.sum(local, axis=0, keepdims=True) - 1
             )
-        near = owner - section * groups
-        code = jnp.where((near >= 0) & (near < groups), slot * groups + near, -1)
-        code = jnp.sum(jnp.where(group == place, code, 0), axis=1, keepdims=True)
-        codes_ref[which] = jnp.broadcast_to(code, codes_ref.shape[1:])
-    most_ref[0] = most
+        if which == 0:
+            ahead_sent = jnp.sum(jnp.where(mine, 1, 0), axis=0, keepdims=True)
+            come = (group == near) & (column(first) == 1)
+            ahead_here = jnp.sum(jnp.where(come, 1, 0), axis=0, keepdims=True)
 
 
 def three_terms(x):
@@ -220,7 +244,7 @@
     n_lanes = width // LANES
     token_tiles = -(-tokens // LANES)
     scalar_tiles = -(-6 * token_tiles // own)
-    slot_tiles = -(-2 * SLOTS * n_lanes // own)
+    slot_tiles = -(-SLOTS * n_lanes // own)
     return n_lanes, token_tiles, scalar_tiles, slot_tiles
 
 
@@ -233,7 +257,7 @@
     def put(at, value):
         room_ref[pl.ds(at, n_plane, stride=stride), :] = value
 
-    for at in range(2 * SLOTS * n_lanes, stride):
+    for at in range(SLOTS * n_lanes, stride):
         put(at, jnp.zeros((n_plane, LANES), F32))
     n_slots = SLOTS * n_plane
     slot_iota = lax.broadcasted_iota(jnp.int32, (vocab_rows, n_slots), 0)
@@ -244,16 +268,14 @@
     tile = 2 * LANES
     for n in range(width // tile):
         columns = slice(n * tile, (n + 1) * tile)
-        moved = (
-            lax.dot_general(pick, table_ref[:, columns], dims, preferred_element_type=F32),
-            lax.dot_general(give, cotangent_ref[:, columns], dims, preferred_element_type=F32),
+        moved = lax.dot_general(pick, table_ref[:, columns], dims, preferred_element_type=F32)
+        moved = moved + lax.dot_general(
+            give, cotangent_ref[:, columns], dims, preferred_element_type=F32
         )
-        for which in range(2):
-            for k in range(SLOTS):
-                block = moved[which][k * n_plane : (k + 1) * n_plane]
-                for half in range(2):
-                    at = (which * SLOTS + k) * n_lanes + 2 * n + half
-                    put(at, block[:, half * LANES : (half + 1) * LANES])
+        for k in range(SLOTS):
+            block = moved[k * n_plane : (k + 1) * n_plane]
+            for half in range(2):
+                put(k * n_lanes + 2 * n + half, block[:, half * LANES : (half + 1) * LANES])
     for p in range(n_plane):
         for t in range(tiles):
             start = p * stride + t * own
@@ -338,17 +360,17 @@
     def take(at):
         return room_ref[pl.ds(at, n_plane, stride=stride), :]
 
-    for which in range(2):
-        for k in range(SLOTS):
-            for j in range(n_lanes):
-                moved_ref[
-                    which, k * n_plane : (k + 1) * n_plane, j * LANES : (j + 1) * LANES
-                ] = take(scalar_tiles * own + (which * SLOTS + k) * n_lanes + j)
-    rows_out_ref[...] = moved_ref[1].astype(BF16)
+    for k in range(SLOTS):
+        for j in range(n_lanes):
+            moved_ref[k * n_plane : (k + 1) * n_plane, j * LANES : (j + 1) * LANES] = take(
+                scalar_tiles * own + k * n_lanes + j
+            )
+    moved = moved_ref[...].astype(BF16)
+    rows_out_ref[...] = moved
     n_slots = SLOTS * n_plane
     own_iota = lax.broadcasted_iota(jnp.int32, (own, n_slots), 1)
     choose = (codes_ref[0, :, :n_slots] == own_iota).astype(F32).astype(BF16)
-    target_rows = jnp.dot(choose, moved_ref[0].astype(BF16), preferred_element_type=F32)
+    target_rows = jnp.dot(choose, moved, preferred_element_type=F32)
     for h in range(halves):
         for i in range(own):
             s = i * halves + h
@@ -608,7 +630,7 @@
         in_specs=[VMEM, SMEM, VMEM],
         scratch=[
             pltpu.VMEM((n_plane * tiles * own, LANES), F32),
-            pltpu.VMEM((2, SLOTS * n_plane, width), F32),
+            pltpu.VMEM((SLOTS * n_plane, width), F32),
             pltpu.VMEM((2 * n_section, piece_width), F32),
         ],
     )
@@ -663,19 +685,21 @@
     lanes = -(-SLOTS * n_plane // LANES) * LANES
     everyone = exchange(jnp.broadcast_to(residual[None], (n_plane, own, width)), PLANE)
     everyone = everyone.reshape(n_plane * own, width)
-    slot_rows, codes, most = call(
+    slot_rows, codes, pairs = call(
         plan_body,
         (
             shape((2, 1, lanes), jnp.int32),
             shape((2, own, lanes), jnp.int32),
-            shape((1,), jnp.int32),
+            shape((2, own, n_plane), jnp.int32),
         ),
         1000,
         1000,
         ids, me,
         in_specs=[VMEM, SMEM],
-        out_specs=(VMEM, VMEM, SMEM),
-    )
+    )
+    pairs = pairs.reshape(-1)
+    alike = (pairs[:, None] == pairs[None, :]) & (pairs[:, None] >= 0)
+    fits = jnp.max(jnp.sum(alike.astype(jnp.int32), axis=1)) <= SLOTS
     slot_tiles = slot_layout(own, width, own * n_plane)[3]
     slots = call(
         slots_body,
@@ -686,7 +710,7 @@
         scratch=[pltpu.VMEM((n_plane * slot_tiles * own, LANES), F32)],
     )
     return lax.cond(
-        most[0] < SLOTS,
+        fits,
         compact,
         general,
         everyone, (slot_rows, codes, slots, me), residual, final_gain, table, targets, input_ids, loss_mask,

time: 146 us -> 142 us (0.973)
  Pallas kernels: 17.4 us -> 13.6 us
  blocking collectives: 68.6 us -> 66.3 us
    pallas_call x8, Pallas kernels: 17.4 us -> 13.6 us  [call(): pl.pallas_call(body, out_shape=outs, in_specs=in_specs or [VMEM] * len(op...]
    all_to_all x2, blocking collectives: 68.6 us -> 66.3 us  [exchange(): return lax.all_to_all(pieces, axes, 0, 0, tiled=True)]
  transfers between devices with their start and end apart: 4 -> 4, of which waited for: 4 -> 4; matrix products, arithmetic and copies ran while one was open for 0% -> 1% of each run, Pallas kernels for 6% -> 5%
where the time goes in v5:
time: 142 us
  blocking collectives  66.3 us (47%)
  waiting for transfers between devices  22.2 us (16%)
  starting transfers between devices  20.4 us (14%)
  between operations  14.8 us (10%)
  Pallas kernels  13.6 us (10%)
  local copies, waits for them, and re-layouts  3.05 us (2%)
    all_to_all x2, blocking collectives, exchange(): return lax.all_to_all(pieces, axes, 0, 0, tiled=True)  66.3 us
    all_to_all x3, waiting for transfers between devices, exchange(): return lax.all_to_all(pieces, axes, 0, 0, tiled=True)  21.2 us
    all_to_all x3, starting transfers between devices, exchange(): return lax.all_to_all(pieces, axes, 0, 0, tiled=True)  18.3 us
    pallas_call x8, Pallas kernels, call(): pl.pallas_call(body, out_shape=outs, in_specs=in_specs or [VMEM] * len(op...  13.6 us
  transfers between devices with their start and end apart: 4, of which 4 were waited for; matrix products, arithmetic and copies ran while one was open for 1% of the time, Pallas kernels for 5%

profile of v5, /device:TPU:1, one launch (start us, length us, event | category | flops | bytes accessed | tf_op | source)
XLA Modules:
  0.0 141.7 jit_solution(13887768875291540264)
XLA Ops:
  7.2 2.0 %broadcast_in_dim.2 = bf16[16,16,2304]{2,1,0:T(8,128)(2,1)} broadcast(bf16[16,2304]{1,0:T(8,128)(2,1)} %param.9), dimensions={1,2} | broadcast | bytes 1253376 | tf_op jit(solution)/shard_map/broadcast_in_dim | solution.py:686
  9.2 7.8 %all-to-all-start.9 = ((bf16[16,16,2304]{2,1,0:T(8,128)(2,1)}), bf16[16,16,2304]{2,1,0:T(8,128)(2,1)}, u32[]{:S(2)}, u32[]{:S(2)}) async-start(bf16[16,16,2304]{2,1,0:T(8,128)(2,1)} %broadcast_in_dim.2), calls=%async_computation.9 | async-start | bytes 2359296 | tf_op jit(solution)/shard_map/all_to_all | solution.py:25
  17.3 0.1 pad_add_fusion.1.me_ref
  17.4 1.0 shard_map.96
  18.4 0.8 shard_map.97
  19.2 0.3 convert_reduce_fusion
  19.5 0.6 reduce_max.9
  20.8 10.6 %all-to-all-done.9 = bf16[16,16,2304]{2,1,0:T(8,128)(2,1)} async-done(((bf16[16,16,2304]{2,1,0:T(8,128)(2,1)}), bf16[16,16,2304]{2,1,0:T(8,128)(2,1)}, u32[]{:S(2)}, u32[]{:S(2)}) %all-to-all-start.9) | async-done | bytes 1179680 | tf_op jit(solution)/shard_map/all_to_all | solution.py:25
  31.4 102.8 %conditional.1 = (bf16[16,2304]{1,0:T(8,128)(2,1)S(1)}, bf16[500,2304]{1,0:T(8,128)(2,1)}, f32[2304]{0:T(1024)S(1)}) conditional(s32[]{:T(128)} %convert_element_type.9, (f32[2304]{0:T(1024)S(1)}, bf16[256,2304]{1,0:T(8,128)(2,1)}, bf16[500,2304]{1,0:T(8,128)(2,1)S(1)}, s32[256]{0:T(256)S(1)}, s32[256]{0:T(256)S(1)}, /*index=5*/s32[256]{0:T(256)S(1)}, ...), branch_computations={%region_2.3_spmd, %region_3.5_spmd} | conditional | flops 3539939584 | bytes 25218406 | solution.py:712
  31.5 3.6 %branch_1_fun.6 = bf16[16,16,2944]{2,1,0:T(8,128)(2,1)S(1)} custom-call(bf16[256,2304]{1,0:T(8,128)(2,1)} %get-tuple-element.54.res_hbm.res_ref, bf16[500,2304]{1,0:T(8,128)(2,1)S(1)} %get-tuple-element.55.table_hbm.table_ref, bf16[16,16,512]{2,1,0:T(8,128)(2,1)S(1)} %get-tuple-element.56.slots_hbm, f32[1,2304]{1,0:T(1,128)S(1)} %reshape.52.gain_ref, ...), custom_call_target="tpu_custom_call" | custom-call | flops 1179648000 | bytes 2304000 | tf_op jit(solution)/shard_map/cond/branch_1_fun/pallas_call | solution.py:30
  35.0 28.0 %all_to_all.44.in_ref = bf16[16,16,2944]{2,1,0:T(8,128)(2,1)S(1)} all-to-all(bf16[16,16,2944]{2,1,0:T(8,128)(2,1)S(1)} %branch_1_fun.6), channel_id=1, replica_groups=mesh['z'=16,'core'=2,'tensor'=2,'dp'=8] {'tensor','dp'}, dimensions={0} | all-to-all | bytes 3014656 | tf_op jit(solution)/shard_map/cond/branch_1_fun/all_to_all | solution.py:25
  63.0 0.6 branch_1_fun.7
  63.6 38.3 %all_to_all.45.in_ref = bf16[32,2,1664]{2,1,0:T(2,128)(2,1)S(1)} all-to-all(bf16[32,2,1664]{2,1,0:T(2,128)(2,1)S(1)} %get-tuple-element.64), channel_id=1, replica_groups=mesh['z'=16,'core'=2,'tensor'=2,'dp'=8] {'z','core'}, dimensions={0} | all-to-all | bytes 425984 | tf_op jit(solution)/shard_map/cond/branch_1_fun/all_to_all | solution.py:25
  101.9 1.4 branch_1_fun.8
  103.3 3.5 %all-to-all-start.7 = ((f32[16,1,1152]{2,1,0:T(1,128)}), f32[16,1,1152]{2,1,0:T(1,128)S(1)}, u32[]{:S(2)}, u32[]{:S(2)}) async-start(f32[16,1,1152]{2,1,0:T(1,128)} %get-tuple-element.66), calls=%async_computation.7 | async-start | bytes 147456 | tf_op jit(solution)/shard_map/cond/branch_1_fun/all_to_all | solution.py:25
  106.8 5.3 %branch_1_fun.9 = bf16[500,2304]{1,0:T(8,128)(2,1)} custom-call(s32[1,256]{1,0:T(1,128)S(1)} %bitcast.19, f32[1,256]{1,0:T(1,128)S(1)} %get-tuple-element.67.totals_ref, s32[1,256]{1,0:T(1,128)S(1)} %bitcast.27, bf16[256,2304]{1,0:T(8,128)(2,1)} %get-tuple-element.54.res_hbm.res_ref, f32[1,2304]{1,0:T(1,128)S(1)} %reshape.52.gain_ref, ...), custom_call_target="tpu_custom_call" | custom-call | flops 1769472000 | bytes 4608000 | tf_op jit(solution)/shard_map/cond/branch_1_fun/pallas_call | solution.py:30
  112.1 6.3 %all-to-all-done.7.in_ref = f32[16,1,1152]{2,1,0:T(1,128)S(1)} async-done(((f32[16,1,1152]{2,1,0:T(1,128)}), f32[16,1,1152]{2,1,0:T(1,128)S(1)}, u32[]{:S(2)}, u32[]{:S(2)}) %all-to-all-start.7) | async-done | bytes 73760 | tf_op jit(solution)/shard_map/cond/branch_1_fun/all_to_all | solution.py:25
  118.4 0.8 branch_1_fun.11
  119.2 7.0 %all-to-all-start.8 = ((f32[32,1,1152]{2,1,0:T(1,128)}), f32[32,1,1152]{2,1,0:T(1,128)S(1)}, u32[]{:S(2)}, u32[]{:S(2)}) async-start(f32[32,1,1152]{2,1,0:T(1,128)} %branch_1_fun.11), calls=%async_computation.8 | async-start | bytes 294912 | tf_op jit(solution)/shard_map/cond/branch_1_fun/all_to_all | solution.py:25
  126.2 2.1 %collective-permute-start = (f32[16,1,1152]{2,1,0:T(1,128)S(1)}, f32[16,1,1152]{2,1,0:T(1,128)S(1)}, u32[]{:S(2)}, u32[]{:S(2)}) collective-permute-start(f32[16,1,1152]{2,1,0:T(1,128)S(1)} %all-to-all-done.7.in_ref), channel_id=1, source_target_pairs={{0,16},{16,0},{1,17},{17,1},{2,18},{18,2},{3,19},{19,3},{4,20},{20... | collective-permute-start | bytes 221192 | tf_op jit(solution)/shard_map/cond/branch_1_fun/ppermute | solution.py:657
  128.4 1.0 collective-permute-done.other_ref
  129.4 0.2 branch_1_fun.10
  129.6 4.3 %all-to-all-done.8 = f32[32,1,1152]{2,1,0:T(1,128)S(1)} async-done(((f32[32,1,1152]{2,1,0:T(1,128)}), f32[32,1,1152]{2,1,0:T(1,128)S(1)}, u32[]{:S(2)}, u32[]{:S(2)}) %all-to-all-start.8) | async-done | bytes 147488 | tf_op jit(solution)/shard_map/cond/branch_1_fun/all_to_all | solution.py:25
  134.2 0.6 copy-done.8
  (29 shorter events, 0.5 us)
Async XLA Ops:
  7.2 9.8 %copy-start.7 = (s32[256]{0:T(256)S(1)}, s32[256]{0:T(256)}, u32[]{:S(2)}) copy-start(s32[256]{0:T(256)} %param.13) | copy-start | bytes 3076
  7.2 10.0 %copy-start.6 = (s32[256]{0:T(256)S(1)}, s32[256]{0:T(256)}, u32[]{:S(2)}) copy-start(s32[256]{0:T(256)} %param.12) | copy-start | bytes 3076
  9.2 9.2 %copy-start.1 = (bf16[500,2304]{1,0:T(8,128)(2,1)S(1)}, bf16[500,2304]{1,0:T(8,128)(2,1)}, u32[]{:S(2)}) copy-start(bf16[500,2304]{1,0:T(8,128)(2,1)} %table_ref.1) | copy-start | bytes 6912004
  9.2 9.2 %copy-start.3 = (bf16[16,2304]{1,0:T(8,128)(2,1)S(1)}, bf16[16,2304]{1,0:T(8,128)(2,1)}, u32[]{:S(2)}) copy-start(bf16[16,2304]{1,0:T(8,128)(2,1)} %cotangent_ref.1) | copy-start | bytes 221188
  9.2 22.2 %all-to-all-start.9 = ((bf16[16,16,2304]{2,1,0:T(8,128)(2,1)}), bf16[16,16,2304]{2,1,0:T(8,128)(2,1)}, u32[]{:S(2)}, u32[]{:S(2)}) async-start(bf16[16,16,2304]{2,1,0:T(8,128)(2,1)} %broadcast_in_dim.2), calls=%async_computation.9 | async-start | bytes 2359296 | tf_op jit(solution)/shard_map/all_to_all | solution.py:25
  16.9 14.4 %copy-start.2 = (bf16[16,2304]{1,0:T(8,128)(2,1)S(1)}, bf16[16,2304]{1,0:T(8,128)(2,1)}, u32[]{:S(2)}) copy-start(bf16[16,2304]{1,0:T(8,128)(2,1)} %param.9) | copy-start | bytes 221188
  17.0 14.4 %copy-start.4 = (f32[2304]{0:T(1024)S(1)}, f32[2304]{0:T(1024)}, u32[]{:S(2)}) copy-start(f32[2304]{0:T(1024)} %param.10) | copy-start | bytes 27652
  17.0 14.4 %copy-start.5 = (s32[256]{0:T(256)S(1)}, s32[256]{0:T(256)}, u32[]{:S(2)}) copy-start(s32[256]{0:T(256)} %param.14) | copy-start | bytes 3076
  103.3 15.1 %all-to-all-start.7 = ((f32[16,1,1152]{2,1,0:T(1,128)}), f32[16,1,1152]{2,1,0:T(1,128)S(1)}, u32[]{:S(2)}, u32[]{:S(2)}) async-start(f32[16,1,1152]{2,1,0:T(1,128)} %get-tuple-element.66), calls=%async_computation.7 | async-start | bytes 147456 | tf_op jit(solution)/shard_map/cond/branch_1_fun/all_to_all | solution.py:25
  119.2 14.7 %all-to-all-start.8 = ((f32[32,1,1152]{2,1,0:T(1,128)}), f32[32,1,1152]{2,1,0:T(1,128)S(1)}, u32[]{:S(2)}, u32[]{:S(2)}) async-start(f32[32,1,1152]{2,1,0:T(1,128)} %branch_1_fun.11), calls=%async_computation.8 | async-start | bytes 294912 | tf_op jit(solution)/shard_map/cond/branch_1_fun/all_to_all | solution.py:25
  126.2 3.2 %collective-permute-start = (f32[16,1,1152]{2,1,0:T(1,128)S(1)}, f32[16,1,1152]{2,1,0:T(1,128)S(1)}, u32[]{:S(2)}, u32[]{:S(2)}) collective-permute-start(f32[16,1,1152]{2,1,0:T(1,128)S(1)} %all-to-all-done.7.in_ref), channel_id=1, source_target_pairs={{0,16},{16,0},{1,17},{17,1},{2,18},{18,2},{3,19},{19,3},{4,20},{20... | collective-permute-start | bytes 221192 | tf_op jit(solution)/shard_map/cond/branch_1_fun/ppermute | solution.py:657
  134.2 0.6 copy-start.8
  134.2 0.6 copy-start.9

commit v6 on v5

--- a/solution.py
+++ b/solution.py
@@ -1,3 +1,4 @@
+import functools
 import math
 
 import jax
@@ -84,9 +85,10 @@
     return (mask_ref[...].astype(F32) * (share - hit) * (1.0 - bend * bend)).astype(BF16)
 
 
-def sums_body(res_ref, gain_ref, table_ref, sums_ref, hidden_ref, inverse_ref):
+def sums_body(vocab_rows, res_ref, gain_ref, table_ref, sums_ref, hidden_ref, inverse_ref):
     capped = capped_scores(res_ref, gain_ref, table_ref, hidden_ref, inverse_ref)
-    sums = jnp.sum(jnp.exp(capped), axis=0, keepdims=True)
+    rows = lax.broadcasted_iota(jnp.int32, capped.shape, 0)
+    sums = jnp.sum(jnp.where(rows < vocab_rows, jnp.exp(capped), 0.0), axis=0, keepdims=True)
     for i in range(sums_ref.shape[0]):
         sums_ref[i] = sums
 
@@ -182,7 +184,7 @@
         columns = slice(n * tile, (n + 1) * tile)
         head = jnp.dot(dlogits, hidden_ref[:, columns], preferred_element_type=F32)
         inputs = jnp.dot(onehot, cotangent_ref[:, columns], preferred_element_type=F32)
-        out_ref[:, columns] = (head + scale * inputs).astype(BF16)
+        out_ref[:, columns] = (head + scale * inputs)[:vocab_rows].astype(BF16)
 
 
 def plan_body(ids_ref, me_ref, rows_ref, codes_ref, pairs_ref):
@@ -248,7 +250,9 @@
     return n_lanes, token_tiles, scalar_tiles, slot_tiles
 
 
-def slots_body(table_ref, slot_rows_ref, codes_ref, cotangent_ref, out_ref, room_ref):
+def slots_body(
+    table_ref, slot_rows_ref, codes_ref, cotangent_ref, out_ref, tail_ref, room_ref
+):
     n_plane, own, _ = out_ref.shape
     vocab_rows, width = table_ref.shape
     n_lanes, _, _, tiles = slot_layout(own, width, own * n_plane)
@@ -262,13 +266,22 @@
     n_slots = SLOTS * n_plane
     slot_iota = lax.broadcasted_iota(jnp.int32, (vocab_rows, n_slots), 0)
     pick = (slot_rows_ref[0, :, :n_slots] == slot_iota).astype(F32).astype(BF16)
+    last = tail_ref.shape[0]
+    last_start = (vocab_rows - 1) // last * last
+    last_rows = lax.broadcasted_iota(jnp.int32, (vocab_rows, last), 0) - last_start
+    pick_last = last_rows == lax.broadcasted_iota(jnp.int32, (vocab_rows, last), 1)
+    pick_last = pick_last.astype(F32).astype(BF16)
     own_iota = lax.broadcasted_iota(jnp.int32, (own, n_slots), 1)
     give = (codes_ref[1, :, :n_slots] == own_iota).astype(F32).astype(BF16)
     dims = (((0,), (0,)), ((), ()))
     tile = 2 * LANES
     for n in range(width // tile):
         columns = slice(n * tile, (n + 1) * tile)
-        moved = lax.dot_general(pick, table_ref[:, columns], dims, preferred_element_type=F32)
+        rows = table_ref[:, columns]
+        tail_ref[:, columns] = lax.dot_general(
+            pick_last, rows, dims, preferred_element_type=F32
+        ).astype(BF16)
+        moved = lax.dot_general(pick, rows, dims, preferred_element_type=F32)
         moved = moved + lax.dot_general(
             give, cotangent_ref[:, columns], dims, preferred_element_type=F32
         )
@@ -284,13 +297,18 @@
             )
 
 
+def whole_rows(table_hbm, table_ref, sem):
+    rows = table_ref.shape[0] - 16
+    return pltpu.make_async_copy(table_hbm.at[:rows, :], table_ref.at[:rows, :], sem)
+
+
 def compact_body(
-    res_hbm, table_hbm, slots_hbm, gain_ref, target_row_ref, mask_ref,
+    vocab_rows, me_ref, res_hbm, table_hbm, slots_hbm, tail_ref, gain_ref, targets_ref, mask_ref,
     packed_ref, res_ref, table_ref, slots_ref, hidden_ref, inverse_ref, tokens_ref, room_ref, sems,
 ):
     copies = [
         pltpu.make_async_copy(res_hbm, res_ref, sems.at[0]),
-        pltpu.make_async_copy(table_hbm, table_ref, sems.at[1]),
+        whole_rows(table_hbm, table_ref, sems.at[1]),
         pltpu.make_async_copy(slots_hbm, slots_ref, sems.at[2]),
     ]
     for copy in copies:
@@ -301,10 +319,12 @@
     copies[0].wait()
     norm_rows(res_ref, gain_ref, hidden_ref, inverse_ref)
     copies[1].wait()
+    table_ref[table_ref.shape[0] - tail_ref.shape[0] :, :] = tail_ref[...]
     capped = scores_of(table_ref, hidden_ref)
     rows = lax.broadcasted_iota(jnp.int32, capped.shape, 0)
-    hit = target_row_ref[...] == rows
-    expterm = jnp.exp(capped)
+    device = me_ref[0] * n_plane + me_ref[1]
+    hit = targets_ref[...] - device * vocab_rows == rows
+    expterm = jnp.where(rows < vocab_rows, jnp.exp(capped), 0.0)
     bend = capped * (1.0 / 30.0)
     weight = mask_ref[...].astype(F32) * (1.0 - bend * bend)
     unscaled = jnp.where(hit, 0.0, weight * expterm).astype(BF16)
@@ -474,18 +494,24 @@
 
 
 def compact_table_body(
-    target_row_ref, totals_ref, mask_ref, res_ref, gain_ref, table_ref, slot_rows_ref, moved_ref,
-    out_ref, hidden_ref, inverse_ref,
+    me_ref, table_hbm, tail_ref, targets_ref, totals_ref, mask_ref, res_ref, gain_ref, slot_rows_ref,
+    moved_ref, out_ref, table_ref, hidden_ref, inverse_ref, sem,
 ):
     vocab_rows, width = out_ref.shape
-    capped = capped_scores(res_ref, gain_ref, table_ref, hidden_ref, inverse_ref)
+    copy = whole_rows(table_hbm, table_ref, sem)
+    copy.start()
+    norm_rows(res_ref, gain_ref, hidden_ref, inverse_ref)
+    copy.wait()
+    table_ref[table_ref.shape[0] - tail_ref.shape[0] :, :] = tail_ref[...]
+    capped = scores_of(table_ref, hidden_ref)
     rows = lax.broadcasted_iota(jnp.int32, capped.shape, 0)
-    hit = (target_row_ref[...] == rows).astype(F32)
+    device = me_ref[0] * (moved_ref.shape[0] // SLOTS) + me_ref[1]
+    hit = (targets_ref[...] - device * vocab_rows == rows).astype(F32)
     share = jnp.exp(capped) * (1.0 / totals_ref[...])
     bend = capped * (1.0 / 30.0)
     dlogits = (mask_ref[...].astype(F32) * (share - hit) * (1.0 - bend * bend)).astype(BF16)
     n_slots = moved_ref.shape[0]
-    slot_iota = lax.broadcasted_iota(jnp.int32, (vocab_rows, n_slots), 0)
+    slot_iota = lax.broadcasted_iota(jnp.int32, (capped.shape[0], n_slots), 0)
     onehot = (slot_rows_ref[1, :, :n_slots] == slot_iota).astype(F32).astype(BF16)
     scale = math.sqrt(width)
     tile = 2 * LANES
@@ -493,13 +519,14 @@
         columns = slice(n * tile, (n + 1) * tile)
         head = jnp.dot(dlogits, hidden_ref[:, columns], preferred_element_type=F32)
         inputs = jnp.dot(onehot, moved_ref[:, columns], preferred_element_type=F32)
-        out_ref[:, columns] = (head + scale * inputs).astype(BF16)
+        out_ref[:, columns] = (head + scale * inputs)[:vocab_rows].astype(BF16)
 
 
 def general(
     everyone, plan, residual, final_gain, table, targets, input_ids, loss_mask, embed_cotangent
 ):
     del plan
+    padded = jnp.pad(table, ((0, -table.shape[0] % 16), (0, 0)))
     own, width = residual.shape
     vocab_rows = table.shape[0]
     n_plane, n_section = lax.axis_size(PLANE), lax.axis_size(SECTION)
@@ -520,11 +547,11 @@
     all_cotangent = lax.all_gather(wide, PLANE, axis=0, tiled=True)
 
     sums = call(
-        sums_body,
+        functools.partial(sums_body, vocab_rows),
         shape((n_section, 1, tokens), F32),
         product,
         rows_bytes,
-        everyone, gain_row, table,
+        everyone, gain_row, padded,
         scratch=norm_rooms,
     )
     sums = call(
@@ -532,7 +559,7 @@
     )
     given = (
         first, exchange(sums, PLANE), targets.reshape(1, tokens), loss_mask.reshape(1, tokens),
-        everyone, gain_row, table,
+        everyone, gain_row, padded,
     )
     packed = call(
         partial_body,
@@ -583,7 +610,7 @@
     everyone, plan, residual, final_gain, table, targets, input_ids, loss_mask, embed_cotangent
 ):
     del input_ids, embed_cotangent
-    slot_rows, codes, slots, me = plan
+    slot_rows, codes, slots, me, tail = plan
     own, width = residual.shape
     vocab_rows = table.shape[0]
     n_plane, n_section = lax.axis_size(PLANE), lax.axis_size(SECTION)
@@ -599,18 +626,19 @@
     norm_rooms = [pltpu.VMEM((tokens, width), BF16), pltpu.VMEM((tokens, LANES), F32)]
     gain_row = final_gain.reshape(1, width)
     mask = loss_mask.reshape(1, tokens)
-    target_row = targets.reshape(1, tokens) - (me[0] * n_plane + me[1]) * vocab_rows
-
+    targets = targets.reshape(1, tokens)
+
+    table_room = pltpu.VMEM((-(-vocab_rows // 16) * 16, width), BF16)
     packed = call(
-        compact_body,
+        functools.partial(compact_body, vocab_rows),
         shape((n_plane, own, packed_width), BF16),
         2 * product,
         rows_bytes,
-        everyone, table, slots, gain_row, target_row, mask,
-        in_specs=[ANY] * 3 + [VMEM] * 3,
+        me, everyone, table, slots, tail, gain_row, targets, mask,
+        in_specs=[SMEM] + [ANY] * 3 + [VMEM] * 4,
         scratch=[
             pltpu.VMEM((tokens, width), BF16),
-            pltpu.VMEM((vocab_rows, width), BF16),
+            table_room,
             pltpu.VMEM((n_plane, own, slot_tiles * LANES), BF16),
         ] + norm_rooms + [
             pltpu.VMEM((1, token_tiles * LANES), F32),
@@ -648,8 +676,9 @@
         shape((vocab_rows, width), BF16),
         3 * product,
         2 * rows_bytes,
-        target_row, totals, mask, everyone, gain_row, table, slot_rows, moved,
-        scratch=norm_rooms,
+        me, table, tail, targets, totals, mask, everyone, gain_row, slot_rows, moved,
+        in_specs=[SMEM, ANY] + [VMEM] * 8,
+        scratch=[table_room] + norm_rooms + [pltpu.SemaphoreType.DMA],
     )
     mine, grad_table = lax.optimization_barrier((exchange(half_token, "z"), grad_table))
     core = lax.axis_index("core").astype(jnp.int32).reshape(1)
@@ -701,9 +730,9 @@
     alike = (pairs[:, None] == pairs[None, :]) & (pairs[:, None] >= 0)
     fits = jnp.max(jnp.sum(alike.astype(jnp.int32), axis=1)) <= SLOTS
     slot_tiles = slot_layout(own, width, own * n_plane)[3]
-    slots = call(
+    slots, tail = call(
         slots_body,
-        shape((n_plane, own, slot_tiles * LANES), BF16),
+        (shape((n_plane, own, slot_tiles * LANES), BF16), shape((16, width), BF16)),
         1000,
         1000,
         table, slot_rows, codes, embed_cotangent,
@@ -713,7 +742,7 @@
         fits,
         compact,
         general,
-        everyone, (slot_rows, codes, slots, me), residual, final_gain, table, targets, input_ids, loss_mask,
+        everyone, (slot_rows, codes, slots, me, tail), residual, final_gain, table, targets, input_ids, loss_mask,
         embed_cotangent,
     )
 

time: 142 us -> 143 us (level)
  waiting for transfers between devices: 22.2 us -> 18.6 us
  Pallas kernels: 13.6 us -> 16.8 us
    all_to_all x3, waiting for transfers between devices: 21.2 us -> 17.6 us  [exchange(): return lax.all_to_all(pieces, axes, 0, 0, tiled=True)]
    pallas_call x8, Pallas kernels: 13.6 us -> 16.8 us  [call(): pl.pallas_call(body, out_shape=outs, in_specs=in_specs or [VMEM] * len(op...]
  transfers between devices with their start and end apart: 4 -> 4, of which waited for: 4 -> 4; matrix products, arithmetic and copies ran while one was open for 1% -> 1% of each run, Pallas kernels for 5% -> 7%
where the time goes in v6:
time: 143 us; the launch traced here: 142 us
  blocking collectives  66.2 us (46%)
  starting transfers between devices  20.4 us (14%)
  waiting for transfers between devices  18.6 us (13%)
  Pallas kernels  16.8 us (12%)
  between operations  14.7 us (10%)
  local copies, waits for them, and re-layouts  3.67 us (3%)
    all_to_all x2, blocking collectives, exchange(): return lax.all_to_all(pieces, axes, 0, 0, tiled=True)  66.2 us
    all_to_all x3, starting transfers between devices, exchange(): return lax.all_to_all(pieces, axes, 0, 0, tiled=True)  18.2 us
    all_to_all x3, waiting for transfers between devices, exchange(): return lax.all_to_all(pieces, axes, 0, 0, tiled=True)  17.6 us
    pallas_call x8, Pallas kernels, call(): pl.pallas_call(body, out_shape=outs, in_specs=in_specs or [VMEM] * len(op...  16.8 us
  transfers between devices with their start and end apart: 4, of which 4 were waited for; matrix products, arithmetic and copies ran while one was open for 1% of the time, Pallas kernels for 7%

profile of v6, /device:TPU:1, one launch (start us, length us, event | category | flops | bytes accessed | tf_op | source)
XLA Modules:
  0.0 141.9 jit_solution(16149182987703143123)
XLA Ops:
  7.2 2.0 %broadcast_in_dim.2 = bf16[16,16,2304]{2,1,0:T(8,128)(2,1)} broadcast(bf16[16,2304]{1,0:T(8,128)(2,1)} %param.9), dimensions={1,2} | broadcast | bytes 1253376 | tf_op jit(solution)/shard_map/broadcast_in_dim | solution.py:715
  9.2 7.7 %all-to-all-start.9 = ((bf16[16,16,2304]{2,1,0:T(8,128)(2,1)}), bf16[16,16,2304]{2,1,0:T(8,128)(2,1)S(1)}, u32[]{:S(2)}, u32[]{:S(2)}) async-start(bf16[16,16,2304]{2,1,0:T(8,128)(2,1)} %broadcast_in_dim.2), calls=%async_computation.9 | async-start | bytes 2359296 | tf_op jit(solution)/shard_map/all_to_all | solution.py:26
  17.3 1.0 shard_map.96
  18.3 0.6 copy-done.7
  18.9 2.7 %shard_map.97 = (bf16[16,16,512]{2,1,0:T(8,128)(2,1)}, bf16[16,2304]{1,0:T(8,128)(2,1)}) custom-call(bf16[500,2304]{1,0:T(8,128)(2,1)S(1)} %copy-done.2, s32[2,1,128]{2,1,0:T(1,128)S(1)} %get-tuple-element.79.slot_rows_ref, s32[2,16,128]{2,1,0:T(8,128)S(1)} %get-tuple-element.80.codes_ref, bf16[16,2304]{1,0:T(8,128)(2,1)} %cotangent_ref.1), custom_call_target="tpu_custom_call" | custom-call | flops 1000 | bytes 1000 | tf_op jit(solution)/shard_map/pallas_call | solution.py:31
  21.7 0.3 convert_reduce_fusion
  22.0 0.6 reduce_max.9
  23.3 8.1 %all-to-all-done.9 = bf16[16,16,2304]{2,1,0:T(8,128)(2,1)S(1)} async-done(((bf16[16,16,2304]{2,1,0:T(8,128)(2,1)}), bf16[16,16,2304]{2,1,0:T(8,128)(2,1)S(1)}, u32[]{:S(2)}, u32[]{:S(2)}) %all-to-all-start.9) | async-done | bytes 1179680 | tf_op jit(solution)/shard_map/all_to_all | solution.py:26
  31.4 103.0 %conditional.1 = (bf16[16,2304]{1,0:T(8,128)(2,1)S(1)}, bf16[500,2304]{1,0:T(8,128)(2,1)}, f32[2304]{0:T(1024)S(1)}) conditional(s32[]{:T(128)} %convert_element_type.11, (f32[2304]{0:T(1024)S(1)}, bf16[500,2304]{1,0:T(8,128)(2,1)S(1)}, bf16[256,2304]{1,0:T(8,128)(2,1)S(1)}, s32[256]{0:T(256)}, s32[256]{0:T(256)S(1)}, /*index=5*/s32[256]{0:T(256)}, ...), branch_computations={%region_2.3_spmd, %region_3.5_spmd} | conditional | flops 3539939584 | bytes 44119540 | solution.py:741
  31.4 3.9 %branch_1_fun.6 = bf16[16,16,2944]{2,1,0:T(8,128)(2,1)S(1)} custom-call(s32[4]{0:T(128)} %get-tuple-element.52.me_ref, bf16[256,2304]{1,0:T(8,128)(2,1)S(1)} %get-tuple-element.53.res_hbm.res_ref, bf16[500,2304]{1,0:T(8,128)(2,1)S(1)} %get-tuple-element.54.table_hbm, bf16[16,16,512]{2,1,0:T(8,128)(2,1)} %get-tuple-element.55.slots_hbm, ...), custom_call_target="tpu_custom_call" | custom-call | flops 1179648000 | bytes 2304000 | tf_op jit(solution)/shard_map/cond/branch_1_fun/pallas_call | solution.py:31
  35.3 27.0 %all_to_all.44.in_ref = bf16[16,16,2944]{2,1,0:T(8,128)(2,1)S(1)} all-to-all(bf16[16,16,2944]{2,1,0:T(8,128)(2,1)S(1)} %branch_1_fun.6), channel_id=1, replica_groups=mesh['z'=16,'core'=2,'tensor'=2,'dp'=8] {'tensor','dp'}, dimensions={0} | all-to-all | bytes 3014656 | tf_op jit(solution)/shard_map/cond/branch_1_fun/all_to_all | solution.py:26
  62.4 0.6 branch_1_fun.7
  62.9 39.2 %all_to_all.45.in_ref = bf16[32,2,1664]{2,1,0:T(2,128)(2,1)S(1)} all-to-all(bf16[32,2,1664]{2,1,0:T(2,128)(2,1)S(1)} %get-tuple-element.62), channel_id=1, replica_groups=mesh['z'=16,'core'=2,'tensor'=2,'dp'=8] {'z','core'}, dimensions={0} | all-to-all | bytes 425984 | tf_op jit(solution)/shard_map/cond/branch_1_fun/all_to_all | solution.py:26
  102.1 1.4 branch_1_fun.8
  103.5 3.5 %all-to-all-start.7 = ((f32[16,1,1152]{2,1,0:T(1,128)}), f32[16,1,1152]{2,1,0:T(1,128)S(1)}, u32[]{:S(2)}, u32[]{:S(2)}) async-start(f32[16,1,1152]{2,1,0:T(1,128)} %get-tuple-element.63), calls=%async_computation.7 | async-start | bytes 147456 | tf_op jit(solution)/shard_map/cond/branch_1_fun/all_to_all | solution.py:26
  107.1 6.3 %branch_1_fun.9 = bf16[500,2304]{1,0:T(8,128)(2,1)} custom-call(s32[4]{0:T(128)S(1)} %copy-done.15, bf16[500,2304]{1,0:T(8,128)(2,1)} %copy-done.4, bf16[16,2304]{1,0:T(8,128)(2,1)} %get-tuple-element.56.tail_ref, s32[1,256]{1,0:T(1,128)S(1)} %bitcast.31, f32[1,256]{1,0:T(1,128)S(1)} %get-tuple-element.64.totals_ref, s32[1,256]{1,0:T(1,128)S(1)} %bitcast.27, ...), custom_call_target="tpu_custom_call" | custom-call | flops 1769472000 | bytes 4608000 | tf_op jit(solution)/shard_map/cond/branch_1_fun/pallas_call | solution.py:31
  113.3 5.3 %all-to-all-done.7.in_ref = f32[16,1,1152]{2,1,0:T(1,128)S(1)} async-done(((f32[16,1,1152]{2,1,0:T(1,128)}), f32[16,1,1152]{2,1,0:T(1,128)S(1)}, u32[]{:S(2)}, u32[]{:S(2)}) %all-to-all-start.7) | async-done | bytes 73760 | tf_op jit(solution)/shard_map/cond/branch_1_fun/all_to_all | solution.py:26
  118.6 0.8 branch_1_fun.11
  119.4 7.0 %all-to-all-start.8 = ((f32[32,1,1152]{2,1,0:T(1,128)}), f32[32,1,1152]{2,1,0:T(1,128)S(1)}, u32[]{:S(2)}, u32[]{:S(2)}) async-start(f32[32,1,1152]{2,1,0:T(1,128)} %branch_1_fun.11), calls=%async_computation.8 | async-start | bytes 294912 | tf_op jit(solution)/shard_map/cond/branch_1_fun/all_to_all | solution.py:26
  126.4 2.1 %collective-permute-start = (f32[16,1,1152]{2,1,0:T(1,128)S(1)}, f32[16,1,1152]{2,1,0:T(1,128)S(1)}, u32[]{:S(2)}, u32[]{:S(2)}) collective-permute-start(f32[16,1,1152]{2,1,0:T(1,128)S(1)} %all-to-all-done.7.in_ref), channel_id=1, source_target_pairs={{0,16},{16,0},{1,17},{17,1},{2,18},{18,2},{3,19},{19,3},{4,20},{20... | collective-permute-start | bytes 221192 | tf_op jit(solution)/shard_map/cond/branch_1_fun/ppermute | solution.py:686
  128.6 1.0 collective-permute-done.other_ref
  129.6 0.2 branch_1_fun.10
  129.8 4.3 %all-to-all-done.8 = f32[32,1,1152]{2,1,0:T(1,128)S(1)} async-done(((f32[32,1,1152]{2,1,0:T(1,128)}), f32[32,1,1152]{2,1,0:T(1,128)S(1)}, u32[]{:S(2)}, u32[]{:S(2)}) %all-to-all-start.8) | async-done | bytes 147488 | tf_op jit(solution)/shard_map/cond/branch_1_fun/all_to_all | solution.py:26
  134.4 0.6 copy-done.20
  (42 shorter events, 0.6 us)
Async XLA Ops:
  7.2 9.8 %copy-start.16 = (s32[256]{0:T(256)S(1)}, s32[256]{0:T(256)}, u32[]{:S(2)}) copy-start(s32[256]{0:T(256)} %param.13) | copy-start | bytes 3076
  9.2 7.9 %copy-start.11 = (s32[256]{0:T(256)S(1)}, s32[256]{0:T(256)}, u32[]{:S(2)}) copy-start(s32[256]{0:T(256)} %param.12) | copy-start | bytes 3076
  9.2 9.7 %copy-start.2 = (bf16[500,2304]{1,0:T(8,128)(2,1)S(1)}, bf16[500,2304]{1,0:T(8,128)(2,1)}, u32[]{:S(2)}) copy-start(bf16[500,2304]{1,0:T(8,128)(2,1)} %table_ref.1) | copy-start | bytes 6912004
  9.2 22.2 %all-to-all-start.9 = ((bf16[16,16,2304]{2,1,0:T(8,128)(2,1)}), bf16[16,16,2304]{2,1,0:T(8,128)(2,1)S(1)}, u32[]{:S(2)}, u32[]{:S(2)}) async-start(bf16[16,16,2304]{2,1,0:T(8,128)(2,1)} %broadcast_in_dim.2), calls=%async_computation.9 | async-start | bytes 2359296 | tf_op jit(solution)/shard_map/all_to_all | solution.py:26
  16.9 14.5 %copy-start.9 = (f32[2304]{0:T(1024)S(1)}, f32[2304]{0:T(1024)}, u32[]{:S(2)}) copy-start(f32[2304]{0:T(1024)} %param.10) | copy-start | bytes 27652
  16.9 14.5 %copy-start.10 = (s32[256]{0:T(256)S(1)}, s32[256]{0:T(256)}, u32[]{:S(2)}) copy-start(s32[256]{0:T(256)} %param.14) | copy-start | bytes 3076
  17.3 4.3 %copy-start.14 = (s32[4]{0:T(128)}, s32[4]{0:T(128)S(1)}, u32[]{:S(2)}) copy-start(s32[4]{0:T(128)S(1)} %pad_add_fusion.1.me_ref) | copy-start | bytes 52
  18.3 0.6 copy-start.7
  31.4 3.9 %copy-start.18 = (s32[2,1,128]{2,1,0:T(1,128)}, s32[2,1,128]{2,1,0:T(1,128)S(1)}, u32[]{:S(2)}) copy-start(s32[2,1,128]{2,1,0:T(1,128)S(1)} %get-tuple-element.65.slot_rows_ref) | copy-start | bytes 3076 | tf_op jit(solution)/shard_map/cond
  31.4 31.0 %copy-start.4 = (bf16[500,2304]{1,0:T(8,128)(2,1)}, bf16[500,2304]{1,0:T(8,128)(2,1)S(1)}, u32[]{:S(2)}) copy-start(bf16[500,2304]{1,0:T(8,128)(2,1)S(1)} %get-tuple-element.54.table_hbm) | copy-start | bytes 6912004 | tf_op jit(solution)/shard_map/cond
  35.3 27.0 %copy-start.8 = (s32[2,16,128]{2,1,0:T(8,128)S(1)}, s32[2,16,128]{2,1,0:T(8,128)}, u32[]{:S(2)}) copy-start(s32[2,16,128]{2,1,0:T(8,128)} %get-tuple-element.61.codes_ref) | copy-start | bytes 49156 | tf_op jit(solution)/shard_map/cond
  62.3 39.8 %copy-start.15 = (s32[4]{0:T(128)S(1)}, s32[4]{0:T(128)}, u32[]{:S(2)}) copy-start(s32[4]{0:T(128)} %get-tuple-element.52.me_ref) | copy-start | bytes 52 | tf_op jit(solution)/shard_map/cond
  62.3 44.7 %copy-start.13 = (s32[256]{0:T(256)S(1)}, s32[256]{0:T(256)}, u32[]{:S(2)}) copy-start(s32[256]{0:T(256)} %get-tuple-element.58) | copy-start | bytes 3076 | tf_op jit(solution)/shard_map/cond
  62.3 44.7 %copy-start.19 = (s32[2,1,128]{2,1,0:T(1,128)S(1)}, s32[2,1,128]{2,1,0:T(1,128)}, u32[]{:S(2)}) copy-start(s32[2,1,128]{2,1,0:T(1,128)} %copy-done.18) | copy-start | bytes 3076 | tf_op jit(solution)/shard_map/cond
  103.5 15.1 %all-to-all-start.7 = ((f32[16,1,1152]{2,1,0:T(1,128)}), f32[16,1,1152]{2,1,0:T(1,128)S(1)}, u32[]{:S(2)}, u32[]{:S(2)}) async-start(f32[16,1,1152]{2,1,0:T(1,128)} %get-tuple-element.63), calls=%async_computation.7 | async-start | bytes 147456 | tf_op jit(solution)/shard_map/cond/branch_1_fun/all_to_all | solution.py:26
  107.0 11.6 %copy-start.6 = (bf16[16,2304]{1,0:T(8,128)(2,1)S(1)}, bf16[16,2304]{1,0:T(8,128)(2,1)}, u32[]{:S(2)}) copy-start(bf16[16,2304]{1,0:T(8,128)(2,1)} %get-tuple-element.68.res_ref) | copy-start | bytes 221188 | tf_op jit(solution)/shard_map/cond
  119.4 14.7 %all-to-all-start.8 = ((f32[32,1,1152]{2,1,0:T(1,128)}), f32[32,1,1152]{2,1,0:T(1,128)S(1)}, u32[]{:S(2)}, u32[]{:S(2)}) async-start(f32[32,1,1152]{2,1,0:T(1,128)} %branch_1_fun.11), calls=%async_computation.8 | async-start | bytes 294912 | tf_op jit(solution)/shard_map/cond/branch_1_fun/all_to_all | solution.py:26
  126.4 3.2 %collective-permute-start = (f32[16,1,1152]{2,1,0:T(1,128)S(1)}, f32[16,1,1152]{2,1,0:T(1,128)S(1)}, u32[]{:S(2)}, u32[]{:S(2)}) collective-permute-start(f32[16,1,1152]{2,1,0:T(1,128)S(1)} %all-to-all-done.7.in_ref), channel_id=1, source_target_pairs={{0,16},{16,0},{1,17},{17,1},{2,18},{18,2},{3,19},{19,3},{4,20},{20... | collective-permute-start | bytes 221192 | tf_op jit(solution)/shard_map/cond/branch_1_fun/ppermute | solution.py:686
  134.4 0.6 copy-start.20
  134.4 0.6 copy-start.21

commit v7 on v6

--- a/solution.py
+++ b/solution.py
@@ -187,10 +187,12 @@
         out_ref[:, columns] = (head + scale * inputs)[:vocab_rows].astype(BF16)
 
 
-def plan_body(ids_ref, me_ref, rows_ref, codes_ref, pairs_ref):
+def plan_body(ids_ref, me_ref, rows_ref, codes_ref, pairs_ref, here_ref):
     _, own, groups = ids_ref.shape
     section, place, vocab_rows = me_ref[0], me_ref[1], me_ref[2]
     device = section * groups + place
+    lane = lax.broadcasted_iota(jnp.int32, here_ref.shape, 1)
+    here_ref[...] = jnp.where(lane == 0, section, jnp.where(lane == 1, place, 0))
     token = lax.broadcasted_iota(jnp.int32, (own, groups), 0)
     group = lax.broadcasted_iota(jnp.int32, (own, groups), 1)
 
@@ -303,7 +305,7 @@
 
 
 def compact_body(
-    vocab_rows, me_ref, res_hbm, table_hbm, slots_hbm, tail_ref, gain_ref, targets_ref, mask_ref,
+    vocab_rows, here_ref, res_hbm, table_hbm, slots_hbm, tail_ref, gain_ref, targets_ref, mask_ref,
     packed_ref, res_ref, table_ref, slots_ref, hidden_ref, inverse_ref, tokens_ref, room_ref, sems,
 ):
     copies = [
@@ -322,7 +324,7 @@
     table_ref[table_ref.shape[0] - tail_ref.shape[0] :, :] = tail_ref[...]
     capped = scores_of(table_ref, hidden_ref)
     rows = lax.broadcasted_iota(jnp.int32, capped.shape, 0)
-    device = me_ref[0] * n_plane + me_ref[1]
+    device = here_ref[:, 0:1] * n_plane + here_ref[:, 1:2]
     hit = targets_ref[...] - device * vocab_rows == rows
     expterm = jnp.where(rows < vocab_rows, jnp.exp(capped), 0.0)
     bend = capped * (1.0 / 30.0)
@@ -356,7 +358,7 @@
 
 
 def unpack_body(
-    in_ref, place_ref, codes_ref, out_ref, rows_out_ref, room_ref, moved_ref, rest_ref
+    in_ref, here_ref, codes_ref, out_ref, rows_out_ref, room_ref, moved_ref, rest_ref
 ):
     n_plane, own, packed_width = in_ref.shape
     tokens = n_plane * own
@@ -408,7 +410,7 @@
         return tiles_of
 
     lane = lax.broadcasted_iota(jnp.int32, (own, LANES), 1)
-    token = lax.broadcasted_iota(jnp.int32, (own, LANES), 0) + place_ref[0] * own
+    token = lax.broadcasted_iota(jnp.int32, (own, LANES), 0) + here_ref[:, 1:2] * own
     score = jnp.zeros((own, 1), F32)
     for t, value in enumerate(summed(1)):
         score = score + jnp.sum(
@@ -433,7 +435,7 @@
         out_ref[s] = rest_ref[2 * s : 2 * s + 2, :].astype(BF16)
 
 
-def combine_body(in_ref, me_ref, mask_ref, out_ref, totals_ref, tokens_ref):
+def combine_body(in_ref, here_ref, mask_ref, out_ref, totals_ref, tokens_ref):
     n_section, _, piece_width = in_ref.shape
     cut = out_ref.shape[2]
     tokens = totals_ref.shape[1]
@@ -455,7 +457,7 @@
         )
     totals = tokens_ref[:, :tokens]
     totals_ref[...] = totals
-    token = me_ref[1] * own + lax.div(me_ref[0], halves)
+    token = here_ref[:, 1:2] * own + lax.div(here_ref[:, 0:1], halves)
     here = lax.broadcasted_iota(jnp.int32, totals.shape, 1) == token
     whole = jnp.sum(jnp.where(here, totals, 0.0), axis=1, keepdims=True)
     weight = jnp.sum(jnp.where(here, mask_ref[...].astype(F32), 0.0), axis=1, keepdims=True)
@@ -474,19 +476,23 @@
     return x * inverse, inverse
 
 
-def gain_body(in_ref, core_ref, res_ref, out_ref):
+def at_left(here_ref, shape):
+    return lax.rem(jnp.broadcast_to(here_ref[:, 0:1], shape), 2) == 0
+
+
+def gain_body(in_ref, here_ref, res_ref, out_ref):
     own, _, cut = in_ref.shape
     normed, _ = normed_rows(res_ref)
-    half = jnp.where(core_ref[0] == 0, normed[:, :cut], normed[:, cut:])
+    half = jnp.where(at_left(here_ref, (own, cut)), normed[:, :cut], normed[:, cut:])
     gain = jnp.sum(in_ref[:, 0, :] * half, axis=0, keepdims=True)
     for i in range(out_ref.shape[0]):
         out_ref[i] = gain
 
 
-def close_body(in_ref, other_ref, core_ref, res_ref, gain_ref, grad_ref):
+def close_body(in_ref, other_ref, here_ref, res_ref, gain_ref, grad_ref):
     mine, other = in_ref[:, 0, :], other_ref[:, 0, :]
-    at_left = core_ref[0] == 0
-    left, right = jnp.where(at_left, mine, other), jnp.where(at_left, other, mine)
+    first = at_left(here_ref, mine.shape)
+    left, right = jnp.where(first, mine, other), jnp.where(first, other, mine)
     normed, inverse = normed_rows(res_ref)
     scaled = jnp.concatenate([left, right], axis=1) * gain_ref[...]
     along = jnp.mean(scaled * normed, axis=1, keepdims=True)
@@ -494,7 +500,7 @@
 
 
 def compact_table_body(
-    me_ref, table_hbm, tail_ref, targets_ref, totals_ref, mask_ref, res_ref, gain_ref, slot_rows_ref,
+    here_ref, table_hbm, tail_ref, targets_ref, totals_ref, mask_ref, res_ref, gain_ref, slot_rows_ref,
     moved_ref, out_ref, table_ref, hidden_ref, inverse_ref, sem,
 ):
     vocab_rows, width = out_ref.shape
@@ -505,7 +511,7 @@
     table_ref[table_ref.shape[0] - tail_ref.shape[0] :, :] = tail_ref[...]
     capped = scores_of(table_ref, hidden_ref)
     rows = lax.broadcasted_iota(jnp.int32, capped.shape, 0)
-    device = me_ref[0] * (moved_ref.shape[0] // SLOTS) + me_ref[1]
+    device = here_ref[:, 0:1] * (moved_ref.shape[0] // SLOTS) + here_ref[:, 1:2]
     hit = (targets_ref[...] - device * vocab_rows == rows).astype(F32)
     share = jnp.exp(capped) * (1.0 / totals_ref[...])
     bend = capped * (1.0 / 30.0)
@@ -610,7 +616,7 @@
     everyone, plan, residual, final_gain, table, targets, input_ids, loss_mask, embed_cotangent
 ):
     del input_ids, embed_cotangent
-    slot_rows, codes, slots, me, tail = plan
+    slot_rows, codes, slots, here, tail = plan
     own, width = residual.shape
     vocab_rows = table.shape[0]
     n_plane, n_section = lax.axis_size(PLANE), lax.axis_size(SECTION)
@@ -634,8 +640,8 @@
         shape((n_plane, own, packed_width), BF16),
         2 * product,
         rows_bytes,
-        me, everyone, table, slots, tail, gain_row, targets, mask,
-        in_specs=[SMEM] + [ANY] * 3 + [VMEM] * 4,
+        here, everyone, table, slots, tail, gain_row, targets, mask,
+        in_specs=[VMEM] + [ANY] * 3 + [VMEM] * 4,
         scratch=[
             pltpu.VMEM((tokens, width), BF16),
             table_room,
@@ -654,8 +660,7 @@
         ),
         tokens * width,
         tokens * packed_width * 2,
-        exchange(packed, PLANE), me[1:2], codes,
-        in_specs=[VMEM, SMEM, VMEM],
+        exchange(packed, PLANE), here, codes,
         scratch=[
             pltpu.VMEM((n_plane * tiles * own, LANES), F32),
             pltpu.VMEM((SLOTS * n_plane, width), F32),
@@ -667,8 +672,7 @@
         (shape((own, 1, cut), F32), shape((1, tokens), F32)),
         own * width,
         own * width * 8,
-        exchange(pieces, SECTION), me, mask,
-        in_specs=[VMEM, SMEM, VMEM],
+        exchange(pieces, SECTION), here, mask,
         scratch=[pltpu.VMEM((1, token_tiles * LANES), F32)],
     )
     grad_table = call(
@@ -676,12 +680,11 @@
         shape((vocab_rows, width), BF16),
         3 * product,
         2 * rows_bytes,
-        me, table, tail, targets, totals, mask, everyone, gain_row, slot_rows, moved,
-        in_specs=[SMEM, ANY] + [VMEM] * 8,
+        here, table, tail, targets, totals, mask, everyone, gain_row, slot_rows, moved,
+        in_specs=[VMEM, ANY] + [VMEM] * 8,
         scratch=[table_room] + norm_rooms + [pltpu.SemaphoreType.DMA],
     )
     mine, grad_table = lax.optimization_barrier((exchange(half_token, "z"), grad_table))
-    core = lax.axis_index("core").astype(jnp.int32).reshape(1)
     n_chips = lax.axis_size(CHIPS)
     other = lax.ppermute(mine, "core", [(0, 1), (1, 0)])
     gain_part = call(
@@ -689,16 +692,14 @@
         shape((n_chips, 1, cut), F32),
         own * width * 4,
         own * width * 8,
-        mine, core, residual,
-        in_specs=[VMEM, SMEM, VMEM],
+        mine, here, residual,
     )
     grad_residual = call(
         close_body,
         shape((own, width), BF16),
         own * width * 10,
         own * width * 8,
-        mine, other, core, residual, gain_row,
-        in_specs=[VMEM, VMEM, SMEM, VMEM, VMEM],
+        mine, other, here, residual, gain_row,
     )
     grad_gain = exchange(gain_part, CHIPS).reshape(n_chips // n_plane, n_plane, cut)
     return (grad_residual, jnp.sum(grad_gain, axis=1).reshape(width), grad_table)
@@ -714,12 +715,13 @@
     lanes = -(-SLOTS * n_plane // LANES) * LANES
     everyone = exchange(jnp.broadcast_to(residual[None], (n_plane, own, width)), PLANE)
     everyone = everyone.reshape(n_plane * own, width)
-    slot_rows, codes, pairs = call(
+    slot_rows, codes, pairs, here = call(
         plan_body,
         (
             shape((2, 1, lanes), jnp.int32),
             shape((2, own, lanes), jnp.int32),
             shape((2, own, n_plane), jnp.int32),
+            shape((1, LANES), jnp.int32),
         ),
         1000,
         1000,
@@ -742,7 +744,7 @@
         fits,
         compact,
         general,
-        everyone, (slot_rows, codes, slots, me, tail), residual, final_gain, table, targets, input_ids, loss_mask,
+        everyone, (slot_rows, codes, slots, here, tail), residual, final_gain, table, targets, input_ids, loss_mask,
         embed_cotangent,
     )
 

time: 143 us -> 142 us (level)
  no operation moved by 1% of the time
where the time goes in v7:
time: 142 us; the launch traced here: 141 us
  blocking collectives  66.2 us (47%)
  starting transfers between devices  20.4 us (14%)
  waiting for transfers between devices  19.1 us (13%)
  Pallas kernels  16 us (11%)
  between operations  14.7 us (10%)
  local copies, waits for them, and re-layouts  3.67 us (3%)
    all_to_all x2, blocking collectives, exchange(): return lax.all_to_all(pieces, axes, 0, 0, tiled=True)  66.2 us
    all_to_all x3, starting transfers between devices, exchange(): return lax.all_to_all(pieces, axes, 0, 0, tiled=True)  18.2 us
    all_to_all x3, waiting for transfers between devices, exchange(): return lax.all_to_all(pieces, axes, 0, 0, tiled=True)  18.1 us
    pallas_call x8, Pallas kernels, call(): pl.pallas_call(body, out_shape=outs, in_specs=in_specs or [VMEM] * len(op...  16 us
  transfers between devices with their start and end apart: 4, of which 4 were waited for; matrix products, arithmetic and copies ran while one was open for 1% of the time, Pallas kernels for 7%

profile of v7, /device:TPU:1, one launch (start us, length us, event | category | flops | bytes accessed | tf_op | source)
XLA Modules:
  0.0 141.4 jit_solution(3404329501622890578)
XLA Ops:
  7.2 2.0 %broadcast_in_dim.2 = bf16[16,16,2304]{2,1,0:T(8,128)(2,1)} broadcast(bf16[16,2304]{1,0:T(8,128)(2,1)} %param.9), dimensions={1,2} | broadcast | bytes 1253376 | tf_op jit(solution)/shard_map/broadcast_in_dim | solution.py:716
  9.2 7.7 %all-to-all-start.9 = ((bf16[16,16,2304]{2,1,0:T(8,128)(2,1)}), bf16[16,16,2304]{2,1,0:T(8,128)(2,1)S(1)}, u32[]{:S(2)}, u32[]{:S(2)}) async-start(bf16[16,16,2304]{2,1,0:T(8,128)(2,1)} %broadcast_in_dim.2), calls=%async_computation.9 | async-start | bytes 2359296 | tf_op jit(solution)/shard_map/all_to_all | solution.py:26
  17.3 1.5 %shard_map.96 = (s32[2,1,128]{2,1,0:T(1,128)S(1)}, s32[2,16,128]{2,1,0:T(8,128)S(1)}, s32[2,16,16]{2,1,0:T(8,128)S(1)}, s32[1,128]{1,0:T(1,128)}) custom-call(s32[2,16,16]{2,1,0:T(8,128)S(1)} %pad_add_fusion.ids_ref, s32[4]{0:T(128)S(1)} %pad_add_fusion.1.me_ref), custom_call_target="tpu_custom_call" | custom-call | flops 1000 | bytes 1000 | tf_op jit(solution)/shard_map/pallas_call | solution.py:31
  18.8 0.6 copy-done.8
  19.4 2.7 %shard_map.97 = (bf16[16,16,512]{2,1,0:T(8,128)(2,1)}, bf16[16,2304]{1,0:T(8,128)(2,1)}) custom-call(bf16[500,2304]{1,0:T(8,128)(2,1)S(1)} %copy-done.2, s32[2,1,128]{2,1,0:T(1,128)S(1)} %get-tuple-element.78.slot_rows_ref, s32[2,16,128]{2,1,0:T(8,128)S(1)} %get-tuple-element.79.codes_ref, bf16[16,2304]{1,0:T(8,128)(2,1)} %cotangent_ref.1), custom_call_target="tpu_custom_call" | custom-call | flops 1000 | bytes 1000 | tf_op jit(solution)/shard_map/pallas_call | solution.py:31
  22.2 0.3 convert_reduce_fusion
  22.5 0.6 reduce_max.9
  23.7 7.6 %all-to-all-done.9 = bf16[16,16,2304]{2,1,0:T(8,128)(2,1)S(1)} async-done(((bf16[16,16,2304]{2,1,0:T(8,128)(2,1)}), bf16[16,16,2304]{2,1,0:T(8,128)(2,1)S(1)}, u32[]{:S(2)}, u32[]{:S(2)}) %all-to-all-start.9) | async-done | bytes 1179680 | tf_op jit(solution)/shard_map/all_to_all | solution.py:26
  31.4 102.6 %conditional.1 = (bf16[16,2304]{1,0:T(8,128)(2,1)S(1)}, bf16[500,2304]{1,0:T(8,128)(2,1)}, f32[2304]{0:T(1024)S(1)}) conditional(s32[]{:T(128)} %convert_element_type.11, (f32[2304]{0:T(1024)S(1)}, bf16[500,2304]{1,0:T(8,128)(2,1)S(1)}, bf16[256,2304]{1,0:T(8,128)(2,1)S(1)}, s32[256]{0:T(256)}, s32[256]{0:T(256)S(1)}, /*index=5*/s32[256]{0:T(256)}, ...), branch_computations={%region_2.3_spmd, %region_3.5_spmd} | conditional | flops 3539939584 | bytes 44119540 | solution.py:743
  31.4 3.9 %branch_1_fun.6 = bf16[16,16,2944]{2,1,0:T(8,128)(2,1)S(1)} custom-call(s32[1,128]{1,0:T(1,128)} %get-tuple-element.50.here_ref, bf16[256,2304]{1,0:T(8,128)(2,1)S(1)} %get-tuple-element.51.res_hbm.res_ref, bf16[500,2304]{1,0:T(8,128)(2,1)S(1)} %get-tuple-element.52.table_hbm, bf16[16,16,512]{2,1,0:T(8,128)(2,1)} %get-tuple-element.53.slots_hbm, ...), custom_call_target="tpu_custom_call" | custom-call | flops 1179648000 | bytes 2304000 | tf_op jit(solution)/shard_map/cond/branch_1_fun/pallas_call | solution.py:31
  35.3 27.1 %all_to_all.44.in_ref = bf16[16,16,2944]{2,1,0:T(8,128)(2,1)S(1)} all-to-all(bf16[16,16,2944]{2,1,0:T(8,128)(2,1)S(1)} %branch_1_fun.6), channel_id=1, replica_groups=mesh['z'=16,'core'=2,'tensor'=2,'dp'=8] {'tensor','dp'}, dimensions={0} | all-to-all | bytes 3014656 | tf_op jit(solution)/shard_map/cond/branch_1_fun/all_to_all | solution.py:26
  62.4 0.6 branch_1_fun.7
  63.0 39.1 %all_to_all.45.in_ref = bf16[32,2,1664]{2,1,0:T(2,128)(2,1)S(1)} all-to-all(bf16[32,2,1664]{2,1,0:T(2,128)(2,1)S(1)} %get-tuple-element.59), channel_id=1, replica_groups=mesh['z'=16,'core'=2,'tensor'=2,'dp'=8] {'z','core'}, dimensions={0} | all-to-all | bytes 425984 | tf_op jit(solution)/shard_map/cond/branch_1_fun/all_to_all | solution.py:26
  102.2 0.9 branch_1_fun.8
  103.1 3.5 %all-to-all-start.7 = ((f32[16,1,1152]{2,1,0:T(1,128)}), f32[16,1,1152]{2,1,0:T(1,128)S(1)}, u32[]{:S(2)}, u32[]{:S(2)}) async-start(f32[16,1,1152]{2,1,0:T(1,128)} %get-tuple-element.60), calls=%async_computation.7 | async-start | bytes 147456 | tf_op jit(solution)/shard_map/cond/branch_1_fun/all_to_all | solution.py:26
  106.6 5.4 %branch_1_fun.9 = bf16[500,2304]{1,0:T(8,128)(2,1)} custom-call(s32[1,128]{1,0:T(1,128)S(1)} %copy-done.15, bf16[500,2304]{1,0:T(8,128)(2,1)} %copy-done.4, bf16[16,2304]{1,0:T(8,128)(2,1)S(1)} %copy-done.7, s32[1,256]{1,0:T(1,128)S(1)} %bitcast.30, f32[1,256]{1,0:T(1,128)S(1)} %get-tuple-element.61.totals_ref, s32[1,256]{1,0:T(1,128)S(1)} %bitcast.26, ...), custom_call_target="tpu_custom_call" | custom-call | flops 1769472000 | bytes 4608000 | tf_op jit(solution)/shard_map/cond/branch_1_fun/pallas_call | solution.py:31
  112.0 6.2 %all-to-all-done.7.in_ref = f32[16,1,1152]{2,1,0:T(1,128)S(1)} async-done(((f32[16,1,1152]{2,1,0:T(1,128)}), f32[16,1,1152]{2,1,0:T(1,128)S(1)}, u32[]{:S(2)}, u32[]{:S(2)}) %all-to-all-start.7) | async-done | bytes 73760 | tf_op jit(solution)/shard_map/cond/branch_1_fun/all_to_all | solution.py:26
  118.2 0.8 branch_1_fun.11
  119.0 7.0 %all-to-all-start.8 = ((f32[32,1,1152]{2,1,0:T(1,128)}), f32[32,1,1152]{2,1,0:T(1,128)S(1)}, u32[]{:S(2)}, u32[]{:S(2)}) async-start(f32[32,1,1152]{2,1,0:T(1,128)} %branch_1_fun.11), calls=%async_computation.8 | async-start | bytes 294912 | tf_op jit(solution)/shard_map/cond/branch_1_fun/all_to_all | solution.py:26
  126.0 2.1 %collective-permute-start = (f32[16,1,1152]{2,1,0:T(1,128)S(1)}, f32[16,1,1152]{2,1,0:T(1,128)S(1)}, u32[]{:S(2)}, u32[]{:S(2)}) collective-permute-start(f32[16,1,1152]{2,1,0:T(1,128)S(1)} %all-to-all-done.7.in_ref), channel_id=1, source_target_pairs={{0,16},{16,0},{1,17},{17,1},{2,18},{18,2},{3,19},{19,3},{4,20},{20... | collective-permute-start | bytes 221192 | tf_op jit(solution)/shard_map/cond/branch_1_fun/ppermute | solution.py:689
  128.2 1.0 collective-permute-done.other_ref
  129.2 0.2 branch_1_fun.10
  129.4 4.3 %all-to-all-done.8 = f32[32,1,1152]{2,1,0:T(1,128)S(1)} async-done(((f32[32,1,1152]{2,1,0:T(1,128)}), f32[32,1,1152]{2,1,0:T(1,128)S(1)}, u32[]{:S(2)}, u32[]{:S(2)}) %all-to-all-start.8) | async-done | bytes 147488 | tf_op jit(solution)/shard_map/cond/branch_1_fun/all_to_all | solution.py:26
  134.0 0.6 copy-done.20
  (42 shorter events, 0.6 us)
Async XLA Ops:
  7.2 9.8 %copy-start.16 = (s32[256]{0:T(256)S(1)}, s32[256]{0:T(256)}, u32[]{:S(2)}) copy-start(s32[256]{0:T(256)} %param.13) | copy-start | bytes 3076
  9.2 7.9 %copy-start.12 = (s32[256]{0:T(256)S(1)}, s32[256]{0:T(256)}, u32[]{:S(2)}) copy-start(s32[256]{0:T(256)} %param.12) | copy-start | bytes 3076
  9.2 10.3 %copy-start.2 = (bf16[500,2304]{1,0:T(8,128)(2,1)S(1)}, bf16[500,2304]{1,0:T(8,128)(2,1)}, u32[]{:S(2)}) copy-start(bf16[500,2304]{1,0:T(8,128)(2,1)} %table_ref.1) | copy-start | bytes 6912004
  9.2 22.2 %all-to-all-start.9 = ((bf16[16,16,2304]{2,1,0:T(8,128)(2,1)}), bf16[16,16,2304]{2,1,0:T(8,128)(2,1)S(1)}, u32[]{:S(2)}, u32[]{:S(2)}) async-start(bf16[16,16,2304]{2,1,0:T(8,128)(2,1)} %broadcast_in_dim.2), calls=%async_computation.9 | async-start | bytes 2359296 | tf_op jit(solution)/shard_map/all_to_all | solution.py:26
  16.9 14.5 %copy-start.10 = (f32[2304]{0:T(1024)S(1)}, f32[2304]{0:T(1024)}, u32[]{:S(2)}) copy-start(f32[2304]{0:T(1024)} %param.10) | copy-start | bytes 27652
  16.9 14.5 %copy-start.11 = (s32[256]{0:T(256)S(1)}, s32[256]{0:T(256)}, u32[]{:S(2)}) copy-start(s32[256]{0:T(256)} %param.14) | copy-start | bytes 3076
  18.8 0.6 copy-start.8
  18.8 3.3 %copy-start.18 = (s32[2,1,128]{2,1,0:T(1,128)}, s32[2,1,128]{2,1,0:T(1,128)S(1)}, u32[]{:S(2)}) copy-start(s32[2,1,128]{2,1,0:T(1,128)S(1)} %get-tuple-element.78.slot_rows_ref) | copy-start | bytes 3076
  31.4 31.0 %copy-start.4 = (bf16[500,2304]{1,0:T(8,128)(2,1)}, bf16[500,2304]{1,0:T(8,128)(2,1)S(1)}, u32[]{:S(2)}) copy-start(bf16[500,2304]{1,0:T(8,128)(2,1)S(1)} %get-tuple-element.52.table_hbm) | copy-start | bytes 6912004 | tf_op jit(solution)/shard_map/cond
  35.3 27.1 %copy-start.9 = (s32[2,16,128]{2,1,0:T(8,128)S(1)}, s32[2,16,128]{2,1,0:T(8,128)}, u32[]{:S(2)}) copy-start(s32[2,16,128]{2,1,0:T(8,128)} %get-tuple-element.58.codes_ref) | copy-start | bytes 49156 | tf_op jit(solution)/shard_map/cond
  35.3 27.1 %copy-start.15 = (s32[1,128]{1,0:T(1,128)S(1)}, s32[1,128]{1,0:T(1,128)}, u32[]{:S(2)}) copy-start(s32[1,128]{1,0:T(1,128)} %get-tuple-element.50.here_ref) | copy-start | bytes 1540 | tf_op jit(solution)/shard_map/cond
  62.4 44.2 %copy-start.14 = (s32[256]{0:T(256)S(1)}, s32[256]{0:T(256)}, u32[]{:S(2)}) copy-start(s32[256]{0:T(256)} %get-tuple-element.56) | copy-start | bytes 3076 | tf_op jit(solution)/shard_map/cond
  62.4 44.2 %copy-start.19 = (s32[2,1,128]{2,1,0:T(1,128)S(1)}, s32[2,1,128]{2,1,0:T(1,128)}, u32[]{:S(2)}) copy-start(s32[2,1,128]{2,1,0:T(1,128)} %get-tuple-element.62.slot_rows_ref) | copy-start | bytes 3076 | tf_op jit(solution)/shard_map/cond
  62.4 44.2 %copy-start.7 = (bf16[16,2304]{1,0:T(8,128)(2,1)S(1)}, bf16[16,2304]{1,0:T(8,128)(2,1)}, u32[]{:S(2)}) copy-start(bf16[16,2304]{1,0:T(8,128)(2,1)} %get-tuple-element.54.tail_ref) | copy-start | bytes 221188 | tf_op jit(solution)/shard_map/cond
  103.1 15.1 %all-to-all-start.7 = ((f32[16,1,1152]{2,1,0:T(1,128)}), f32[16,1,1152]{2,1,0:T(1,128)S(1)}, u32[]{:S(2)}, u32[]{:S(2)}) async-start(f32[16,1,1152]{2,1,0:T(1,128)} %get-tuple-element.60), calls=%async_computation.7 | async-start | bytes 147456 | tf_op jit(solution)/shard_map/cond/branch_1_fun/all_to_all | solution.py:26
  106.6 11.6 %copy-start.6 = (bf16[16,2304]{1,0:T(8,128)(2,1)S(1)}, bf16[16,2304]{1,0:T(8,128)(2,1)}, u32[]{:S(2)}) copy-start(bf16[16,2304]{1,0:T(8,128)(2,1)} %get-tuple-element.65.res_ref) | copy-start | bytes 221188 | tf_op jit(solution)/shard_map/cond
  119.0 14.7 %all-to-all-start.8 = ((f32[32,1,1152]{2,1,0:T(1,128)}), f32[32,1,1152]{2,1,0:T(1,128)S(1)}, u32[]{:S(2)}, u32[]{:S(2)}) async-start(f32[32,1,1152]{2,1,0:T(1,128)} %branch_1_fun.11), calls=%async_computation.8 | async-start | bytes 294912 | tf_op jit(solution)/shard_map/cond/branch_1_fun/all_to_all | solution.py:26
  126.0 3.2 %collective-permute-start = (f32[16,1,1152]{2,1,0:T(1,128)S(1)}, f32[16,1,1152]{2,1,0:T(1,128)S(1)}, u32[]{:S(2)}, u32[]{:S(2)}) collective-permute-start(f32[16,1,1152]{2,1,0:T(1,128)S(1)} %all-to-all-done.7.in_ref), channel_id=1, source_target_pairs={{0,16},{16,0},{1,17},{17,1},{2,18},{18,2},{3,19},{19,3},{4,20},{20... | collective-permute-start | bytes 221192 | tf_op jit(solution)/shard_map/cond/branch_1_fun/ppermute | solution.py:689
  134.0 0.6 copy-start.20
  134.0 0.6 copy-start.21
